TPU v7x, 1024 devices: a whole 8x8x8 slice. The times are simulated.
1024 devices in a mesh: grp: 16 (over z, core), rep: 64 (over x, y).
Axes of the slice: x: 8, y: 8, z: 8, core: 2. Of those that a mesh axis runs over, the one named last changes fastest.
Arguments:
- features: bfloat16 [131072, 512], P(('grp', 'rep'))
- output_grads: bfloat16 [131072, 8192], P(('grp', 'rep'))
- block_order: int32 [16], replicated, may hold values from 0 to 15, each once
- emb_table: float32 [524288, 128], P(('grp', 'rep')), may hold values from -6 to 6
- row_accum: float32 [524288], P(('grp', 'rep')), may hold values from 0.1 to 1
- hot_rows: int32 [131072], P(('grp', 'rep')), may hold values from 0 to 511
- hot_owner: int32 [131072, 1], P(('grp', 'rep')), may hold values from 0 to 15; in each aligned block of 128 rows (0 to 127, 128 to 255, ...) at most 16 rows name the same one
- live_counts: int32 [1024], P(('grp', 'rep')), may hold values from 32 to 128, as said below
- hot_deltas: bfloat16 [131072, 128], P(('grp', 'rep')), may hold values from -6 to 6
Outputs:
- new_table: float32 [524288, 128], P(('grp', 'rep'))
- new_accum: float32 [524288], P(('grp', 'rep'))
- directions: bfloat16 [16, 512, 512], P(None, 'rep')
Inputs may be any that keep to these rules, and one draw needn't show every extreme that they name: `block_order`: A permutation: each block is taken by one owner. `hot_owner`: in the 128 slots of one device at most 16 name the same owner. `live_counts`: the live slots of a device are its first ones. `hot_rows`: A row among the owner's 512 rows.
All inputs are finite; a program needn't handle non-finite values.
Results may differ from a plain program's by a relative error of at most 0.001.
Values may be sent and summed in bfloat16 or wider, within the bound.
No kernel may reach another device: no remote copies, remote signals or barrier semaphores. Data moves between devices by JAX's collectives and lax.ppermute only.
A program may use at most 32 MiB of HBM per device.

v0:
```python
from functools import partial

import jax
import jax.numpy as jnp
from jax import lax
from jax.sharding import PartitionSpec as P

ITERS = 2


highest = lax.Precision.HIGHEST
learning_rate = 1.0


def left_gram(vectors, grad, scale):
    inner = jnp.dot(vectors, grad, precision=highest)
    return jnp.dot(inner, grad.T, precision=highest) / scale


def right_gram(vectors, grad, scale):
    inner = jnp.dot(vectors, grad.T, precision=highest)
    return jnp.dot(inner, grad, precision=highest) / scale


def apply_power(level, vectors, gram):
    if level == 0:
        return gram(vectors)
    inner = apply_power(level - 1, vectors, gram)
    for repeat in range(4):
        inner = apply_factor(level - 1, inner, gram)
    return inner


def apply_factor(level, vectors, gram):
    return (5.0 * vectors - apply_power(level, vectors, gram)) / 4.0


def root_rows(vectors, gram, scale):
    result = vectors
    for level in range(ITERS):
        result = apply_factor(level, result, gram)
    return result * scale ** (-0.25)


def shards(
    features,
    output_grads,
    block_order,
    emb_table,
    row_accum,
    hot_rows,
    hot_owner,
    live_counts,
    hot_deltas,
):
    groups = lax.axis_size("grp")
    replicas = lax.axis_size("rep")
    width = features.shape[1]
    tokens_here = features.shape[0]
    hot_count = hot_rows.shape[0]
    emb_width = hot_deltas.shape[1]
    capacity = max(2, 2 * hot_count // groups)
    targets = hot_owner[:, 0]
    onehot = (targets[:, None] == jnp.arange(groups, dtype=jnp.int32)[None, :]).astype(jnp.int32)
    ranks = jnp.sum((jnp.cumsum(onehot, axis=0) - 1) * onehot, axis=1)
    positions = ranks * groups + targets
    live = jnp.arange(hot_count, dtype=jnp.int32) < live_counts[0]
    masked = jnp.where(live[:, None], hot_deltas, jnp.zeros_like(hot_deltas))
    slot_rows = (
        jnp.zeros((capacity * groups,), jnp.int32)
        .at[positions]
        .set(hot_rows)
        .reshape(capacity, groups)
    )
    slot_deltas = jnp.zeros((capacity * groups, emb_width), jnp.bfloat16).at[positions].set(masked)
    slot_deltas = slot_deltas.reshape(capacity, groups, emb_width)
    grouped = output_grads.reshape(tokens_here, groups, width)
    ordered = jnp.take(grouped, block_order, axis=1)
    got_rows, got_deltas = (
        lax.all_to_all(slot_rows, "grp", split_axis=1, concat_axis=0, tiled=True),
        lax.all_to_all(slot_deltas, "grp", split_axis=1, concat_axis=0, tiled=True),
    )
    got_grads = lax.all_to_all(ordered, "grp", split_axis=1, concat_axis=0, tiled=True)
    row_ids = got_rows.reshape(-1)
    delta_rows = got_deltas.reshape(-1, emb_width).astype(jnp.float32)
    summed = jnp.zeros(emb_table.shape, jnp.float32).at[row_ids].add(delta_rows)
    new_accum = row_accum + jnp.mean(summed * summed, axis=1)
    new_table = emb_table - learning_rate * summed / jnp.sqrt(new_accum)[:, None]
    received = got_grads.reshape(-1, width)
    partial_grad = lax.dot_general(
        lax.all_gather(features, "grp", axis=0, tiled=True),
        received,
        (((0,), (0,)), ((), ())),
        preferred_element_type=jnp.float32,
    )
    grad = lax.psum(partial_grad, "rep")
    frobenius = jnp.sum(grad * grad) + 1e-06
    normal_gram = jnp.dot(grad, grad.T, precision=highest) / frobenius
    squared_gram = jnp.dot(normal_gram, normal_gram, precision=highest)
    spectral_bound = jnp.sqrt(jnp.sqrt(jnp.sum(squared_gram * squared_gram)))
    scale = frobenius * spectral_bound
    share = width // replicas
    first_row = lax.axis_index("rep") * share
    basis = (
        jnp.arange(width, dtype=jnp.int32)[None, :]
        == first_row + jnp.arange(share, dtype=jnp.int32)[:, None]
    ).astype(jnp.float32)
    left_part = root_rows(basis, partial(left_gram, grad=grad, scale=scale), scale)
    middle = jnp.dot(left_part, grad, precision=highest)
    final_rows = root_rows(middle, partial(right_gram, grad=grad, scale=scale), scale)
    own_rows = (width * final_rows).astype(jnp.bfloat16)[None]
    directions = lax.all_gather(own_rows, "grp", axis=0, tiled=True)
    return (new_table, new_accum, directions)


def solution(mesh):
    return jax.shard_map(
        shards,
        mesh=mesh,
        in_specs=(
            P(("grp", "rep"), None),
            P(("grp", "rep"), None),
            P(),
            P(("grp", "rep"), None),
            P(("grp", "rep")),
            P(("grp", "rep")),
            P(("grp", "rep"), None),
            P(("grp", "rep")),
            P(("grp", "rep"), None),
        ),
        out_specs=(P(("grp", "rep"), None), P(("grp", "rep")), P(None, "rep", None)),
        check_vma=False,
    )
```

profile of v0, /device:TPU:1, one launch (start us, length us, event | category | flops | bytes accessed | tf_op | source)
XLA Modules:
  0.0 335.8 jit_solution(12485043948028841415)
XLA Ops:
  8.5 4.1 %copy.19 = bf16[128,8192]{0,1:T(8,128)(2,1)} copy(bf16[128,8192]{1,0:T(8,128)(2,1)} %param.10) | data formatting | bytes 4194304 | tf_op args[1]
  12.6 2.9 copy.20
  15.5 2.0 gather_fusion
  17.4 3.1 select_bitcast_fusion
  20.6 18.3 %all-to-all-start.2 = ((bf16[128,16,512]{2,0,1:T(8,128)(2,1)}), bf16[128,16,512]{2,0,1:T(8,128)(2,1)S(1)}, u32[]{:S(2)}, u32[]{:S(2)}) async-start(bf16[128,16,512]{2,0,1:T(8,128)(2,1)} %select_bitcast_fusion), calls=%async_computation.2 | async-start | bytes 4194304 | tf_op jit(solution)/shard_map/all_to_all | solution.py:83
  40.8 1.0 scatter_custom_fusion.1
  42.4 1.1 scatter_custom_fusion
  44.3 50.0 %all-to-all-done.2 = bf16[128,16,512]{2,0,1:T(8,128)(2,1)S(1)} async-done(((bf16[128,16,512]{2,0,1:T(8,128)(2,1)}), bf16[128,16,512]{2,0,1:T(8,128)(2,1)S(1)}, u32[]{:S(2)}, u32[]{:S(2)}) %all-to-all-start.2) | async-done | bytes 2097184 | tf_op jit(solution)/shard_map/all_to_all | solution.py:83
  94.3 4.3 %all-to-all-start = ((s32[16,16,1]{0,2,1:T(1,128)}), s32[16,16,1]{0,2,1:T(1,128)S(1)}, u32[]{:S(2)}, u32[]{:S(2)}) async-start(s32[16,16,1]{0,2,1:T(1,128)} %copy.17), calls=%async_computation | async-start | bytes 16384 | tf_op jit(solution)/shard_map/all_to_all | solution.py:80
  98.6 8.4 %all-gather.3.cloned.1.call-done = bf16[2048,512]{1,0:T(8,128)(2,1)} async-done(((bf16[128,512]{1,0:T(8,128)(2,1)}), bf16[2048,512]{1,0:T(8,128)(2,1)}) %all-gather.3.cloned.1.call-update) | async-done | bytes 2097168 | tf_op jit(solution)/shard_map/all_gather | solution.py:91
  107.1 3.9 %convolution_bitcast_fusion = f32[512,512]{0,1:T(8,128)} fusion(bf16[2048,512]{1,0:T(8,128)(2,1)S(1)} %bitcast.78, bf16[2048,512]{1,0:T(8,128)(2,1)} %all-gather.3.cloned.1.call-done), kind=kOutput, calls=%fused_computation.7 | convolution fusion | flops 1073741824 | bytes 5242880 | tf_op jit(solution)/shard_map/dot_general | solution.py:90
  111.0 4.4 %all-to-all-start.1 = ((bf16[16,16,128]{2,0,1:T(8,128)(2,1)}), bf16[16,16,128]{2,0,1:T(8,128)(2,1)S(1)}, u32[]{:S(2)}, u32[]{:S(2)}) async-start(bf16[16,16,128]{2,0,1:T(8,128)(2,1)} %copy.18), calls=%async_computation.1 | async-start | bytes 131072 | tf_op jit(solution)/shard_map/all_to_all | solution.py:81
  115.5 7.7 %all-to-all-done.1 = bf16[16,16,128]{2,0,1:T(8,128)(2,1)S(1)} async-done(((bf16[16,16,128]{2,0,1:T(8,128)(2,1)}), bf16[16,16,128]{2,0,1:T(8,128)(2,1)S(1)}, u32[]{:S(2)}, u32[]{:S(2)}) %all-to-all-start.1) | async-done | bytes 65568 | tf_op jit(solution)/shard_map/all_to_all | solution.py:81
  123.2 1.7 scatter_custom_fusion.2
  126.4 148.7 %all-reduce.2.cloned.1.call-done = f32[512,512]{0,1:T(8,128)} async-done(((f32[512,512]{0,1:T(8,128)}), f32[512,512]{0,1:T(8,128)}) %all-reduce.2.cloned.1.call-update) | async-done | bytes 1048592 | tf_op jit(solution)/shard_map/psum | solution.py:96
  275.1 2.1 multiply_reduce_fusion
  277.9 3.4 %convolution_divide_fusion = f32[512,512]{1,0:T(8,128)S(1)} fusion(f32[512,512]{0,1:T(8,128)} %all-reduce.2.cloned.1.call-done, f32[]{:T(128)S(6)} %add.56), kind=kOutput, calls=%fused_computation.6 | convolution fusion | flops 1610874880 | bytes 2097156 | tf_op jit(solution)/shard_map/dot_general | solution.py:98
  281.3 2.6 fusion.18
  287.4 1.0 fusion.65
  295.6 1.0 fusion.8
  298.8 1.0 fusion.7
  300.3 1.0 fusion.6
  303.5 1.0 fusion.17
  304.5 23.8 %all-gather = bf16[128,512]{1,0:T(8,128)(2,1)S(1)} all-gather(bf16[8,512]{1,0:T(8,128)(2,1)S(1)} %fusion.17), channel_id=2, replica_groups=mesh['grp'=16,'rep'=64] {'grp'}, dimensions={0}, use_global_device_ids=true | all-gather | bytes 139264 | tf_op jit(solution)/shard_map/all_gather | solution.py:112
  (55 shorter events, 21.3 us)
Async XLA Ops:
  20.6 19.7 %copy-start.3 = (s32[128,1]{0,1:T(1,128)S(1)}, s32[128,1]{0,1:T(1,128)}, u32[]{:S(2)}) copy-start(s32[128,1]{0,1:T(1,128)} %param.15) | copy-start | bytes 1540
  20.6 20.2 %copy-start.2 = (bf16[128,128]{1,0:T(8,128)(2,1)S(1)}, bf16[128,128]{1,0:T(8,128)(2,1)}, u32[]{:S(2)}) copy-start(bf16[128,128]{1,0:T(8,128)(2,1)} %param.17) | copy-start | bytes 98308
  20.6 73.7 %all-to-all-start.2 = ((bf16[128,16,512]{2,0,1:T(8,128)(2,1)}), bf16[128,16,512]{2,0,1:T(8,128)(2,1)S(1)}, u32[]{:S(2)}, u32[]{:S(2)}) async-start(bf16[128,16,512]{2,0,1:T(8,128)(2,1)} %select_bitcast_fusion), calls=%async_computation.2 | async-start | bytes 4194304 | tf_op jit(solution)/shard_map/all_to_all | solution.py:83
  38.9 68.1 %all-gather.3.cloned.1.call-start = ((), (), s32[]{:S(2)}) async-start(), calls=%async_computation.3 | async-start | bytes 2228224 | tf_op jit(solution)/shard_map/all_gather | solution.py:91
  94.3 16.6 %all-to-all-start = ((s32[16,16,1]{0,2,1:T(1,128)}), s32[16,16,1]{0,2,1:T(1,128)S(1)}, u32[]{:S(2)}, u32[]{:S(2)}) async-start(s32[16,16,1]{0,2,1:T(1,128)} %copy.17), calls=%async_computation | async-start | bytes 16384 | tf_op jit(solution)/shard_map/all_to_all | solution.py:80
  98.6 176.5 %all-reduce.2.cloned.1.call-start = ((), (), s32[]{:S(2)}) async-start(), calls=%async_computation.4 | async-start | bytes 2097152 | tf_op jit(solution)/shard_map/psum | solution.py:96
  107.1 17.9 %copy-start.4 = (f32[512]{0:T(512)S(1)}, f32[512]{0:T(512)}, u32[]{:S(2)}) copy-start(f32[512]{0:T(512)} %param.13) | copy-start | bytes 6148
  110.9 14.7 %copy-start.1 = (f32[512,128]{1,0:T(8,128)S(1)}, f32[512,128]{1,0:T(8,128)}, u32[]{:S(2)}) copy-start(f32[512,128]{1,0:T(8,128)} %param.12) | copy-start | bytes 786436
  111.0 12.2 %all-to-all-start.1 = ((bf16[16,16,128]{2,0,1:T(8,128)(2,1)}), bf16[16,16,128]{2,0,1:T(8,128)(2,1)S(1)}, u32[]{:S(2)}, u32[]{:S(2)}) async-start(bf16[16,16,128]{2,0,1:T(8,128)(2,1)} %copy.18), calls=%async_computation.1 | async-start | bytes 131072 | tf_op jit(solution)/shard_map/all_to_all | solution.py:81
  281.2 3.4 %copy-start = (f32[512,512]{0,1:T(8,128)S(1)}, f32[512,512]{0,1:T(8,128)}, u32[]{:S(2)}) copy-start(f32[512,512]{0,1:T(8,128)} %all-reduce.2.cloned.1.call-done) | copy-start | bytes 3145732
Sparse Core Ops, SparseCore 0:
  42.5 64.5 all-gather.2
  111.1 163.9 all-reduce.1
where the time goes:
time: 337 us; the launch traced here: 336 us
  waiting for transfers between devices  216 us (64%)
  matrix products  29.7 us (9%)
  starting transfers between devices  27 us (8%)
  blocking collectives  23.8 us (7%)
  between operations  16.3 us (5%)
  local copies, waits for them, and re-layouts  12.2 us (4%)
  other arithmetic  11.3 us (3%)
    psum x1, waiting for transfers between devices, shards(): grad = lax.psum(partial_grad, 'rep')  149 us
    all_to_all x1, waiting for transfers between devices, shards(): lax.all_to_all(ordered, 'grp', split_axis=1, concat_axis=0, tiled=True)  50 us
    all_gather x1, blocking collectives, shards(): directions = lax.all_gather(own_rows, 'grp', axis=0, tiled=True)  23.8 us
    all_to_all x1, starting transfers between devices, shards(): lax.all_to_all(ordered, 'grp', split_axis=1, concat_axis=0, tiled=True)  18.3 us
    all_gather x1, waiting for transfers between devices, shards(): lax.all_gather(features, 'grp', axis=0, tiled=True)  8.42 us
    all_to_all x1, waiting for transfers between devices, shards(): lax.all_to_all(slot_deltas, 'grp', split_axis=1, concat_axis=0, tiled=True)  7.69 us
  transfers between devices with their start and end apart: 5, of which 4 were waited for; matrix products, arithmetic and copies ran while one was open for 3% of the time, Pallas kernels for 0%

commit v1 on v0

v1 whole, which is shorter than its diff:
```python
from functools import partial

import jax
import jax.numpy as jnp
from jax import lax
from jax.experimental import pallas as pl
from jax.experimental.pallas import tpu as pltpu
from jax.sharding import PartitionSpec as P

SIDE = 8
AXES = ("grp", "rep")
MIB = 1 << 20


def device(x, y, z, core):
    return ((z % SIDE) * 2 + core) * (SIDE * SIDE) + (x % SIDE) * SIDE + y % SIDE


def chips():
    for x in range(SIDE):
        for y in range(SIDE):
            for z in range(SIDE):
                yield x, y, z


def parity(x, y, z):
    return (y % 2) * 4 + (z % 2) * 2 + x % 2


def cube_groups():
    groups = []
    for core in range(2):
        for x, y, z in chips():
            if x % 2 != core or y % 2 != core or z % 2 != core:
                continue
            members = [None] * 8
            for dx in range(2):
                for dy in range(2):
                    for dz in range(2):
                        spot = ((x + dx) % SIDE, (y + dy) % SIDE, (z + dz) % SIDE)
                        members[parity(*spot)] = device(*spot, core)
            groups.append(members)
    return groups


def piece(x, y, z):
    return (((x // 2) * 4 + y // 2) * 2) + (z // 2) % 2


def stride_groups(split):
    groups = {}
    for core in range(2):
        for x, y, z in chips():
            half = z // 4
            key = (core, parity(x, y, z)) + ((half,) if split else ())
            order = piece(x, y, z) + (0 if split else 32 * half)
            groups.setdefault(key, []).append((order, device(x, y, z, core)))
    return [[d for _, d in sorted(members)] for members in groups.values()]


def core_pairs():
    return [(device(x, y, z, c), device(x, y, z, 1 - c)) for x, y, z in chips() for c in range(2)]


def home_pairs():
    pairs = []
    for x, y, z in chips():
        for core in range(2):
            to_x = (x & 4) | (core << 1) | ((x >> 1) & 1)
            to_y = (y & 6) | ((z >> 1) & 1)
            to_z = (z & 5) | ((y & 1) << 1)
            pairs.append((device(x, y, z, core), device(to_x, to_y, to_z, x & 1)))
    return pairs


def tokens_kernel(order, grads, features, out, sems):
    copies = []
    for spot in range(8):
        for k in range(2):
            first = pl.multiple_of(order[spot + 8 * k] * 512, 512)
            copies.append((grads.at[:, pl.ds(first, 512)], out.at[spot, k]))
        copies.append((features, out.at[spot, 2]))
    started = []
    for n, (source, target) in enumerate(copies):
        copy = pltpu.make_async_copy(source, target, sems.at[n])
        copy.start()
        started.append(copy)
    for copy in started:
        copy.wait()


def pack_tokens(order, grads, features):
    return pl.pallas_call(
        tokens_kernel,
        out_shape=jax.ShapeDtypeStruct((8, 3, 128, 512), jnp.bfloat16),
        in_specs=[
            pl.BlockSpec(memory_space=pltpu.SMEM),
            pl.BlockSpec(memory_space=pl.ANY),
            pl.BlockSpec(memory_space=pl.ANY),
        ],
        out_specs=pl.BlockSpec(memory_space=pl.ANY),
        scratch_shapes=[pltpu.SemaphoreType.DMA((24,))],
    )(order, grads, features)


def slots_kernel(live, rows, owner_col, owner_row, deltas, out):
    count = deltas.shape[0]
    before = lax.broadcasted_iota(jnp.int32, (count, count), 0)
    after = lax.broadcasted_iota(jnp.int32, (count, count), 1)
    same = (owner_col[...] == owner_row[...]) & (before < after)
    rank = jnp.sum(same.astype(jnp.float32), axis=0, keepdims=True)
    position = owner_row[...].astype(jnp.float32) * 16.0 + rank
    place = lax.broadcasted_iota(jnp.int32, (256, count), 0).astype(jnp.float32) == position
    place = place.astype(jnp.float32).astype(jnp.bfloat16)
    masked = jnp.where(before < live[0], deltas[...].astype(jnp.float32), 0.0).astype(jnp.bfloat16)
    high, low = rows[...] // 16, rows[...] % 16
    keys = jnp.where(after < 64, high, low).astype(jnp.float32).astype(jnp.bfloat16)
    moved = jnp.dot(place, masked, preferred_element_type=jnp.float32).astype(jnp.bfloat16)
    named = jnp.dot(place, keys, preferred_element_type=jnp.float32).astype(jnp.bfloat16)
    out[:, 0:16, :] = moved.reshape(16, 16, 128)
    out[:, 16:32, :] = named.reshape(16, 16, 128)


def pack_slots(live, rows, owner, deltas):
    vmem = pl.BlockSpec(memory_space=pltpu.VMEM)
    return pl.pallas_call(
        slots_kernel,
        out_shape=jax.ShapeDtypeStruct((16, 32, 128), jnp.bfloat16),
        in_specs=[pl.BlockSpec(memory_space=pltpu.SMEM), vmem, vmem, vmem, vmem],
        out_specs=vmem,
    )(live, rows.reshape(-1, 1), owner, owner.reshape(1, -1), deltas)


def grad_kernel(half, tokens, out):
    first = pl.multiple_of(half[0] * 128, 128)
    second = pl.multiple_of(256 + half[0] * 128, 128)
    left = jnp.concatenate(
        [
            tokens[:, 2, :, pl.ds(first, 128)].reshape(1024, 128),
            tokens[:, 2, :, pl.ds(second, 128)].reshape(1024, 128),
        ],
        axis=1,
    )
    for k in range(2):
        result = lax.dot_general(
            left,
            tokens[:, k, :, :].reshape(1024, 512),
            (((0,), (0,)), ((), ())),
            preferred_element_type=jnp.float32,
        )
        out[k] = result.reshape(2, 128, 512)


def partial_grads(half, tokens):
    return pl.pallas_call(
        grad_kernel,
        out_shape=jax.ShapeDtypeStruct((2, 2, 128, 512), jnp.float32),
        in_specs=[pl.BlockSpec(memory_space=pltpu.SMEM), pl.BlockSpec(memory_space=pltpu.VMEM)],
        out_specs=pl.BlockSpec(memory_space=pltpu.VMEM),
        compiler_params=pltpu.CompilerParams(vmem_limit_bytes=32 * MIB),
        cost_estimate=pl.CostEstimate(flops=1 << 29, bytes_accessed=4 * MIB, transcendentals=0),
    )(half, tokens)


def parts_of(value):
    high = value.astype(jnp.bfloat16)
    return high, (value - high.astype(jnp.float32)).astype(jnp.bfloat16)


def product(a, b, contract):
    return lax.dot_general(a, b, (contract, ((), ())), preferred_element_type=jnp.float32)


def full_product(a, b, contract):
    (ah, al), (bh, bl) = a, b
    return product(ah, bh, contract) + (product(ah, bl, contract) + product(al, bh, contract))


def rows_product(rows, b):
    bh, bl = b
    count = rows.shape[0]
    high, low = parts_of(rows)
    both = jnp.concatenate([high.astype(jnp.float32), low.astype(jnp.float32)], axis=0)
    first = product(both.astype(jnp.bfloat16), bh, ((1,), (0,)))
    return first[:count] + (first[count:] + product(high, bl, ((1,), (0,))))


def direction_kernel(place, own, other, out, grad, power, square):
    half, first_row = place[0], pl.multiple_of(place[1], 8)
    for k in range(2):
        grad[pl.ds(pl.multiple_of(k * 256 + half * 128, 128), 128), :] = own[k]
        grad[pl.ds(pl.multiple_of(k * 256 + (1 - half) * 128, 128), 128), :] = other[k]
    g = grad[...]
    width = g.shape[0]
    frobenius = jnp.sum(g * g) + 1e-06
    g_parts = parts_of(g)
    normal = full_product(g_parts, g_parts, ((1,), (1,))) / frobenius
    n_parts = parts_of(normal)
    squared = full_product(n_parts, n_parts, ((1,), (0,)))
    total = jnp.sum(jnp.sum(squared * squared, axis=0, keepdims=True), axis=1, keepdims=True)
    bound = jnp.sqrt(jnp.sqrt(total))
    scale = frobenius * bound
    m = normal / bound
    m2 = squared / (bound * bound)
    power[...] = m
    square[...] = m2
    diagonal = lax.broadcasted_iota(jnp.int32, (width, width), 0) == lax.broadcasted_iota(
        jnp.int32, (width, width), 1
    )
    f2 = (jnp.where(diagonal, 25.0, 0.0) - 10.0 * m + m2) / 16.0
    m_parts, f_parts = parts_of(m), parts_of(f2)
    m_rows = power[pl.ds(first_row, 8), :]
    m2_rows = square[pl.ds(first_row, 8), :]
    basis = lax.broadcasted_iota(jnp.int32, (8, width), 1) == first_row + lax.broadcasted_iota(
        jnp.int32, (8, width), 0
    )
    f_rows = (jnp.where(basis, 5.0, 0.0) - m_rows) / 4.0
    fm_rows = (5.0 * m_rows - m2_rows) / 4.0
    root = (5.0 * f_rows - rows_product(rows_product(fm_rows, f_parts), f_parts)) / 4.0
    m_root = rows_product(root, m_parts)
    m2_root = rows_product(m_root, m_parts)
    f_rows = (5.0 * root - m_root) / 4.0
    fm_rows = (5.0 * m_root - m2_root) / 4.0
    root = (5.0 * f_rows - rows_product(rows_product(fm_rows, f_parts), f_parts)) / 4.0
    quarter = 1.0 / jnp.sqrt(jnp.sqrt(scale))
    result = rows_product(root * quarter, g_parts) * quarter * float(width)
    tall = jnp.concatenate([result[:, t * 128 : (t + 1) * 128] for t in range(4)], axis=0)
    out[...] = tall.astype(jnp.bfloat16)


def direction_rows(place, own, other):
    vmem = pl.BlockSpec(memory_space=pltpu.VMEM)
    square = pltpu.VMEM((512, 512), jnp.float32)
    return pl.pallas_call(
        direction_kernel,
        out_shape=jax.ShapeDtypeStruct((32, 128), jnp.bfloat16),
        in_specs=[pl.BlockSpec(memory_space=pltpu.SMEM), vmem, vmem],
        out_specs=vmem,
        scratch_shapes=[square, square, square],
        compiler_params=pltpu.CompilerParams(vmem_limit_bytes=40 * MIB),
    )(place, own, other)


def message_kernel(rows, slots, out):
    for target in range(16):
        out[target, 0:32, :] = rows[...]
    out[:, 32:64, :] = slots[...]


def final_message(rows, slots):
    vmem = pl.BlockSpec(memory_space=pltpu.VMEM)
    return pl.pallas_call(
        message_kernel,
        out_shape=jax.ShapeDtypeStruct((16, 64, 128), jnp.bfloat16),
        in_specs=[vmem, vmem],
        out_specs=vmem,
    )(rows, slots)


def update_kernel(got, table, accum, new_table, new_accum, directions):
    rows = got[:, 0:32, :].astype(jnp.float32).reshape(16, 4, 8, 128)
    wide = jnp.concatenate([rows[:, t] for t in range(4)], axis=2)
    directions[...] = wide.astype(jnp.bfloat16)
    deltas = got[:, 32:48, :].reshape(256, 128)
    keys = got[:, 48:64, :].astype(jnp.float32).reshape(256, 128)
    row = keys[:, 0:1] * 16.0 + keys[:, 64:65]
    count = table.shape[0]
    named = row == lax.broadcasted_iota(jnp.int32, (256, count), 1).astype(jnp.float32)
    named = named.astype(jnp.float32).astype(jnp.bfloat16)
    summed = lax.dot_general(
        named, deltas, (((0,), (0,)), ((), ())), preferred_element_type=jnp.float32
    )
    before = jnp.transpose(jnp.broadcast_to(accum[...], (128, count)))
    after = before + jnp.sum(summed * summed, axis=1, keepdims=True) / 128.0
    new_table[...] = table[...] - summed / jnp.sqrt(after)
    new_accum[...] = jnp.transpose(after)[0:1, :]


def update_rows(got, table, accum):
    vmem = pl.BlockSpec(memory_space=pltpu.VMEM)
    return pl.pallas_call(
        update_kernel,
        out_shape=(
            jax.ShapeDtypeStruct(table.shape, jnp.float32),
            jax.ShapeDtypeStruct((1, accum.shape[0]), jnp.float32),
            jax.ShapeDtypeStruct((16, 8, 512), jnp.bfloat16),
        ),
        in_specs=[vmem, vmem, vmem],
        out_specs=(vmem, vmem, vmem),
    )(got, table, accum.reshape(1, -1))


def shards(
    features,
    output_grads,
    block_order,
    emb_table,
    row_accum,
    hot_rows,
    hot_owner,
    live_counts,
    hot_deltas,
):
    group, replica = lax.axis_index("grp"), lax.axis_index("rep")
    core, z = group % 2, group // 2
    x, y = replica // SIDE, replica % SIDE
    exchange = partial(lax.all_to_all, split_axis=0, concat_axis=0, tiled=True)

    slots = pack_slots(live_counts, hot_rows, hot_owner, hot_deltas)

    message = pack_tokens(block_order, output_grads, features)
    tokens = exchange(message, AXES, axis_index_groups=cube_groups())

    away = partial_grads((1 - core).reshape(1), tokens)
    arrived = lax.ppermute(away, AXES, core_pairs())
    kept = partial_grads(core.reshape(1), tokens)
    shared = (kept + arrived).reshape(64, 8, 512)
    terms = exchange(shared, AXES, axis_index_groups=stride_groups(False))
    reduced = jnp.sum(terms, axis=0)

    spread = jnp.broadcast_to(reduced[None], (32, 8, 512))
    own = exchange(spread, AXES, axis_index_groups=stride_groups(True)).reshape(2, 128, 512)
    other = lax.ppermute(own, AXES, core_pairs())
    turn = piece(x, y, z)
    first_row = (turn // 16) * 256 + core * 128 + (turn % 16) * 8
    rows = direction_rows(jnp.stack([core, first_row]).astype(jnp.int32), own, other)

    home = lax.ppermute(rows, AXES, home_pairs())
    got = exchange(final_message(home, slots), "grp")
    new_table, new_accum, directions = update_rows(got, emb_table, row_accum)
    return (new_table, new_accum.reshape(-1), directions)


def solution(mesh):
    return jax.shard_map(
        shards,
        mesh=mesh,
        in_specs=(
            P(AXES, None),
            P(AXES, None),
            P(),
            P(AXES, None),
            P(AXES),
            P(AXES),
            P(AXES, None),
            P(AXES),
            P(AXES, None),
        ),
        out_specs=(P(AXES, None), P(AXES), P(None, "rep", None)),
        check_vma=False,
    )
```

time: 337 us -> 265 us (0.79)
  waiting for transfers between devices: 216 us -> 30.2 us
  Pallas kernels: 0 us -> 109 us
  blocking collectives: 23.8 us -> 83.4 us
  matrix products: 29.7 us -> 0 us
  between operations: 16.3 us -> 1.51 us
  other arithmetic: 11.3 us -> 0.38 us
  local copies, waits for them, and re-layouts: 12.2 us -> 2.15 us
  starting transfers between devices: 27 us -> 34.3 us
    psum x1 -> x0, waiting for transfers between devices: 149 us -> none  [shards(): grad = lax.psum(partial_grad, 'rep')]
    pallas_call x0 -> x7, Pallas kernels: none -> 109 us  [the longest x1 97.3 us: pack_tokens(): pl.pallas_call(tokens_kernel, out_shape=jax.ShapeDtypeStruct((8, 3, 128,...]
    all_to_all x0 -> x3, blocking collectives: none -> 83.4 us  [the longest x1 38.9 us: shards(): terms = exchange(shared, AXES, axis_index_groups=stride_groups(False))]
    all_to_all x3 -> x1, waiting for transfers between devices: 57.7 us -> 24.9 us  [shards(): tokens = exchange(message, AXES, axis_index_groups=cube_groups())]
    dot_general x28 -> x0, matrix products: 29.7 us -> none  [the longest x6 5.82 us: right_gram(): return jnp.dot(inner, grad, precision=highest) / scale]
    all_gather x1 -> x0, blocking collectives: 23.8 us -> none  [shards(): directions = lax.all_gather(own_rows, 'grp', axis=0, tiled=True)]
    ppermute x0 -> x3, starting transfers between devices: none -> 11 us  [the longest x1 4.76 us: shards(): other = lax.ppermute(own, AXES, core_pairs())]
    all_gather x1 -> x0, waiting for transfers between devices: 8.42 us -> none  [shards(): lax.all_gather(features, 'grp', axis=0, tiled=True)]
  transfers between devices with their start and end apart: 5 -> 4, of which waited for: 4 -> 4; matrix products, arithmetic and copies ran while one was open for 3% -> 1% of each run, Pallas kernels for 0% -> 1%
where the time goes in v1:
time: 265 us; the launch traced here: 261 us
  Pallas kernels  109 us (41%)
  blocking collectives  83.4 us (31%)
  starting transfers between devices  34.3 us (13%)
  waiting for transfers between devices  30.2 us (11%)
    pallas_call x1, Pallas kernels, pack_tokens(): pl.pallas_call(tokens_kernel, out_shape=jax.ShapeDtypeStruct((8, 3, 128,...  97.3 us
    all_to_all x1, blocking collectives, shards(): terms = exchange(shared, AXES, axis_index_groups=stride_groups(False))  38.9 us
    all_to_all x1, blocking collectives, shards(): exchange(spread, AXES, axis_index_groups=stride_groups(True))  29.6 us
    all_to_all x1, waiting for transfers between devices, shards(): tokens = exchange(message, AXES, axis_index_groups=cube_groups())  24.9 us
    all_to_all x1, starting transfers between devices, shards(): tokens = exchange(message, AXES, axis_index_groups=cube_groups())  23.3 us
    all_to_all x1, blocking collectives, shards(): got = exchange(final_message(home, slots), 'grp')  14.8 us
  transfers between devices with their start and end apart: 4, of which 4 were waited for; matrix products, arithmetic and copies ran while one was open for 1% of the time, Pallas kernels for 1%

profile of v1, /device:TPU:1, one launch (start us, length us, event | category | flops | bytes accessed | tf_op | source)
XLA Modules:
  0.0 261.0 jit_solution(6700123140877311899)
XLA Ops:
  0.6 97.3 %shard_map.112 = bf16[8,3,128,512]{3,2,1,0:T(8,128)(2,1)} custom-call(s32[16]{0:T(128)} %order.1, bf16[128,8192]{1,0:T(8,128)(2,1)} %grads.1, bf16[128,512]{1,0:T(8,128)(2,1)} %features.1), custom_call_target="tpu_custom_call" | custom-call | tf_op jit(solution)/shard_map/pallas_call | solution.py:93
  97.9 23.3 %all-to-all-start = ((bf16[8,3,128,512]{3,2,1,0:T(8,128)(2,1)}), bf16[8,3,128,512]{3,2,1,0:T(8,128)(2,1)S(1)}, u32[]{:S(2)}, u32[]{:S(2)}) async-start(bf16[8,3,128,512]{3,2,1,0:T(8,128)(2,1)} %shard_map.112), calls=%async_computation | async-start | bytes 6291456 | tf_op jit(solution)/shard_map/all_to_all | solution.py:312
  121.2 24.9 %all-to-all-done.tokens = bf16[8,3,128,512]{3,2,1,0:T(8,128)(2,1)S(1)} async-done(((bf16[8,3,128,512]{3,2,1,0:T(8,128)(2,1)}), bf16[8,3,128,512]{3,2,1,0:T(8,128)(2,1)S(1)}, u32[]{:S(2)}, u32[]{:S(2)}) %all-to-all-start) | async-done | bytes 3145760 | tf_op jit(solution)/shard_map/all_to_all | solution.py:312
  146.1 0.7 shard_map.114
  146.9 1.9 collective-permute-start
  148.8 0.7 shard_map.113
  149.5 1.9 collective-permute-done
  151.4 0.2 add.42
  151.6 38.9 %all_to_all.20 = f32[64,8,512]{2,1,0:T(8,128)S(1)} all-to-all(f32[64,8,512]{2,1,0:T(8,128)S(1)} %bitcast.11), channel_id=1, replica_groups={{0,256,2,258,4,260,6,262,16,272,18,274,20,276,22,278,32,288,34,290,36,2..., dimensions={0} | all-to-all | bytes 2097152 | tf_op jit(solution)/shard_map/all_to_all | solution.py:318
  190.6 0.1 reduce_sum.9
  190.7 29.6 %all_to_all.21 = f32[32,8,512]{2,1,0:T(8,128)S(1)} all-to-all(f32[32,8,512]{2,1,0:T(8,128)S(1)} %broadcast_in_dim.2), channel_id=1, replica_groups={{0,256,2,258,4,260,6,262,16,272,18,274,20,276,22,278,32,288,34,290,36,2..., dimensions={0} | all-to-all | bytes 1048576 | tf_op jit(solution)/shard_map/all_to_all | solution.py:322
  220.4 4.8 %collective-permute-start.1 = (f32[2,128,512]{2,1,0:T(8,128)S(1)}, f32[2,128,512]{2,1,0:T(8,128)S(1)}, u32[]{:S(2)}, u32[]{:S(2)}) collective-permute-start(f32[2,128,512]{2,1,0:T(8,128)S(1)} %bitcast.9), channel_id=1, source_target_pairs={{0,64},{64,0},{128,192},{192,128},{256,320},{320,256},{384,448},{4... | collective-permute-start | bytes 1572872 | tf_op jit(solution)/shard_map/ppermute | solution.py:323
  225.3 0.1 pad_add_fusion.place
  225.4 1.3 collective-permute-done.1.other
  226.7 4.6 %shard_map.115 = bf16[32,128]{1,0:T(8,128)(2,1)S(1)} custom-call(s32[2]{0:T(128)S(1)} %pad_add_fusion.place, f32[2,128,512]{2,1,0:T(8,128)S(1)} %bitcast.10, f32[2,128,512]{2,1,0:T(8,128)S(1)} %collective-permute-done.1.other), custom_call_target="tpu_custom_call" | custom-call | tf_op jit(solution)/shard_map/pallas_call | solution.py:234
  231.2 4.3 %collective-permute-start.2 = (bf16[32,128]{1,0:T(8,128)(2,1)S(1)}, bf16[32,128]{1,0:T(8,128)(2,1)S(1)}, u32[]{:S(2)}, u32[]{:S(2)}) collective-permute-start(bf16[32,128]{1,0:T(8,128)(2,1)S(1)} %shard_map.115), channel_id=1, source_target_pairs={{0,0},{64,16},{128,128},{192,144},{256,1},{320,17},{384,129},{448,... | collective-permute-start | bytes 24584 | tf_op jit(solution)/shard_map/ppermute | solution.py:328
  236.3 0.7 copy.12.rows
  237.0 0.7 copy.13.owner_col
  237.7 1.8 shard_map.116.slots
  239.5 2.1 collective-permute-done.2.rows
  241.7 0.6 copy-done
  242.3 1.7 shard_map.117
  243.9 14.8 %all_to_all.22.got = bf16[16,64,128]{2,1,0:T(8,128)(2,1)} all-to-all(bf16[16,64,128]{2,1,0:T(8,128)(2,1)} %shard_map.117), channel_id=1, replica_groups=mesh['grp'=16,'rep'=64] {'grp'}, dimensions={0} | all-to-all | bytes 524288 | tf_op jit(solution)/shard_map/all_to_all | solution.py:329
  258.7 2.3 shard_map.118
  (6 shorter events, 0.1 us)
Async XLA Ops:
  97.9 48.2 %all-to-all-start = ((bf16[8,3,128,512]{3,2,1,0:T(8,128)(2,1)}), bf16[8,3,128,512]{3,2,1,0:T(8,128)(2,1)S(1)}, u32[]{:S(2)}, u32[]{:S(2)}) async-start(bf16[8,3,128,512]{3,2,1,0:T(8,128)(2,1)} %shard_map.112), calls=%async_computation | async-start | bytes 6291456 | tf_op jit(solution)/shard_map/all_to_all | solution.py:312
  146.9 4.6 %collective-permute-start = (f32[2,2,128,512]{3,2,1,0:T(8,128)S(1)}, f32[2,2,128,512]{3,2,1,0:T(8,128)S(1)}, u32[]{:S(2)}, u32[]{:S(2)}) collective-permute-start(f32[2,2,128,512]{3,2,1,0:T(8,128)S(1)} %shard_map.114), channel_id=1, source_target_pairs={{0,64},{64,0},{128,192},{192,128},{256,320},{320,256},{384,448},{4... | collective-permute-start | bytes 3145736 | tf_op jit(solution)/shard_map/ppermute | solution.py:315
  151.6 84.6 %copy-start.2 = (s32[128]{0:T(128)S(1)}, s32[128]{0:T(128)}, u32[]{:S(2)}) copy-start(s32[128]{0:T(128)} %param.14) | copy-start | bytes 1540
  151.6 85.4 %copy-start.1 = (s32[128,1]{0,1:T(1,128)S(1)}, s32[128,1]{0,1:T(1,128)}, u32[]{:S(2)}) copy-start(s32[128,1]{0,1:T(1,128)} %param.15) | copy-start | bytes 1540
  220.4 6.3 %collective-permute-start.1 = (f32[2,128,512]{2,1,0:T(8,128)S(1)}, f32[2,128,512]{2,1,0:T(8,128)S(1)}, u32[]{:S(2)}, u32[]{:S(2)}) collective-permute-start(f32[2,128,512]{2,1,0:T(8,128)S(1)} %bitcast.9), channel_id=1, source_target_pairs={{0,64},{64,0},{128,192},{192,128},{256,320},{320,256},{384,448},{4... | collective-permute-start | bytes 1572872 | tf_op jit(solution)/shard_map/ppermute | solution.py:323
  231.2 10.4 %collective-permute-start.2 = (bf16[32,128]{1,0:T(8,128)(2,1)S(1)}, bf16[32,128]{1,0:T(8,128)(2,1)S(1)}, u32[]{:S(2)}, u32[]{:S(2)}) collective-permute-start(bf16[32,128]{1,0:T(8,128)(2,1)S(1)} %shard_map.115), channel_id=1, source_target_pairs={{0,0},{64,16},{128,128},{192,144},{256,1},{320,17},{384,129},{448,... | collective-permute-start | bytes 24584 | tf_op jit(solution)/shard_map/ppermute | solution.py:328
  241.7 0.6 copy-start

commit v2 on v1

--- a/solution.py
+++ b/solution.py
@@ -73,33 +73,22 @@
     return pairs
 
 
-def tokens_kernel(order, grads, features, out, sems):
-    copies = []
+def tokens_kernel(order, grads, features, out):
     for spot in range(8):
         for k in range(2):
             first = pl.multiple_of(order[spot + 8 * k] * 512, 512)
-            copies.append((grads.at[:, pl.ds(first, 512)], out.at[spot, k]))
-        copies.append((features, out.at[spot, 2]))
-    started = []
-    for n, (source, target) in enumerate(copies):
-        copy = pltpu.make_async_copy(source, target, sems.at[n])
-        copy.start()
-        started.append(copy)
-    for copy in started:
-        copy.wait()
+            out[spot, k] = grads[:, pl.ds(first, 512)]
+        out[spot, 2] = features[...]
 
 
 def pack_tokens(order, grads, features):
+    vmem = pl.BlockSpec(memory_space=pltpu.VMEM)
     return pl.pallas_call(
         tokens_kernel,
         out_shape=jax.ShapeDtypeStruct((8, 3, 128, 512), jnp.bfloat16),
-        in_specs=[
-            pl.BlockSpec(memory_space=pltpu.SMEM),
-            pl.BlockSpec(memory_space=pl.ANY),
-            pl.BlockSpec(memory_space=pl.ANY),
-        ],
-        out_specs=pl.BlockSpec(memory_space=pl.ANY),
-        scratch_shapes=[pltpu.SemaphoreType.DMA((24,))],
+        in_specs=[pl.BlockSpec(memory_space=pltpu.SMEM), vmem, vmem],
+        out_specs=vmem,
+        compiler_params=pltpu.CompilerParams(vmem_limit_bytes=32 * MIB),
     )(order, grads, features)
 
 
@@ -310,6 +299,7 @@
 
     message = pack_tokens(block_order, output_grads, features)
     tokens = exchange(message, AXES, axis_index_groups=cube_groups())
+    tokens, slots = lax.optimization_barrier((tokens, slots))
 
     away = partial_grads((1 - core).reshape(1), tokens)
     arrived = lax.ppermute(away, AXES, core_pairs())

time: 265 us -> 173 us (0.65)
  Pallas kernels: 109 us -> 12.6 us
  local copies, waits for them, and re-layouts: 2.15 us -> 6.89 us
    pallas_call x1, Pallas kernels: 97.3 us -> 0.75 us  [pack_tokens(): pl.pallas_call(tokens_kernel, out_shape=jax.ShapeDtypeStruct((8, 3, 128,...]
    unnamed x7 -> x15, local copies, waits for them, and re-layouts: 1.35 us -> 6.09 us
    ppermute x1, waiting for transfers between devices: 2.11 us -> 6.08 us  [shards(): home = lax.ppermute(rows, AXES, home_pairs())]
    all_to_all x1, waiting for transfers between devices: 24.9 us -> 21 us  [shards(): tokens = exchange(message, AXES, axis_index_groups=cube_groups())]
  transfers between devices with their start and end apart: 4 -> 4, of which waited for: 4 -> 4; matrix products, arithmetic and copies ran while one was open for 1% -> 1% of each run, Pallas kernels for 1% -> 2%
where the time goes in v2:
time: 173 us; the launch traced here: 169 us
  blocking collectives  83.2 us (48%)
  starting transfers between devices  34.5 us (20%)
  waiting for transfers between devices  30.3 us (18%)
  Pallas kernels  12.6 us (7%)
  local copies, waits for them, and re-layouts  6.89 us (4%)
    all_to_all x1, blocking collectives, shards(): terms = exchange(shared, AXES, axis_index_groups=stride_groups(False))  38.9 us
    all_to_all x1, blocking collectives, shards(): exchange(spread, AXES, axis_index_groups=stride_groups(True))  29.4 us
    all_to_all x1, starting transfers between devices, shards(): tokens = exchange(message, AXES, axis_index_groups=cube_groups())  23.4 us
    all_to_all x1, waiting for transfers between devices, shards(): tokens = exchange(message, AXES, axis_index_groups=cube_groups())  21 us
    all_to_all x1, blocking collectives, shards(): got = exchange(final_message(home, slots), 'grp')  14.9 us
    unnamed x15, local copies, waits for them, and re-layouts  6.09 us
    ppermute x1, waiting for transfers between devices, shards(): home = lax.ppermute(rows, AXES, home_pairs())  6.08 us
    ppermute x1, starting transfers between devices, shards(): other = lax.ppermute(own, AXES, core_pairs())  4.79 us
  transfers between devices with their start and end apart: 4, of which 4 were waited for; matrix products, arithmetic and copies ran while one was open for 1% of the time, Pallas kernels for 2%

profile of v2, /device:TPU:1, one launch (start us, length us, event | category | flops | bytes accessed | tf_op | source)
XLA Modules:
  0.0 169.3 jit_solution(4232212769589186)
XLA Ops:
  0.6 1.6 copy-done.1
  2.2 0.9 copy-done.2
  3.1 0.7 copy-done.3
  3.8 0.7 shard_map.112
  4.5 1.6 copy-done
  6.2 23.4 %all-to-all-start = ((bf16[8,3,128,512]{3,2,1,0:T(8,128)(2,1)}), bf16[8,3,128,512]{3,2,1,0:T(8,128)(2,1)S(1)}, u32[]{:S(2)}, u32[]{:S(2)}) async-start(bf16[8,3,128,512]{3,2,1,0:T(8,128)(2,1)} %copy-done), calls=%async_computation | async-start | bytes 6291456 | tf_op jit(solution)/shard_map/all_to_all | solution.py:301
  30.2 0.7 copy.12.rows
  31.0 0.7 copy.13.owner_col
  31.7 1.8 %shard_map.113.slots = bf16[16,32,128]{2,1,0:T(8,128)(2,1)} custom-call(s32[1]{0:T(128)S(6)} %copy.14.live, s32[128,1]{1,0:T(8,128)} %copy.12.rows, s32[128,1]{1,0:T(8,128)} %copy.13.owner_col, s32[1,128]{1,0:T(1,128)} %bitcast.13, bf16[128,128]{1,0:T(8,128)(2,1)} %deltas.1), custom_call_target="tpu_custom_call" | custom-call | tf_op jit(solution)/shard_map/pallas_call | solution.py:115
  33.5 21.0 %all-to-all-done.tokens = bf16[8,3,128,512]{3,2,1,0:T(8,128)(2,1)S(1)} async-done(((bf16[8,3,128,512]{3,2,1,0:T(8,128)(2,1)}), bf16[8,3,128,512]{3,2,1,0:T(8,128)(2,1)S(1)}, u32[]{:S(2)}, u32[]{:S(2)}) %all-to-all-start) | async-done | bytes 3145760 | tf_op jit(solution)/shard_map/all_to_all | solution.py:301
  54.5 0.7 shard_map.115
  55.2 1.9 %collective-permute-start = (f32[2,2,128,512]{3,2,1,0:T(8,128)S(1)}, f32[2,2,128,512]{3,2,1,0:T(8,128)S(1)}, u32[]{:S(2)}, u32[]{:S(2)}) collective-permute-start(f32[2,2,128,512]{3,2,1,0:T(8,128)S(1)} %shard_map.115), channel_id=1, source_target_pairs={{0,64},{64,0},{128,192},{192,128},{256,320},{320,256},{384,448},{4... | collective-permute-start | bytes 3145736 | tf_op jit(solution)/shard_map/ppermute | solution.py:305
  57.2 0.7 shard_map.114
  57.9 1.9 %collective-permute-done = f32[2,2,128,512]{3,2,1,0:T(8,128)S(1)} collective-permute-done((f32[2,2,128,512]{3,2,1,0:T(8,128)S(1)}, f32[2,2,128,512]{3,2,1,0:T(8,128)S(1)}, u32[]{:S(2)}, u32[]{:S(2)}) %collective-permute-start) | collective-permute-done | bytes 1048608 | tf_op jit(solution)/shard_map/ppermute | solution.py:305
  60.0 38.9 %all_to_all.20 = f32[64,8,512]{2,1,0:T(8,128)S(1)} all-to-all(f32[64,8,512]{2,1,0:T(8,128)S(1)} %bitcast.11), channel_id=1, replica_groups={{0,256,2,258,4,260,6,262,16,272,18,274,20,276,22,278,32,288,34,290,36,2..., dimensions={0} | all-to-all | bytes 2097152 | tf_op jit(solution)/shard_map/all_to_all | solution.py:308
  99.1 29.4 %all_to_all.21 = f32[32,8,512]{2,1,0:T(8,128)S(1)} all-to-all(f32[32,8,512]{2,1,0:T(8,128)S(1)} %broadcast_in_dim.2), channel_id=1, replica_groups={{0,256,2,258,4,260,6,262,16,272,18,274,20,276,22,278,32,288,34,290,36,2..., dimensions={0} | all-to-all | bytes 1048576 | tf_op jit(solution)/shard_map/all_to_all | solution.py:312
  128.5 4.8 %collective-permute-start.1 = (f32[2,128,512]{2,1,0:T(8,128)S(1)}, f32[2,128,512]{2,1,0:T(8,128)S(1)}, u32[]{:S(2)}, u32[]{:S(2)}) collective-permute-start(f32[2,128,512]{2,1,0:T(8,128)S(1)} %bitcast.9), channel_id=1, source_target_pairs={{0,64},{64,0},{128,192},{192,128},{256,320},{320,256},{384,448},{4... | collective-permute-start | bytes 1572872 | tf_op jit(solution)/shard_map/ppermute | solution.py:313
  133.5 1.3 collective-permute-done.1.other
  134.8 4.6 %shard_map.116 = bf16[32,128]{1,0:T(8,128)(2,1)S(1)} custom-call(s32[2]{0:T(128)S(1)} %pad_add_fusion.place, f32[2,128,512]{2,1,0:T(8,128)S(1)} %bitcast.10, f32[2,128,512]{2,1,0:T(8,128)S(1)} %collective-permute-done.1.other), custom_call_target="tpu_custom_call" | custom-call | tf_op jit(solution)/shard_map/pallas_call | solution.py:223
  139.4 4.4 %collective-permute-start.2 = (bf16[32,128]{1,0:T(8,128)(2,1)S(1)}, bf16[32,128]{1,0:T(8,128)(2,1)S(1)}, u32[]{:S(2)}, u32[]{:S(2)}) collective-permute-start(bf16[32,128]{1,0:T(8,128)(2,1)S(1)} %shard_map.116), channel_id=1, source_target_pairs={{0,0},{64,16},{128,128},{192,144},{256,1},{320,17},{384,129},{448,... | collective-permute-start | bytes 24584 | tf_op jit(solution)/shard_map/ppermute | solution.py:318
  143.8 6.1 %collective-permute-done.2.rows = bf16[32,128]{1,0:T(8,128)(2,1)S(1)} collective-permute-done((bf16[32,128]{1,0:T(8,128)(2,1)S(1)}, bf16[32,128]{1,0:T(8,128)(2,1)S(1)}, u32[]{:S(2)}, u32[]{:S(2)}) %collective-permute-start.2) | collective-permute-done | bytes 8224 | tf_op jit(solution)/shard_map/ppermute | solution.py:318
  150.5 1.7 shard_map.117
  152.1 14.9 %all_to_all.22.got = bf16[16,64,128]{2,1,0:T(8,128)(2,1)} all-to-all(bf16[16,64,128]{2,1,0:T(8,128)(2,1)} %shard_map.117), channel_id=1, replica_groups=mesh['grp'=16,'rep'=64] {'grp'}, dimensions={0} | all-to-all | bytes 524288 | tf_op jit(solution)/shard_map/all_to_all | solution.py:319
  167.0 2.3 %shard_map.118 = (f32[512,128]{1,0:T(8,128)}, f32[1,512]{1,0:T(1,128)}, bf16[16,8,512]{2,1,0:T(8,128)(2,1)}) custom-call(bf16[16,64,128]{2,1,0:T(8,128)(2,1)} %all_to_all.22.got, f32[512,128]{1,0:T(8,128)} %table.1, f32[1,512]{1,0:T(1,128)} %bitcast.12), custom_call_target="tpu_custom_call" | custom-call | tf_op jit(solution)/shard_map/pallas_call | solution.py:270
  (14 shorter events, 1.0 us)
Async XLA Ops:
  0.6 1.6 copy-start.1
  2.2 0.9 copy-start.2
  3.1 0.7 copy-start.3
  4.5 1.6 copy-start
  6.2 24.0 %copy-start.6 = (s32[128]{0:T(128)S(1)}, s32[128]{0:T(128)}, u32[]{:S(2)}) copy-start(s32[128]{0:T(128)} %param.14) | copy-start | bytes 1540
  6.2 24.8 %copy-start.5 = (s32[128,1]{0,1:T(1,128)S(1)}, s32[128,1]{0,1:T(1,128)}, u32[]{:S(2)}) copy-start(s32[128,1]{0,1:T(1,128)} %param.15) | copy-start | bytes 1540
  6.2 48.3 %all-to-all-start = ((bf16[8,3,128,512]{3,2,1,0:T(8,128)(2,1)}), bf16[8,3,128,512]{3,2,1,0:T(8,128)(2,1)S(1)}, u32[]{:S(2)}, u32[]{:S(2)}) async-start(bf16[8,3,128,512]{3,2,1,0:T(8,128)(2,1)} %copy-done), calls=%async_computation | async-start | bytes 6291456 | tf_op jit(solution)/shard_map/all_to_all | solution.py:301
  55.2 4.6 %collective-permute-start = (f32[2,2,128,512]{3,2,1,0:T(8,128)S(1)}, f32[2,2,128,512]{3,2,1,0:T(8,128)S(1)}, u32[]{:S(2)}, u32[]{:S(2)}) collective-permute-start(f32[2,2,128,512]{3,2,1,0:T(8,128)S(1)} %shard_map.115), channel_id=1, source_target_pairs={{0,64},{64,0},{128,192},{192,128},{256,320},{320,256},{384,448},{4... | collective-permute-start | bytes 3145736 | tf_op jit(solution)/shard_map/ppermute | solution.py:305
  128.5 6.3 %collective-permute-start.1 = (f32[2,128,512]{2,1,0:T(8,128)S(1)}, f32[2,128,512]{2,1,0:T(8,128)S(1)}, u32[]{:S(2)}, u32[]{:S(2)}) collective-permute-start(f32[2,128,512]{2,1,0:T(8,128)S(1)} %bitcast.9), channel_id=1, source_target_pairs={{0,64},{64,0},{128,192},{192,128},{256,320},{320,256},{384,448},{4... | collective-permute-start | bytes 1572872 | tf_op jit(solution)/shard_map/ppermute | solution.py:313
  139.4 10.5 %collective-permute-start.2 = (bf16[32,128]{1,0:T(8,128)(2,1)S(1)}, bf16[32,128]{1,0:T(8,128)(2,1)S(1)}, u32[]{:S(2)}, u32[]{:S(2)}) collective-permute-start(bf16[32,128]{1,0:T(8,128)(2,1)S(1)} %shard_map.116), channel_id=1, source_target_pairs={{0,0},{64,16},{128,128},{192,144},{256,1},{320,17},{384,129},{448,... | collective-permute-start | bytes 24584 | tf_op jit(solution)/shard_map/ppermute | solution.py:318
  149.9 0.6 copy-start.4

commit v3 on v2

--- a/solution.py
+++ b/solution.py
@@ -10,6 +10,7 @@
 SIDE = 8
 AXES = ("grp", "rep")
 MIB = 1 << 20
+CODE_RANGE = float((1 << 19) - 1)
 
 
 def device(x, y, z, core):
@@ -73,22 +74,42 @@
     return pairs
 
 
-def tokens_kernel(order, grads, features, out):
+def tokens_kernel(order, grads, features, out, held, arrive, leave):
+    copies = []
     for spot in range(8):
         for k in range(2):
             first = pl.multiple_of(order[spot + 8 * k] * 512, 512)
-            out[spot, k] = grads[:, pl.ds(first, 512)]
-        out[spot, 2] = features[...]
+            copies.append((grads.at[:, pl.ds(first, 512)], spot, k))
+        copies.append((features, spot, 2))
+    coming = []
+    for n, (source, spot, k) in enumerate(copies):
+        copy = pltpu.make_async_copy(source, held.at[spot, k], arrive.at[n])
+        copy.start()
+        coming.append(copy)
+    going = []
+    for n, (source, spot, k) in enumerate(copies):
+        coming[n].wait()
+        copy = pltpu.make_async_copy(held.at[spot, k], out.at[spot, k], leave.at[n])
+        copy.start()
+        going.append(copy)
+    for copy in going:
+        copy.wait()
 
 
 def pack_tokens(order, grads, features):
-    vmem = pl.BlockSpec(memory_space=pltpu.VMEM)
+    shape = (8, 3, 128, 512)
+    hbm = pl.BlockSpec(memory_space=pltpu.HBM)
     return pl.pallas_call(
         tokens_kernel,
-        out_shape=jax.ShapeDtypeStruct((8, 3, 128, 512), jnp.bfloat16),
-        in_specs=[pl.BlockSpec(memory_space=pltpu.SMEM), vmem, vmem],
-        out_specs=vmem,
-        compiler_params=pltpu.CompilerParams(vmem_limit_bytes=32 * MIB),
+        out_shape=jax.ShapeDtypeStruct(shape, jnp.bfloat16),
+        in_specs=[pl.BlockSpec(memory_space=pltpu.SMEM), hbm, hbm],
+        out_specs=hbm,
+        scratch_shapes=[
+            pltpu.VMEM(shape, jnp.bfloat16),
+            pltpu.SemaphoreType.DMA((24,)),
+            pltpu.SemaphoreType.DMA((24,)),
+        ],
+        compiler_params=pltpu.CompilerParams(vmem_limit_bytes=16 * MIB),
     )(order, grads, features)
 
 
@@ -151,6 +172,73 @@
     )(half, tokens)
 
 
+def encode(tiles):
+    largest = jnp.abs(tiles[0])
+    for tile in tiles[1:]:
+        largest = jnp.maximum(largest, jnp.abs(tile))
+    largest = jnp.max(jnp.max(largest, axis=1, keepdims=True), axis=2, keepdims=True)
+    grade = jnp.ceil(8.0 * jnp.log2(jnp.maximum(largest, 1e-30))) + 1.0
+    factor = CODE_RANGE * jnp.exp2(grade * -0.125)
+    words, low = [], None
+    for t, tile in enumerate(tiles):
+        whole = jnp.round(jnp.clip(tile * factor, -CODE_RANGE, CODE_RANGE)).astype(jnp.int32)
+        words.append(whole >> 4)
+        nibble = (whole & 15) << (4 * t)
+        low = nibble if low is None else low | nibble
+    spot = lax.broadcasted_iota(jnp.int32, low.shape, 1) + lax.broadcasted_iota(
+        jnp.int32, low.shape, 2
+    )
+    words.append(jnp.where(spot == 0, grade.astype(jnp.int32), low))
+    return jnp.concatenate(words, axis=1).astype(jnp.int16)
+
+
+def decode(words):
+    words = words.astype(jnp.int32)
+    low = words[:, 32:40, :]
+    grade = low[:, 0:1, 0:1].astype(jnp.float32)
+    factor = jnp.exp2(grade * 0.125) * (1.0 / CODE_RANGE)
+    tiles = []
+    for t in range(4):
+        whole = words[:, 8 * t : 8 * t + 8, :] * 16 + ((low >> (4 * t)) & 15)
+        tiles.append(whole.astype(jnp.float32) * factor)
+    return tiles
+
+
+def share_kernel(kept, arrived, out):
+    tiles = []
+    for t in range(4):
+        cut = slice(t * 128, (t + 1) * 128)
+        tiles.append((kept[:, :, :, cut] + arrived[:, :, :, cut]).reshape(64, 8, 128))
+    out[...] = encode(tiles)
+
+
+def share(kept, arrived):
+    vmem = pl.BlockSpec(memory_space=pltpu.VMEM)
+    return pl.pallas_call(
+        share_kernel,
+        out_shape=jax.ShapeDtypeStruct((64, 40, 128), jnp.int16),
+        in_specs=[vmem, vmem],
+        out_specs=vmem,
+        compiler_params=pltpu.CompilerParams(vmem_limit_bytes=32 * MIB),
+    )(kept, arrived)
+
+
+def total_kernel(terms, out):
+    words = encode([jnp.sum(tile, axis=0, keepdims=True) for tile in decode(terms[...])])
+    out[...] = jnp.broadcast_to(words.astype(jnp.int32), (32, 40, 128)).astype(jnp.int16)
+
+
+def total(terms):
+    vmem = pl.BlockSpec(memory_space=pltpu.VMEM)
+    return pl.pallas_call(
+        total_kernel,
+        out_shape=jax.ShapeDtypeStruct((32, 40, 128), jnp.int16),
+        in_specs=[vmem],
+        out_specs=vmem,
+        compiler_params=pltpu.CompilerParams(vmem_limit_bytes=32 * MIB),
+    )(terms)
+
+
 def parts_of(value):
     high = value.astype(jnp.bfloat16)
     return high, (value - high.astype(jnp.float32)).astype(jnp.bfloat16)
@@ -176,9 +264,12 @@
 
 def direction_kernel(place, own, other, out, grad, power, square):
     half, first_row = place[0], pl.multiple_of(place[1], 8)
-    for k in range(2):
-        grad[pl.ds(pl.multiple_of(k * 256 + half * 128, 128), 128), :] = own[k]
-        grad[pl.ds(pl.multiple_of(k * 256 + (1 - half) * 128, 128), 128), :] = other[k]
+    for side, words in ((half, own), (1 - half, other)):
+        for t, tile in enumerate(decode(words[...])):
+            tile = tile.reshape(2, 128, 128)
+            for k in range(2):
+                rows = pl.ds(pl.multiple_of(k * 256 + side * 128, 128), 128)
+                grad[rows, t * 128 : (t + 1) * 128] = tile[k]
     g = grad[...]
     width = g.shape[0]
     frobenius = jnp.sum(g * g) + 1e-06
@@ -304,12 +395,8 @@
     away = partial_grads((1 - core).reshape(1), tokens)
     arrived = lax.ppermute(away, AXES, core_pairs())
     kept = partial_grads(core.reshape(1), tokens)
-    shared = (kept + arrived).reshape(64, 8, 512)
-    terms = exchange(shared, AXES, axis_index_groups=stride_groups(False))
-    reduced = jnp.sum(terms, axis=0)
-
-    spread = jnp.broadcast_to(reduced[None], (32, 8, 512))
-    own = exchange(spread, AXES, axis_index_groups=stride_groups(True)).reshape(2, 128, 512)
+    terms = exchange(share(kept, arrived), AXES, axis_index_groups=stride_groups(False))
+    own = exchange(total(terms), AXES, axis_index_groups=stride_groups(True))
     other = lax.ppermute(own, AXES, core_pairs())
     turn = piece(x, y, z)
     first_row = (turn // 16) * 256 + core * 128 + (turn % 16) * 8

time: 173 us -> 162 us (0.936); the launches traced: 169 us -> 161 us
  blocking collectives: 83.2 us -> 69.2 us
  Pallas kernels: 12.6 us -> 20.7 us
    all_to_all x2, blocking collectives: 68.3 us -> 51.6 us  [the longest x1 28.6 us: shards(): exchange(share(kept, arrived), AXES, axis_index_groups=stride_groups(False))]
    pallas_call x1 -> x3, Pallas kernels: 0.75 us -> 8.62 us  [the longest x1 7.63 us: pack_tokens(): pl.pallas_call(tokens_kernel, out_shape=jax.ShapeDtypeStruct(shape, jnp.b...]
    all_to_all x1, blocking collectives: 14.9 us -> 17.6 us  [shards(): got = exchange(final_message(home, slots), 'grp')]
    ppermute x1, starting transfers between devices: 4.37 us -> 1.96 us  [shards(): home = lax.ppermute(rows, AXES, home_pairs())]
where the time goes in v3:
time: 162 us; the launch traced here: 161 us
  blocking collectives  69.2 us (43%)
  starting transfers between devices  32.8 us (20%)
  waiting for transfers between devices  29.4 us (18%)
  Pallas kernels  20.7 us (13%)
  local copies, waits for them, and re-layouts  6.84 us (4%)
    all_to_all x1, blocking collectives, shards(): exchange(share(kept, arrived), AXES, axis_index_groups=stride_groups(False))  28.6 us
    all_to_all x1, starting transfers between devices, shards(): tokens = exchange(message, AXES, axis_index_groups=cube_groups())  23.4 us
    all_to_all x1, blocking collectives, shards(): own = exchange(total(terms), AXES, axis_index_groups=stride_groups(True))  23 us
    all_to_all x1, waiting for transfers between devices, shards(): tokens = exchange(message, AXES, axis_index_groups=cube_groups())  21 us
    all_to_all x1, blocking collectives, shards(): got = exchange(final_message(home, slots), 'grp')  17.6 us
    pallas_call x1, Pallas kernels, pack_tokens(): pl.pallas_call(tokens_kernel, out_shape=jax.ShapeDtypeStruct(shape, jnp.b...  7.63 us
    unnamed x15, local copies, waits for them, and re-layouts  6.1 us
    ppermute x1, starting transfers between devices, shards(): other = lax.ppermute(own, AXES, core_pairs())  5.52 us
  transfers between devices with their start and end apart: 4, of which 4 were waited for; matrix products, arithmetic and copies ran while one was open for 1% of the time, Pallas kernels for 2%

profile of v3, /device:TPU:1, one launch (start us, length us, event | category | flops | bytes accessed | tf_op | source)
XLA Modules:
  0.0 160.5 jit_solution(14544704281093257421)
XLA Ops:
  0.6 1.6 copy-done.1
  2.2 0.9 copy-done.2
  3.1 0.7 copy-done.3
  3.8 7.6 %shard_map.112 = bf16[8,3,128,512]{3,2,1,0:T(8,128)(2,1)S(1)} custom-call(s32[16]{0:T(128)S(1)} %copy-done.3, bf16[128,8192]{1,0:T(8,128)(2,1)S(1)} %copy-done.1, bf16[128,512]{1,0:T(8,128)(2,1)S(1)} %copy-done.2), custom_call_target="tpu_custom_call" | custom-call | tf_op jit(solution)/shard_map/pallas_call | solution.py:102
  11.4 1.6 %copy-done = bf16[8,3,128,512]{3,2,1,0:T(8,128)(2,1)} copy-done((bf16[8,3,128,512]{3,2,1,0:T(8,128)(2,1)}, bf16[8,3,128,512]{3,2,1,0:T(8,128)(2,1)S(1)}, u32[]{:S(2)}) %copy-start) | copy-done | bytes 3145752
  13.1 23.4 %all-to-all-start = ((bf16[8,3,128,512]{3,2,1,0:T(8,128)(2,1)}), bf16[8,3,128,512]{3,2,1,0:T(8,128)(2,1)S(1)}, u32[]{:S(2)}, u32[]{:S(2)}) async-start(bf16[8,3,128,512]{3,2,1,0:T(8,128)(2,1)} %copy-done), calls=%async_computation | async-start | bytes 6291456 | tf_op jit(solution)/shard_map/all_to_all | solution.py:392
  37.1 0.7 copy.12.rows
  37.8 0.7 copy.13.owner_col
  38.6 1.8 %shard_map.113.slots = bf16[16,32,128]{2,1,0:T(8,128)(2,1)} custom-call(s32[1]{0:T(128)S(6)} %copy.14.live, s32[128,1]{1,0:T(8,128)} %copy.12.rows, s32[128,1]{1,0:T(8,128)} %copy.13.owner_col, s32[1,128]{1,0:T(1,128)} %bitcast.8, bf16[128,128]{1,0:T(8,128)(2,1)} %deltas.1), custom_call_target="tpu_custom_call" | custom-call | tf_op jit(solution)/shard_map/pallas_call | solution.py:136
  40.4 21.0 %all-to-all-done.tokens = bf16[8,3,128,512]{3,2,1,0:T(8,128)(2,1)S(1)} async-done(((bf16[8,3,128,512]{3,2,1,0:T(8,128)(2,1)}), bf16[8,3,128,512]{3,2,1,0:T(8,128)(2,1)S(1)}, u32[]{:S(2)}, u32[]{:S(2)}) %all-to-all-start) | async-done | bytes 3145760 | tf_op jit(solution)/shard_map/all_to_all | solution.py:392
  61.4 0.7 shard_map.115
  62.1 1.9 %collective-permute-start = (f32[2,2,128,512]{3,2,1,0:T(8,128)S(1)}, f32[2,2,128,512]{3,2,1,0:T(8,128)S(1)}, u32[]{:S(2)}, u32[]{:S(2)}) collective-permute-start(f32[2,2,128,512]{3,2,1,0:T(8,128)S(1)} %shard_map.115), channel_id=1, source_target_pairs={{0,64},{64,0},{128,192},{192,128},{256,320},{320,256},{384,448},{4... | collective-permute-start | bytes 3145736 | tf_op jit(solution)/shard_map/ppermute | solution.py:396
  64.0 0.7 shard_map.114.kept
  64.8 1.9 %collective-permute-done.arrived = f32[2,2,128,512]{3,2,1,0:T(8,128)S(1)} collective-permute-done((f32[2,2,128,512]{3,2,1,0:T(8,128)S(1)}, f32[2,2,128,512]{3,2,1,0:T(8,128)S(1)}, u32[]{:S(2)}, u32[]{:S(2)}) %collective-permute-start) | collective-permute-done | bytes 1048608 | tf_op jit(solution)/shard_map/ppermute | solution.py:396
  67.2 28.6 %all_to_all.20.terms = s16[64,40,128]{2,1,0:T(8,128)(2,1)S(1)} all-to-all(s16[64,40,128]{2,1,0:T(8,128)(2,1)S(1)} %shard_map.116), channel_id=1, replica_groups={{0,256,2,258,4,260,6,262,16,272,18,274,20,276,22,278,32,288,34,290,36,2..., dimensions={0} | all-to-all | bytes 1310720 | tf_op jit(solution)/shard_map/all_to_all | solution.py:398
  96.3 23.0 %all_to_all.21.own = s16[32,40,128]{2,1,0:T(8,128)(2,1)S(1)} all-to-all(s16[32,40,128]{2,1,0:T(8,128)(2,1)S(1)} %shard_map.117), channel_id=1, replica_groups={{0,256,2,258,4,260,6,262,16,272,18,274,20,276,22,278,32,288,34,290,36,2..., dimensions={0} | all-to-all | bytes 655360 | tf_op jit(solution)/shard_map/all_to_all | solution.py:399
  119.2 5.5 %collective-permute-start.1 = (s16[32,40,128]{2,1,0:T(8,128)(2,1)S(1)}, s16[32,40,128]{2,1,0:T(8,128)(2,1)S(1)}, u32[]{:S(2)}, u32[]{:S(2)}) collective-permute-start(s16[32,40,128]{2,1,0:T(8,128)(2,1)S(1)} %all_to_all.21.own), channel_id=1, source_target_pairs={{0,64},{64,0},{128,192},{192,128},{256,320},{320,256},{384,448},{4... | collective-permute-start | bytes 983048 | tf_op jit(solution)/shard_map/ppermute | solution.py:400
  125.0 1.0 collective-permute-done.1.other
  126.0 4.9 %shard_map.118 = bf16[32,128]{1,0:T(8,128)(2,1)S(1)} custom-call(s32[2]{0:T(128)S(1)} %pad_add_fusion.place, s16[32,40,128]{2,1,0:T(8,128)(2,1)S(1)} %all_to_all.21.own, s16[32,40,128]{2,1,0:T(8,128)(2,1)S(1)} %collective-permute-done.1.other), custom_call_target="tpu_custom_call" | custom-call | tf_op jit(solution)/shard_map/pallas_call | solution.py:314
  130.9 2.0 %collective-permute-start.2 = (bf16[32,128]{1,0:T(8,128)(2,1)S(1)}, bf16[32,128]{1,0:T(8,128)(2,1)S(1)}, u32[]{:S(2)}, u32[]{:S(2)}) collective-permute-start(bf16[32,128]{1,0:T(8,128)(2,1)S(1)} %shard_map.118), channel_id=1, source_target_pairs={{0,0},{64,16},{128,128},{192,144},{256,1},{320,17},{384,129},{448,... | collective-permute-start | bytes 24584 | tf_op jit(solution)/shard_map/ppermute | solution.py:405
  132.8 5.5 %collective-permute-done.2.rows = bf16[32,128]{1,0:T(8,128)(2,1)S(1)} collective-permute-done((bf16[32,128]{1,0:T(8,128)(2,1)S(1)}, bf16[32,128]{1,0:T(8,128)(2,1)S(1)}, u32[]{:S(2)}, u32[]{:S(2)}) %collective-permute-start.2) | collective-permute-done | bytes 8224 | tf_op jit(solution)/shard_map/ppermute | solution.py:405
  138.9 1.7 %shard_map.119 = bf16[16,64,128]{2,1,0:T(8,128)(2,1)} custom-call(bf16[32,128]{1,0:T(8,128)(2,1)} %copy-done.4, bf16[16,32,128]{2,1,0:T(8,128)(2,1)} %shard_map.113.slots), custom_call_target="tpu_custom_call" | custom-call | tf_op jit(solution)/shard_map/pallas_call | solution.py:332
  140.6 17.6 %all_to_all.22.got = bf16[16,64,128]{2,1,0:T(8,128)(2,1)} all-to-all(bf16[16,64,128]{2,1,0:T(8,128)(2,1)} %shard_map.119), channel_id=1, replica_groups=mesh['grp'=16,'rep'=64] {'grp'}, dimensions={0} | all-to-all | bytes 524288 | tf_op jit(solution)/shard_map/all_to_all | solution.py:406
  158.2 2.3 %shard_map.120 = (f32[512,128]{1,0:T(8,128)}, f32[1,512]{1,0:T(1,128)}, bf16[16,8,512]{2,1,0:T(8,128)(2,1)}) custom-call(bf16[16,64,128]{2,1,0:T(8,128)(2,1)} %all_to_all.22.got, f32[512,128]{1,0:T(8,128)} %table.1, f32[1,512]{1,0:T(1,128)} %bitcast.7), custom_call_target="tpu_custom_call" | custom-call | tf_op jit(solution)/shard_map/pallas_call | solution.py:361
  (13 shorter events, 1.7 us)
Async XLA Ops:
  0.6 1.6 copy-start.1
  2.2 0.9 copy-start.2
  3.1 0.7 copy-start.3
  11.4 1.6 %copy-start = (bf16[8,3,128,512]{3,2,1,0:T(8,128)(2,1)}, bf16[8,3,128,512]{3,2,1,0:T(8,128)(2,1)S(1)}, u32[]{:S(2)}) copy-start(bf16[8,3,128,512]{3,2,1,0:T(8,128)(2,1)S(1)} %shard_map.112) | copy-start | bytes 9437188
  13.0 24.0 %copy-start.6 = (s32[128]{0:T(128)S(1)}, s32[128]{0:T(128)}, u32[]{:S(2)}) copy-start(s32[128]{0:T(128)} %param.14) | copy-start | bytes 1540
  13.0 24.8 %copy-start.5 = (s32[128,1]{0,1:T(1,128)S(1)}, s32[128,1]{0,1:T(1,128)}, u32[]{:S(2)}) copy-start(s32[128,1]{0,1:T(1,128)} %param.15) | copy-start | bytes 1540
  13.1 48.3 %all-to-all-start = ((bf16[8,3,128,512]{3,2,1,0:T(8,128)(2,1)}), bf16[8,3,128,512]{3,2,1,0:T(8,128)(2,1)S(1)}, u32[]{:S(2)}, u32[]{:S(2)}) async-start(bf16[8,3,128,512]{3,2,1,0:T(8,128)(2,1)} %copy-done), calls=%async_computation | async-start | bytes 6291456 | tf_op jit(solution)/shard_map/all_to_all | solution.py:392
  62.1 4.6 %collective-permute-start = (f32[2,2,128,512]{3,2,1,0:T(8,128)S(1)}, f32[2,2,128,512]{3,2,1,0:T(8,128)S(1)}, u32[]{:S(2)}, u32[]{:S(2)}) collective-permute-start(f32[2,2,128,512]{3,2,1,0:T(8,128)S(1)} %shard_map.115), channel_id=1, source_target_pairs={{0,64},{64,0},{128,192},{192,128},{256,320},{320,256},{384,448},{4... | collective-permute-start | bytes 3145736 | tf_op jit(solution)/shard_map/ppermute | solution.py:396
  119.2 6.8 %collective-permute-start.1 = (s16[32,40,128]{2,1,0:T(8,128)(2,1)S(1)}, s16[32,40,128]{2,1,0:T(8,128)(2,1)S(1)}, u32[]{:S(2)}, u32[]{:S(2)}) collective-permute-start(s16[32,40,128]{2,1,0:T(8,128)(2,1)S(1)} %all_to_all.21.own), channel_id=1, source_target_pairs={{0,64},{64,0},{128,192},{192,128},{256,320},{320,256},{384,448},{4... | collective-permute-start | bytes 983048 | tf_op jit(solution)/shard_map/ppermute | solution.py:400
  130.9 7.5 %collective-permute-start.2 = (bf16[32,128]{1,0:T(8,128)(2,1)S(1)}, bf16[32,128]{1,0:T(8,128)(2,1)S(1)}, u32[]{:S(2)}, u32[]{:S(2)}) collective-permute-start(bf16[32,128]{1,0:T(8,128)(2,1)S(1)} %shard_map.118), channel_id=1, source_target_pairs={{0,0},{64,16},{128,128},{192,144},{256,1},{320,17},{384,129},{448,... | collective-permute-start | bytes 24584 | tf_op jit(solution)/shard_map/ppermute | solution.py:405
  138.3 0.6 copy-start.4

commit v4 on v3

--- a/solution.py
+++ b/solution.py
@@ -74,42 +74,22 @@
     return pairs
 
 
-def tokens_kernel(order, grads, features, out, held, arrive, leave):
-    copies = []
+def tokens_kernel(order, grads, features, out):
     for spot in range(8):
         for k in range(2):
             first = pl.multiple_of(order[spot + 8 * k] * 512, 512)
-            copies.append((grads.at[:, pl.ds(first, 512)], spot, k))
-        copies.append((features, spot, 2))
-    coming = []
-    for n, (source, spot, k) in enumerate(copies):
-        copy = pltpu.make_async_copy(source, held.at[spot, k], arrive.at[n])
-        copy.start()
-        coming.append(copy)
-    going = []
-    for n, (source, spot, k) in enumerate(copies):
-        coming[n].wait()
-        copy = pltpu.make_async_copy(held.at[spot, k], out.at[spot, k], leave.at[n])
-        copy.start()
-        going.append(copy)
-    for copy in going:
-        copy.wait()
+            out[spot, k] = grads[:, pl.ds(first, 512)]
+        out[spot, 2] = features[...]
 
 
 def pack_tokens(order, grads, features):
-    shape = (8, 3, 128, 512)
-    hbm = pl.BlockSpec(memory_space=pltpu.HBM)
+    vmem = pl.BlockSpec(memory_space=pltpu.VMEM)
     return pl.pallas_call(
         tokens_kernel,
-        out_shape=jax.ShapeDtypeStruct(shape, jnp.bfloat16),
-        in_specs=[pl.BlockSpec(memory_space=pltpu.SMEM), hbm, hbm],
-        out_specs=hbm,
-        scratch_shapes=[
-            pltpu.VMEM(shape, jnp.bfloat16),
-            pltpu.SemaphoreType.DMA((24,)),
-            pltpu.SemaphoreType.DMA((24,)),
-        ],
-        compiler_params=pltpu.CompilerParams(vmem_limit_bytes=16 * MIB),
+        out_shape=jax.ShapeDtypeStruct((8, 3, 128, 512), jnp.bfloat16),
+        in_specs=[pl.BlockSpec(memory_space=pltpu.SMEM), vmem, vmem],
+        out_specs=vmem,
+        compiler_params=pltpu.CompilerParams(vmem_limit_bytes=32 * MIB),
     )(order, grads, features)
 
 
@@ -304,8 +284,7 @@
     root = (5.0 * f_rows - rows_product(rows_product(fm_rows, f_parts), f_parts)) / 4.0
     quarter = 1.0 / jnp.sqrt(jnp.sqrt(scale))
     result = rows_product(root * quarter, g_parts) * quarter * float(width)
-    tall = jnp.concatenate([result[:, t * 128 : (t + 1) * 128] for t in range(4)], axis=0)
-    out[...] = tall.astype(jnp.bfloat16)
+    out[...] = result.astype(jnp.bfloat16)
 
 
 def direction_rows(place, own, other):
@@ -313,7 +292,7 @@
     square = pltpu.VMEM((512, 512), jnp.float32)
     return pl.pallas_call(
         direction_kernel,
-        out_shape=jax.ShapeDtypeStruct((32, 128), jnp.bfloat16),
+        out_shape=jax.ShapeDtypeStruct((8, 512), jnp.bfloat16),
         in_specs=[pl.BlockSpec(memory_space=pltpu.SMEM), vmem, vmem],
         out_specs=vmem,
         scratch_shapes=[square, square, square],
@@ -321,28 +300,9 @@
     )(place, own, other)
 
 
-def message_kernel(rows, slots, out):
-    for target in range(16):
-        out[target, 0:32, :] = rows[...]
-    out[:, 32:64, :] = slots[...]
-
-
-def final_message(rows, slots):
-    vmem = pl.BlockSpec(memory_space=pltpu.VMEM)
-    return pl.pallas_call(
-        message_kernel,
-        out_shape=jax.ShapeDtypeStruct((16, 64, 128), jnp.bfloat16),
-        in_specs=[vmem, vmem],
-        out_specs=vmem,
-    )(rows, slots)
-
-
-def update_kernel(got, table, accum, new_table, new_accum, directions):
-    rows = got[:, 0:32, :].astype(jnp.float32).reshape(16, 4, 8, 128)
-    wide = jnp.concatenate([rows[:, t] for t in range(4)], axis=2)
-    directions[...] = wide.astype(jnp.bfloat16)
-    deltas = got[:, 32:48, :].reshape(256, 128)
-    keys = got[:, 48:64, :].astype(jnp.float32).reshape(256, 128)
+def update_kernel(got, table, accum, new_table, new_accum):
+    deltas = got[:, 0:16, :].reshape(256, 128)
+    keys = got[:, 16:32, :].astype(jnp.float32).reshape(256, 128)
     row = keys[:, 0:1] * 16.0 + keys[:, 64:65]
     count = table.shape[0]
     named = row == lax.broadcasted_iota(jnp.int32, (256, count), 1).astype(jnp.float32)
@@ -363,10 +323,9 @@
         out_shape=(
             jax.ShapeDtypeStruct(table.shape, jnp.float32),
             jax.ShapeDtypeStruct((1, accum.shape[0]), jnp.float32),
-            jax.ShapeDtypeStruct((16, 8, 512), jnp.bfloat16),
         ),
         in_specs=[vmem, vmem, vmem],
-        out_specs=(vmem, vmem, vmem),
+        out_specs=(vmem, vmem),
     )(got, table, accum.reshape(1, -1))
 
 
@@ -397,14 +356,15 @@
     kept = partial_grads(core.reshape(1), tokens)
     terms = exchange(share(kept, arrived), AXES, axis_index_groups=stride_groups(False))
     own = exchange(total(terms), AXES, axis_index_groups=stride_groups(True))
+    got = exchange(slots, "grp")
     other = lax.ppermute(own, AXES, core_pairs())
     turn = piece(x, y, z)
     first_row = (turn // 16) * 256 + core * 128 + (turn % 16) * 8
     rows = direction_rows(jnp.stack([core, first_row]).astype(jnp.int32), own, other)
-
     home = lax.ppermute(rows, AXES, home_pairs())
-    got = exchange(final_message(home, slots), "grp")
-    new_table, new_accum, directions = update_rows(got, emb_table, row_accum)
+
+    new_table, new_accum = update_rows(got, emb_table, row_accum)
+    directions = exchange(jnp.broadcast_to(home[None], (16, 8, 512)), "grp")
     return (new_table, new_accum.reshape(-1), directions)
 
 

time: 162 us -> 155 us (0.957)
  blocking collectives: 69.2 us -> 51.7 us
  starting transfers between devices: 32.8 us -> 45.7 us
  Pallas kernels: 20.7 us -> 12.1 us
  waiting for transfers between devices: 29.4 us -> 33.5 us
    all_to_all x1 -> x0, blocking collectives: 17.6 us -> none  [shards(): got = exchange(final_message(home, slots), 'grp')]
    all_to_all x0 -> x2, starting transfers between devices: none -> 13 us  [the longest x1 7.43 us: shards(): directions = exchange(jnp.broadcast_to(home[None], (16, 8, 512)), 'grp')]
    all_to_all x0 -> x2, waiting for transfers between devices: none -> 9.17 us  [the longest x1 6.91 us: shards(): directions = exchange(jnp.broadcast_to(home[None], (16, 8, 512)), 'grp')]
    pallas_call x3 -> x2, Pallas kernels: 14.1 us -> 5.62 us  [the longest x1 4.86 us: direction_rows(): pl.pallas_call(direction_kernel, out_shape=jax.ShapeDtypeStruct((8, 512),...]
    ppermute x1, waiting for transfers between devices: 5.51 us -> 1.49 us  [shards(): home = lax.ppermute(rows, AXES, home_pairs())]
    unnamed x15 -> x16, local copies, waits for them, and re-layouts: 6.1 us -> 6.2 us
  transfers between devices with their start and end apart: 4 -> 6, of which waited for: 4 -> 5; matrix products, arithmetic and copies ran while one was open for 1% -> 1% of each run, Pallas kernels for 2% -> 6%
where the time goes in v4:
time: 155 us; the launch traced here: 152 us
  blocking collectives  51.7 us (33%)
  starting transfers between devices  45.7 us (29%)
  waiting for transfers between devices  33.5 us (22%)
  Pallas kernels  12.1 us (8%)
  local copies, waits for them, and re-layouts  7.6 us (5%)
    all_to_all x1, blocking collectives, shards(): exchange(share(kept, arrived), AXES, axis_index_groups=stride_groups(False))  28.6 us
    all_to_all x1, starting transfers between devices, shards(): tokens = exchange(message, AXES, axis_index_groups=cube_groups())  23.4 us
    all_to_all x1, blocking collectives, shards(): own = exchange(total(terms), AXES, axis_index_groups=stride_groups(True))  23.1 us
    all_to_all x1, waiting for transfers between devices, shards(): tokens = exchange(message, AXES, axis_index_groups=cube_groups())  21 us
    all_to_all x1, starting transfers between devices, shards(): directions = exchange(jnp.broadcast_to(home[None], (16, 8, 512)), 'grp')  7.43 us
    all_to_all x1, waiting for transfers between devices, shards(): directions = exchange(jnp.broadcast_to(home[None], (16, 8, 512)), 'grp')  6.91 us
    unnamed x16, local copies, waits for them, and re-layouts  6.2 us
    all_to_all x1, starting transfers between devices, shards(): got = exchange(slots, 'grp')  5.53 us
  transfers between devices with their start and end apart: 6, of which 5 were waited for; matrix products, arithmetic and copies ran while one was open for 1% of the time, Pallas kernels for 6%

profile of v4, /device:TPU:1, one launch (start us, length us, event | category | flops | bytes accessed | tf_op | source)
XLA Modules:
  0.0 152.1 jit_solution(7408642016696352197)
XLA Ops:
  0.6 1.6 %copy-done.1 = bf16[128,8192]{1,0:T(8,128)(2,1)S(1)} copy-done((bf16[128,8192]{1,0:T(8,128)(2,1)S(1)}, bf16[128,8192]{1,0:T(8,128)(2,1)}, u32[]{:S(2)}) %copy-start.1) | copy-done | bytes 2097176
  2.2 0.9 copy-done.2
  3.8 0.8 shard_map.112
  4.6 1.6 %copy-done = bf16[8,3,128,512]{3,2,1,0:T(8,128)(2,1)} copy-done((bf16[8,3,128,512]{3,2,1,0:T(8,128)(2,1)}, bf16[8,3,128,512]{3,2,1,0:T(8,128)(2,1)S(1)}, u32[]{:S(2)}) %copy-start) | copy-done | bytes 3145752
  6.2 23.4 %all-to-all-start = ((bf16[8,3,128,512]{3,2,1,0:T(8,128)(2,1)}), bf16[8,3,128,512]{3,2,1,0:T(8,128)(2,1)S(1)}, u32[]{:S(2)}, u32[]{:S(2)}) async-start(bf16[8,3,128,512]{3,2,1,0:T(8,128)(2,1)} %copy-done), calls=%async_computation | async-start | bytes 6291456 | tf_op jit(solution)/shard_map/all_to_all | solution.py:351
  30.2 0.7 copy.12.rows
  31.0 0.7 copy.13.owner_col
  31.7 1.8 %shard_map.113 = bf16[16,32,128]{2,1,0:T(8,128)(2,1)} custom-call(s32[1]{0:T(128)S(6)} %copy.15.live, s32[128,1]{1,0:T(8,128)} %copy.12.rows, s32[128,1]{1,0:T(8,128)} %copy.13.owner_col, s32[1,128]{1,0:T(1,128)} %bitcast.8, bf16[128,128]{1,0:T(8,128)(2,1)} %deltas.1), custom_call_target="tpu_custom_call" | custom-call | tf_op jit(solution)/shard_map/pallas_call | solution.py:116
  33.5 21.0 %all-to-all-done.tokens = bf16[8,3,128,512]{3,2,1,0:T(8,128)(2,1)S(1)} async-done(((bf16[8,3,128,512]{3,2,1,0:T(8,128)(2,1)}), bf16[8,3,128,512]{3,2,1,0:T(8,128)(2,1)S(1)}, u32[]{:S(2)}, u32[]{:S(2)}) %all-to-all-start) | async-done | bytes 3145760 | tf_op jit(solution)/shard_map/all_to_all | solution.py:351
  54.5 0.7 shard_map.116
  55.3 1.9 %collective-permute-start = (f32[2,2,128,512]{3,2,1,0:T(8,128)S(1)}, f32[2,2,128,512]{3,2,1,0:T(8,128)S(1)}, u32[]{:S(2)}, u32[]{:S(2)}) collective-permute-start(f32[2,2,128,512]{3,2,1,0:T(8,128)S(1)} %shard_map.116), channel_id=1, source_target_pairs={{0,64},{64,0},{128,192},{192,128},{256,320},{320,256},{384,448},{4... | collective-permute-start | bytes 3145736 | tf_op jit(solution)/shard_map/ppermute | solution.py:355
  57.2 0.7 shard_map.115.kept
  57.9 1.9 %collective-permute-done.arrived = f32[2,2,128,512]{3,2,1,0:T(8,128)S(1)} collective-permute-done((f32[2,2,128,512]{3,2,1,0:T(8,128)S(1)}, f32[2,2,128,512]{3,2,1,0:T(8,128)S(1)}, u32[]{:S(2)}, u32[]{:S(2)}) %collective-permute-start) | collective-permute-done | bytes 1048608 | tf_op jit(solution)/shard_map/ppermute | solution.py:355
  60.3 28.6 %all_to_all.25.terms = s16[64,40,128]{2,1,0:T(8,128)(2,1)S(1)} all-to-all(s16[64,40,128]{2,1,0:T(8,128)(2,1)S(1)} %shard_map.117), channel_id=1, replica_groups={{0,256,2,258,4,260,6,262,16,272,18,274,20,276,22,278,32,288,34,290,36,2..., dimensions={0} | all-to-all | bytes 1310720 | tf_op jit(solution)/shard_map/all_to_all | solution.py:357
  89.4 23.1 %all_to_all.26.own = s16[32,40,128]{2,1,0:T(8,128)(2,1)S(1)} all-to-all(s16[32,40,128]{2,1,0:T(8,128)(2,1)S(1)} %shard_map.118), channel_id=1, replica_groups={{0,256,2,258,4,260,6,262,16,272,18,274,20,276,22,278,32,288,34,290,36,2..., dimensions={0} | all-to-all | bytes 655360 | tf_op jit(solution)/shard_map/all_to_all | solution.py:358
  112.5 5.5 %collective-permute-start.1 = (s16[32,40,128]{2,1,0:T(8,128)(2,1)S(1)}, s16[32,40,128]{2,1,0:T(8,128)(2,1)S(1)}, u32[]{:S(2)}, u32[]{:S(2)}) collective-permute-start(s16[32,40,128]{2,1,0:T(8,128)(2,1)S(1)} %all_to_all.26.own), channel_id=1, source_target_pairs={{0,64},{64,0},{128,192},{192,128},{256,320},{320,256},{384,448},{4... | collective-permute-start | bytes 983048 | tf_op jit(solution)/shard_map/ppermute | solution.py:360
  118.0 5.5 %all-to-all-start.1 = ((bf16[16,32,128]{2,1,0:T(8,128)(2,1)}), bf16[16,32,128]{2,1,0:T(8,128)(2,1)S(1)}, u32[]{:S(2)}, u32[]{:S(2)}) async-start(bf16[16,32,128]{2,1,0:T(8,128)(2,1)} %shard_map.113), calls=%async_computation.1 | async-start | bytes 262144 | tf_op jit(solution)/shard_map/all_to_all | solution.py:359
  123.6 4.9 %shard_map.119 = bf16[8,512]{1,0:T(8,128)(2,1)S(1)} custom-call(s32[2]{0:T(128)S(1)} %pad_add_fusion.place, s16[32,40,128]{2,1,0:T(8,128)(2,1)S(1)} %all_to_all.26.own, s16[32,40,128]{2,1,0:T(8,128)(2,1)S(1)} %collective-permute-done.1.other), custom_call_target="tpu_custom_call" | custom-call | tf_op jit(solution)/shard_map/pallas_call | solution.py:293
  128.4 2.0 %collective-permute-start.2 = (bf16[8,512]{1,0:T(8,128)(2,1)S(1)}, bf16[8,512]{1,0:T(8,128)(2,1)S(1)}, u32[]{:S(2)}, u32[]{:S(2)}) collective-permute-start(bf16[8,512]{1,0:T(8,128)(2,1)S(1)} %shard_map.119), channel_id=1, source_target_pairs={{0,0},{64,16},{128,128},{192,144},{256,1},{320,17},{384,129},{448,... | collective-permute-start | bytes 24584 | tf_op jit(solution)/shard_map/ppermute | solution.py:364
  130.4 2.3 %all-to-all-done.1.got = bf16[16,32,128]{2,1,0:T(8,128)(2,1)S(1)} async-done(((bf16[16,32,128]{2,1,0:T(8,128)(2,1)}), bf16[16,32,128]{2,1,0:T(8,128)(2,1)S(1)}, u32[]{:S(2)}, u32[]{:S(2)}) %all-to-all-start.1) | async-done | bytes 131104 | tf_op jit(solution)/shard_map/all_to_all | solution.py:359
  132.7 1.5 collective-permute-done.2
  134.8 7.4 %all-to-all-start.4 = ((bf16[16,8,512]{2,1,0:T(8,128)(2,1)}), bf16[16,8,512]{2,1,0:T(8,128)(2,1)S(1)}, u32[]{:S(2)}, u32[]{:S(2)}) async-start(bf16[16,8,512]{2,1,0:T(8,128)(2,1)} %broadcast_in_dim.2), calls=%async_computation.4 | async-start | bytes 262144 | tf_op jit(solution)/shard_map/all_to_all | solution.py:367
  142.3 2.3 %shard_map.114 = (f32[512,128]{1,0:T(8,128)}, f32[1,512]{1,0:T(1,128)}) custom-call(bf16[16,32,128]{2,1,0:T(8,128)(2,1)} %copy-done.4, f32[512,128]{1,0:T(8,128)} %table.1, f32[1,512]{1,0:T(1,128)} %bitcast.7), custom_call_target="tpu_custom_call" | custom-call | tf_op jit(solution)/shard_map/pallas_call | solution.py:321
  144.5 6.9 %all-to-all-done.4 = bf16[16,8,512]{2,1,0:T(8,128)(2,1)S(1)} async-done(((bf16[16,8,512]{2,1,0:T(8,128)(2,1)}), bf16[16,8,512]{2,1,0:T(8,128)(2,1)S(1)}, u32[]{:S(2)}, u32[]{:S(2)}) %all-to-all-start.4) | async-done | bytes 131104 | tf_op jit(solution)/shard_map/all_to_all | solution.py:367
  (17 shorter events, 3.1 us)
Async XLA Ops:
  0.6 1.6 %copy-start.1 = (bf16[128,8192]{1,0:T(8,128)(2,1)S(1)}, bf16[128,8192]{1,0:T(8,128)(2,1)}, u32[]{:S(2)}) copy-start(bf16[128,8192]{1,0:T(8,128)(2,1)} %grads.1) | copy-start | bytes 6291460
  2.2 0.9 copy-start.2
  3.1 0.7 copy-start.3
  4.5 1.7 %copy-start = (bf16[8,3,128,512]{3,2,1,0:T(8,128)(2,1)}, bf16[8,3,128,512]{3,2,1,0:T(8,128)(2,1)S(1)}, u32[]{:S(2)}) copy-start(bf16[8,3,128,512]{3,2,1,0:T(8,128)(2,1)S(1)} %shard_map.112) | copy-start | bytes 9437188
  6.2 24.0 %copy-start.6 = (s32[128]{0:T(128)S(1)}, s32[128]{0:T(128)}, u32[]{:S(2)}) copy-start(s32[128]{0:T(128)} %param.14) | copy-start | bytes 1540
  6.2 24.8 %copy-start.5 = (s32[128,1]{0,1:T(1,128)S(1)}, s32[128,1]{0,1:T(1,128)}, u32[]{:S(2)}) copy-start(s32[128,1]{0,1:T(1,128)} %param.15) | copy-start | bytes 1540
  6.2 48.3 %all-to-all-start = ((bf16[8,3,128,512]{3,2,1,0:T(8,128)(2,1)}), bf16[8,3,128,512]{3,2,1,0:T(8,128)(2,1)S(1)}, u32[]{:S(2)}, u32[]{:S(2)}) async-start(bf16[8,3,128,512]{3,2,1,0:T(8,128)(2,1)} %copy-done), calls=%async_computation | async-start | bytes 6291456 | tf_op jit(solution)/shard_map/all_to_all | solution.py:351
  55.3 4.6 %collective-permute-start = (f32[2,2,128,512]{3,2,1,0:T(8,128)S(1)}, f32[2,2,128,512]{3,2,1,0:T(8,128)S(1)}, u32[]{:S(2)}, u32[]{:S(2)}) collective-permute-start(f32[2,2,128,512]{3,2,1,0:T(8,128)S(1)} %shard_map.116), channel_id=1, source_target_pairs={{0,64},{64,0},{128,192},{192,128},{256,320},{320,256},{384,448},{4... | collective-permute-start | bytes 3145736 | tf_op jit(solution)/shard_map/ppermute | solution.py:355
  112.5 11.1 %collective-permute-start.1 = (s16[32,40,128]{2,1,0:T(8,128)(2,1)S(1)}, s16[32,40,128]{2,1,0:T(8,128)(2,1)S(1)}, u32[]{:S(2)}, u32[]{:S(2)}) collective-permute-start(s16[32,40,128]{2,1,0:T(8,128)(2,1)S(1)} %all_to_all.26.own), channel_id=1, source_target_pairs={{0,64},{64,0},{128,192},{192,128},{256,320},{320,256},{384,448},{4... | collective-permute-start | bytes 983048 | tf_op jit(solution)/shard_map/ppermute | solution.py:360
  118.0 14.7 %all-to-all-start.1 = ((bf16[16,32,128]{2,1,0:T(8,128)(2,1)}), bf16[16,32,128]{2,1,0:T(8,128)(2,1)S(1)}, u32[]{:S(2)}, u32[]{:S(2)}) async-start(bf16[16,32,128]{2,1,0:T(8,128)(2,1)} %shard_map.113), calls=%async_computation.1 | async-start | bytes 262144 | tf_op jit(solution)/shard_map/all_to_all | solution.py:359
  128.4 5.7 %collective-permute-start.2 = (bf16[8,512]{1,0:T(8,128)(2,1)S(1)}, bf16[8,512]{1,0:T(8,128)(2,1)S(1)}, u32[]{:S(2)}, u32[]{:S(2)}) collective-permute-start(bf16[8,512]{1,0:T(8,128)(2,1)S(1)} %shard_map.119), channel_id=1, source_target_pairs={{0,0},{64,16},{128,128},{192,144},{256,1},{320,17},{384,129},{448,... | collective-permute-start | bytes 24584 | tf_op jit(solution)/shard_map/ppermute | solution.py:364
  132.7 9.6 %copy-start.4 = (bf16[16,32,128]{2,1,0:T(8,128)(2,1)}, bf16[16,32,128]{2,1,0:T(8,128)(2,1)S(1)}, u32[]{:S(2)}) copy-start(bf16[16,32,128]{2,1,0:T(8,128)(2,1)S(1)} %all-to-all-done.1.got) | copy-start | bytes 393220
  134.8 16.6 %all-to-all-start.4 = ((bf16[16,8,512]{2,1,0:T(8,128)(2,1)}), bf16[16,8,512]{2,1,0:T(8,128)(2,1)S(1)}, u32[]{:S(2)}, u32[]{:S(2)}) async-start(bf16[16,8,512]{2,1,0:T(8,128)(2,1)} %broadcast_in_dim.2), calls=%async_computation.4 | async-start | bytes 262144 | tf_op jit(solution)/shard_map/all_to_all | solution.py:367

commit v5 on v4

--- a/solution.py
+++ b/solution.py
@@ -89,7 +89,7 @@
         out_shape=jax.ShapeDtypeStruct((8, 3, 128, 512), jnp.bfloat16),
         in_specs=[pl.BlockSpec(memory_space=pltpu.SMEM), vmem, vmem],
         out_specs=vmem,
-        compiler_params=pltpu.CompilerParams(vmem_limit_bytes=32 * MIB),
+        compiler_params=pltpu.CompilerParams(vmem_limit_bytes=60 * MIB),
     )(order, grads, features)
 
 

time: 155 us -> 153 us (0.987)
  local copies, waits for them, and re-layouts: 7.6 us -> 2.8 us
  Pallas kernels: 12.1 us -> 14.8 us
    unnamed x16 -> x8, local copies, waits for them, and re-layouts: 6.2 us -> 1.4 us
    pallas_call x1, Pallas kernels: 0.76 us -> 3.44 us  [pack_tokens(): pl.pallas_call(tokens_kernel, out_shape=jax.ShapeDtypeStruct((8, 3, 128,...]
where the time goes in v5:
time: 153 us; the launch traced here: 150 us
  blocking collectives  51.6 us (34%)
  starting transfers between devices  45.8 us (30%)
  waiting for transfers between devices  33.5 us (22%)
  Pallas kernels  14.8 us (10%)
  local copies, waits for them, and re-layouts  2.8 us (2%)
    all_to_all x1, blocking collectives, shards(): exchange(share(kept, arrived), AXES, axis_index_groups=stride_groups(False))  28.6 us
    all_to_all x1, starting transfers between devices, shards(): tokens = exchange(message, AXES, axis_index_groups=cube_groups())  23.4 us
    all_to_all x1, blocking collectives, shards(): own = exchange(total(terms), AXES, axis_index_groups=stride_groups(True))  23 us
    all_to_all x1, waiting for transfers between devices, shards(): tokens = exchange(message, AXES, axis_index_groups=cube_groups())  21 us
    all_to_all x1, starting transfers between devices, shards(): directions = exchange(jnp.broadcast_to(home[None], (16, 8, 512)), 'grp')  7.5 us
    all_to_all x1, waiting for transfers between devices, shards(): directions = exchange(jnp.broadcast_to(home[None], (16, 8, 512)), 'grp')  6.91 us
    ppermute x1, starting transfers between devices, shards(): other = lax.ppermute(own, AXES, core_pairs())  5.52 us
    all_to_all x1, starting transfers between devices, shards(): got = exchange(slots, 'grp')  5.5 us
  transfers between devices with their start and end apart: 6, of which 5 were waited for; matrix products, arithmetic and copies ran while one was open for 1% of the time, Pallas kernels for 6%

profile of v5, /device:TPU:1, one launch (start us, length us, event | category | flops | bytes accessed | tf_op | source)
XLA Modules:
  0.0 150.0 jit_solution(8696260664685425124)
XLA Ops:
  0.6 3.4 %shard_map.112 = bf16[8,3,128,512]{3,2,1,0:T(8,128)(2,1)} custom-call(s32[16]{0:T(128)} %order.1, bf16[128,8192]{1,0:T(8,128)(2,1)} %grads.1, bf16[128,512]{1,0:T(8,128)(2,1)} %features.1), custom_call_target="tpu_custom_call" | custom-call | tf_op jit(solution)/shard_map/pallas_call | solution.py:87
  4.1 23.4 %all-to-all-start = ((bf16[8,3,128,512]{3,2,1,0:T(8,128)(2,1)}), bf16[8,3,128,512]{3,2,1,0:T(8,128)(2,1)S(1)}, u32[]{:S(2)}, u32[]{:S(2)}) async-start(bf16[8,3,128,512]{3,2,1,0:T(8,128)(2,1)} %shard_map.112), calls=%async_computation | async-start | bytes 6291456 | tf_op jit(solution)/shard_map/all_to_all | solution.py:351
  28.1 0.7 copy.12.rows
  28.9 0.7 copy.13.owner_col
  29.6 1.8 %shard_map.113 = bf16[16,32,128]{2,1,0:T(8,128)(2,1)} custom-call(s32[1]{0:T(128)S(6)} %copy.15.live, s32[128,1]{1,0:T(8,128)} %copy.12.rows, s32[128,1]{1,0:T(8,128)} %copy.13.owner_col, s32[1,128]{1,0:T(1,128)} %bitcast.8, bf16[128,128]{1,0:T(8,128)(2,1)} %deltas.1), custom_call_target="tpu_custom_call" | custom-call | tf_op jit(solution)/shard_map/pallas_call | solution.py:116
  31.4 21.0 %all-to-all-done.tokens = bf16[8,3,128,512]{3,2,1,0:T(8,128)(2,1)S(1)} async-done(((bf16[8,3,128,512]{3,2,1,0:T(8,128)(2,1)}), bf16[8,3,128,512]{3,2,1,0:T(8,128)(2,1)S(1)}, u32[]{:S(2)}, u32[]{:S(2)}) %all-to-all-start) | async-done | bytes 3145760 | tf_op jit(solution)/shard_map/all_to_all | solution.py:351
  52.4 0.7 shard_map.116
  53.1 1.9 %collective-permute-start = (f32[2,2,128,512]{3,2,1,0:T(8,128)S(1)}, f32[2,2,128,512]{3,2,1,0:T(8,128)S(1)}, u32[]{:S(2)}, u32[]{:S(2)}) collective-permute-start(f32[2,2,128,512]{3,2,1,0:T(8,128)S(1)} %shard_map.116), channel_id=1, source_target_pairs={{0,64},{64,0},{128,192},{192,128},{256,320},{320,256},{384,448},{4... | collective-permute-start | bytes 3145736 | tf_op jit(solution)/shard_map/ppermute | solution.py:355
  55.1 0.7 shard_map.115.kept
  55.8 1.9 %collective-permute-done.arrived = f32[2,2,128,512]{3,2,1,0:T(8,128)S(1)} collective-permute-done((f32[2,2,128,512]{3,2,1,0:T(8,128)S(1)}, f32[2,2,128,512]{3,2,1,0:T(8,128)S(1)}, u32[]{:S(2)}, u32[]{:S(2)}) %collective-permute-start) | collective-permute-done | bytes 1048608 | tf_op jit(solution)/shard_map/ppermute | solution.py:355
  57.7 0.5 shard_map.117
  58.2 28.6 %all_to_all.25.terms = s16[64,40,128]{2,1,0:T(8,128)(2,1)S(1)} all-to-all(s16[64,40,128]{2,1,0:T(8,128)(2,1)S(1)} %shard_map.117), channel_id=1, replica_groups={{0,256,2,258,4,260,6,262,16,272,18,274,20,276,22,278,32,288,34,290,36,2..., dimensions={0} | all-to-all | bytes 1310720 | tf_op jit(solution)/shard_map/all_to_all | solution.py:357
  87.3 23.0 %all_to_all.26.own = s16[32,40,128]{2,1,0:T(8,128)(2,1)S(1)} all-to-all(s16[32,40,128]{2,1,0:T(8,128)(2,1)S(1)} %shard_map.118), channel_id=1, replica_groups={{0,256,2,258,4,260,6,262,16,272,18,274,20,276,22,278,32,288,34,290,36,2..., dimensions={0} | all-to-all | bytes 655360 | tf_op jit(solution)/shard_map/all_to_all | solution.py:358
  110.3 5.5 %collective-permute-start.1 = (s16[32,40,128]{2,1,0:T(8,128)(2,1)S(1)}, s16[32,40,128]{2,1,0:T(8,128)(2,1)S(1)}, u32[]{:S(2)}, u32[]{:S(2)}) collective-permute-start(s16[32,40,128]{2,1,0:T(8,128)(2,1)S(1)} %all_to_all.26.own), channel_id=1, source_target_pairs={{0,64},{64,0},{128,192},{192,128},{256,320},{320,256},{384,448},{4... | collective-permute-start | bytes 983048 | tf_op jit(solution)/shard_map/ppermute | solution.py:360
  115.8 5.5 %all-to-all-start.1 = ((bf16[16,32,128]{2,1,0:T(8,128)(2,1)}), bf16[16,32,128]{2,1,0:T(8,128)(2,1)S(1)}, u32[]{:S(2)}, u32[]{:S(2)}) async-start(bf16[16,32,128]{2,1,0:T(8,128)(2,1)} %shard_map.113), calls=%async_computation.1 | async-start | bytes 262144 | tf_op jit(solution)/shard_map/all_to_all | solution.py:359
  121.4 4.9 %shard_map.119 = bf16[8,512]{1,0:T(8,128)(2,1)S(1)} custom-call(s32[2]{0:T(128)S(1)} %pad_add_fusion.place, s16[32,40,128]{2,1,0:T(8,128)(2,1)S(1)} %all_to_all.26.own, s16[32,40,128]{2,1,0:T(8,128)(2,1)S(1)} %collective-permute-done.1.other), custom_call_target="tpu_custom_call" | custom-call | tf_op jit(solution)/shard_map/pallas_call | solution.py:293
  126.3 2.0 %collective-permute-start.2 = (bf16[8,512]{1,0:T(8,128)(2,1)S(1)}, bf16[8,512]{1,0:T(8,128)(2,1)S(1)}, u32[]{:S(2)}, u32[]{:S(2)}) collective-permute-start(bf16[8,512]{1,0:T(8,128)(2,1)S(1)} %shard_map.119), channel_id=1, source_target_pairs={{0,0},{64,16},{128,128},{192,144},{256,1},{320,17},{384,129},{448,... | collective-permute-start | bytes 24584 | tf_op jit(solution)/shard_map/ppermute | solution.py:364
  128.3 2.2 %all-to-all-done.1.got = bf16[16,32,128]{2,1,0:T(8,128)(2,1)S(1)} async-done(((bf16[16,32,128]{2,1,0:T(8,128)(2,1)}), bf16[16,32,128]{2,1,0:T(8,128)(2,1)S(1)}, u32[]{:S(2)}, u32[]{:S(2)}) %all-to-all-start.1) | async-done | bytes 131104 | tf_op jit(solution)/shard_map/all_to_all | solution.py:359
  130.5 1.5 %collective-permute-done.2 = bf16[8,512]{1,0:T(8,128)(2,1)S(1)} collective-permute-done((bf16[8,512]{1,0:T(8,128)(2,1)S(1)}, bf16[8,512]{1,0:T(8,128)(2,1)S(1)}, u32[]{:S(2)}, u32[]{:S(2)}) %collective-permute-start.2) | collective-permute-done | bytes 8224 | tf_op jit(solution)/shard_map/ppermute | solution.py:364
  132.0 0.7 broadcast_in_dim.2
  132.7 7.5 %all-to-all-start.4 = ((bf16[16,8,512]{2,1,0:T(8,128)(2,1)}), bf16[16,8,512]{2,1,0:T(8,128)(2,1)S(1)}, u32[]{:S(2)}, u32[]{:S(2)}) async-start(bf16[16,8,512]{2,1,0:T(8,128)(2,1)} %broadcast_in_dim.2), calls=%async_computation.4 | async-start | bytes 262144 | tf_op jit(solution)/shard_map/all_to_all | solution.py:367
  140.2 2.2 %shard_map.114 = (f32[512,128]{1,0:T(8,128)}, f32[1,512]{1,0:T(1,128)}) custom-call(bf16[16,32,128]{2,1,0:T(8,128)(2,1)} %copy-done, f32[512,128]{1,0:T(8,128)} %table.1, f32[1,512]{1,0:T(1,128)} %bitcast.7), custom_call_target="tpu_custom_call" | custom-call | tf_op jit(solution)/shard_map/pallas_call | solution.py:321
  142.4 6.9 %all-to-all-done.4 = bf16[16,8,512]{2,1,0:T(8,128)(2,1)S(1)} async-done(((bf16[16,8,512]{2,1,0:T(8,128)(2,1)}), bf16[16,8,512]{2,1,0:T(8,128)(2,1)S(1)}, u32[]{:S(2)}, u32[]{:S(2)}) %all-to-all-start.4) | async-done | bytes 131104 | tf_op jit(solution)/shard_map/all_to_all | solution.py:367
  149.3 0.7 copy.16
  (9 shorter events, 0.6 us)
Async XLA Ops:
  4.1 24.0 %copy-start.2 = (s32[128]{0:T(128)S(1)}, s32[128]{0:T(128)}, u32[]{:S(2)}) copy-start(s32[128]{0:T(128)} %param.14) | copy-start | bytes 1540
  4.1 24.8 %copy-start.1 = (s32[128,1]{0,1:T(1,128)S(1)}, s32[128,1]{0,1:T(1,128)}, u32[]{:S(2)}) copy-start(s32[128,1]{0,1:T(1,128)} %param.15) | copy-start | bytes 1540
  4.1 48.3 %all-to-all-start = ((bf16[8,3,128,512]{3,2,1,0:T(8,128)(2,1)}), bf16[8,3,128,512]{3,2,1,0:T(8,128)(2,1)S(1)}, u32[]{:S(2)}, u32[]{:S(2)}) async-start(bf16[8,3,128,512]{3,2,1,0:T(8,128)(2,1)} %shard_map.112), calls=%async_computation | async-start | bytes 6291456 | tf_op jit(solution)/shard_map/all_to_all | solution.py:351
  53.1 4.6 %collective-permute-start = (f32[2,2,128,512]{3,2,1,0:T(8,128)S(1)}, f32[2,2,128,512]{3,2,1,0:T(8,128)S(1)}, u32[]{:S(2)}, u32[]{:S(2)}) collective-permute-start(f32[2,2,128,512]{3,2,1,0:T(8,128)S(1)} %shard_map.116), channel_id=1, source_target_pairs={{0,64},{64,0},{128,192},{192,128},{256,320},{320,256},{384,448},{4... | collective-permute-start | bytes 3145736 | tf_op jit(solution)/shard_map/ppermute | solution.py:355
  110.3 11.1 %collective-permute-start.1 = (s16[32,40,128]{2,1,0:T(8,128)(2,1)S(1)}, s16[32,40,128]{2,1,0:T(8,128)(2,1)S(1)}, u32[]{:S(2)}, u32[]{:S(2)}) collective-permute-start(s16[32,40,128]{2,1,0:T(8,128)(2,1)S(1)} %all_to_all.26.own), channel_id=1, source_target_pairs={{0,64},{64,0},{128,192},{192,128},{256,320},{320,256},{384,448},{4... | collective-permute-start | bytes 983048 | tf_op jit(solution)/shard_map/ppermute | solution.py:360
  115.8 14.7 %all-to-all-start.1 = ((bf16[16,32,128]{2,1,0:T(8,128)(2,1)}), bf16[16,32,128]{2,1,0:T(8,128)(2,1)S(1)}, u32[]{:S(2)}, u32[]{:S(2)}) async-start(bf16[16,32,128]{2,1,0:T(8,128)(2,1)} %shard_map.113), calls=%async_computation.1 | async-start | bytes 262144 | tf_op jit(solution)/shard_map/all_to_all | solution.py:359
  126.3 5.7 %collective-permute-start.2 = (bf16[8,512]{1,0:T(8,128)(2,1)S(1)}, bf16[8,512]{1,0:T(8,128)(2,1)S(1)}, u32[]{:S(2)}, u32[]{:S(2)}) collective-permute-start(bf16[8,512]{1,0:T(8,128)(2,1)S(1)} %shard_map.119), channel_id=1, source_target_pairs={{0,0},{64,16},{128,128},{192,144},{256,1},{320,17},{384,129},{448,... | collective-permute-start | bytes 24584 | tf_op jit(solution)/shard_map/ppermute | solution.py:364
  130.5 9.7 %copy-start = (bf16[16,32,128]{2,1,0:T(8,128)(2,1)}, bf16[16,32,128]{2,1,0:T(8,128)(2,1)S(1)}, u32[]{:S(2)}) copy-start(bf16[16,32,128]{2,1,0:T(8,128)(2,1)S(1)} %all-to-all-done.1.got) | copy-start | bytes 393220
  132.7 16.7 %all-to-all-start.4 = ((bf16[16,8,512]{2,1,0:T(8,128)(2,1)}), bf16[16,8,512]{2,1,0:T(8,128)(2,1)S(1)}, u32[]{:S(2)}, u32[]{:S(2)}) async-start(bf16[16,8,512]{2,1,0:T(8,128)(2,1)} %broadcast_in_dim.2), calls=%async_computation.4 | async-start | bytes 262144 | tf_op jit(solution)/shard_map/all_to_all | solution.py:367

commit v6 on v5

--- a/solution.py
+++ b/solution.py
@@ -63,6 +63,10 @@
     return [(device(x, y, z, c), device(x, y, z, 1 - c)) for x, y, z in chips() for c in range(2)]
 
 
+def z_pairs(step):
+    return [(device(x, y, z, c), device(x, y, z ^ step, c)) for x, y, z in chips() for c in range(2)]
+
+
 def home_pairs():
     pairs = []
     for x, y, z in chips():
@@ -93,13 +97,14 @@
     )(order, grads, features)
 
 
-def slots_kernel(live, rows, owner_col, owner_row, deltas, out):
+def slots_kernel(live, core, rows, owner_col, owner_row, deltas, away, kept, placed):
     count = deltas.shape[0]
     before = lax.broadcasted_iota(jnp.int32, (count, count), 0)
     after = lax.broadcasted_iota(jnp.int32, (count, count), 1)
     same = (owner_col[...] == owner_row[...]) & (before < after)
     rank = jnp.sum(same.astype(jnp.float32), axis=0, keepdims=True)
-    position = owner_row[...].astype(jnp.float32) * 16.0 + rank
+    owner = owner_row[...]
+    position = ((owner % 2) * 128 + (owner // 2) * 16).astype(jnp.float32) + rank
     place = lax.broadcasted_iota(jnp.int32, (256, count), 0).astype(jnp.float32) == position
     place = place.astype(jnp.float32).astype(jnp.bfloat16)
     masked = jnp.where(before < live[0], deltas[...].astype(jnp.float32), 0.0).astype(jnp.bfloat16)
@@ -107,18 +112,43 @@
     keys = jnp.where(after < 64, high, low).astype(jnp.float32).astype(jnp.bfloat16)
     moved = jnp.dot(place, masked, preferred_element_type=jnp.float32).astype(jnp.bfloat16)
     named = jnp.dot(place, keys, preferred_element_type=jnp.float32).astype(jnp.bfloat16)
-    out[:, 0:16, :] = moved.reshape(16, 16, 128)
-    out[:, 16:32, :] = named.reshape(16, 16, 128)
-
-
-def pack_slots(live, rows, owner, deltas):
-    vmem = pl.BlockSpec(memory_space=pltpu.VMEM)
+    placed[:, :, 0:16, :] = moved.reshape(2, 8, 16, 128)
+    placed[:, :, 16:32, :] = named.reshape(2, 8, 16, 128)
+    away[...] = placed[1 - core[0]]
+    kept[...] = placed[core[0]]
+
+
+def pack_slots(live, core, rows, owner, deltas):
+    vmem = pl.BlockSpec(memory_space=pltpu.VMEM)
+    smem = pl.BlockSpec(memory_space=pltpu.SMEM)
+    half = jax.ShapeDtypeStruct((8, 32, 128), jnp.bfloat16)
     return pl.pallas_call(
         slots_kernel,
-        out_shape=jax.ShapeDtypeStruct((16, 32, 128), jnp.bfloat16),
-        in_specs=[pl.BlockSpec(memory_space=pltpu.SMEM), vmem, vmem, vmem, vmem],
-        out_specs=vmem,
-    )(live, rows.reshape(-1, 1), owner, owner.reshape(1, -1), deltas)
+        out_shape=(half, half),
+        in_specs=[smem, smem, vmem, vmem, vmem, vmem],
+        out_specs=(vmem, vmem),
+        scratch_shapes=[pltpu.VMEM((2, 8, 32, 128), jnp.bfloat16)],
+    )(live, core, rows.reshape(-1, 1), owner, owner.reshape(1, -1), deltas)
+
+
+def sort_kernel(bit, first, second, away, kept):
+    count = first.shape[0]
+    for n, source in enumerate((first, second)):
+        rows = pl.ds(n * count, count)
+        away[rows] = source[:, 1 - bit[0]]
+        kept[rows] = source[:, bit[0]]
+
+
+def sort_slots(bit, first, second, count):
+    vmem = pl.BlockSpec(memory_space=pltpu.VMEM)
+    split = (count, 2, 4 // count, 32, 128)
+    half = jax.ShapeDtypeStruct((2 * count, 4 // count, 32, 128), jnp.bfloat16)
+    return pl.pallas_call(
+        sort_kernel,
+        out_shape=(half, half),
+        in_specs=[pl.BlockSpec(memory_space=pltpu.SMEM), vmem, vmem],
+        out_specs=(vmem, vmem),
+    )(bit, first.reshape(split), second.reshape(split))
 
 
 def grad_kernel(half, tokens, out):
@@ -228,9 +258,9 @@
     return lax.dot_general(a, b, (contract, ((), ())), preferred_element_type=jnp.float32)
 
 
-def full_product(a, b, contract):
-    (ah, al), (bh, bl) = a, b
-    return product(ah, bh, contract) + (product(ah, bl, contract) + product(al, bh, contract))
+def symmetric_product(high, low, contract):
+    side = product(high, low, contract)
+    return product(high, high, contract) + (side + jnp.transpose(side))
 
 
 def rows_product(rows, b):
@@ -254,31 +284,33 @@
     width = g.shape[0]
     frobenius = jnp.sum(g * g) + 1e-06
     g_parts = parts_of(g)
-    normal = full_product(g_parts, g_parts, ((1,), (1,))) / frobenius
+    normal = symmetric_product(*g_parts, ((1,), (1,))) * (1.0 / frobenius)
     n_parts = parts_of(normal)
-    squared = full_product(n_parts, n_parts, ((1,), (0,)))
+    squared = symmetric_product(*n_parts, ((1,), (1,)))
     total = jnp.sum(jnp.sum(squared * squared, axis=0, keepdims=True), axis=1, keepdims=True)
     bound = jnp.sqrt(jnp.sqrt(total))
     scale = frobenius * bound
-    m = normal / bound
-    m2 = squared / (bound * bound)
-    power[...] = m
-    square[...] = m2
+    to_m = 1.0 / bound
+    to_m2 = to_m * to_m
+    power[...] = normal
+    square[...] = squared
     diagonal = lax.broadcasted_iota(jnp.int32, (width, width), 0) == lax.broadcasted_iota(
         jnp.int32, (width, width), 1
     )
-    f2 = (jnp.where(diagonal, 25.0, 0.0) - 10.0 * m + m2) / 16.0
-    m_parts, f_parts = parts_of(m), parts_of(f2)
-    m_rows = power[pl.ds(first_row, 8), :]
-    m2_rows = square[pl.ds(first_row, 8), :]
+    f2 = jnp.where(diagonal, 25.0 / 16.0, 0.0) + (
+        normal * (to_m * (-10.0 / 16.0)) + squared * (to_m2 / 16.0)
+    )
+    f_parts = parts_of(f2)
+    m_rows = power[pl.ds(first_row, 8), :] * to_m
+    m2_rows = square[pl.ds(first_row, 8), :] * to_m2
     basis = lax.broadcasted_iota(jnp.int32, (8, width), 1) == first_row + lax.broadcasted_iota(
         jnp.int32, (8, width), 0
     )
     f_rows = (jnp.where(basis, 5.0, 0.0) - m_rows) / 4.0
     fm_rows = (5.0 * m_rows - m2_rows) / 4.0
     root = (5.0 * f_rows - rows_product(rows_product(fm_rows, f_parts), f_parts)) / 4.0
-    m_root = rows_product(root, m_parts)
-    m2_root = rows_product(m_root, m_parts)
+    m_root = rows_product(root, n_parts) * to_m
+    m2_root = rows_product(m_root, n_parts) * to_m
     f_rows = (5.0 * root - m_root) / 4.0
     fm_rows = (5.0 * m_root - m2_root) / 4.0
     root = (5.0 * f_rows - rows_product(rows_product(fm_rows, f_parts), f_parts)) / 4.0
@@ -300,9 +332,13 @@
     )(place, own, other)
 
 
-def update_kernel(got, table, accum, new_table, new_accum):
-    deltas = got[:, 0:16, :].reshape(256, 128)
-    keys = got[:, 16:32, :].astype(jnp.float32).reshape(256, 128)
+def update_kernel(first, second, table, accum, new_table, new_accum):
+    deltas = jnp.concatenate(
+        [got[:, 0:16, :].reshape(128, 128) for got in (first, second)], axis=0
+    )
+    keys = jnp.concatenate(
+        [got[:, 16:32, :].astype(jnp.float32).reshape(128, 128) for got in (first, second)], axis=0
+    )
     row = keys[:, 0:1] * 16.0 + keys[:, 64:65]
     count = table.shape[0]
     named = row == lax.broadcasted_iota(jnp.int32, (256, count), 1).astype(jnp.float32)
@@ -316,7 +352,7 @@
     new_accum[...] = jnp.transpose(after)[0:1, :]
 
 
-def update_rows(got, table, accum):
+def update_rows(first, second, table, accum):
     vmem = pl.BlockSpec(memory_space=pltpu.VMEM)
     return pl.pallas_call(
         update_kernel,
@@ -324,9 +360,9 @@
             jax.ShapeDtypeStruct(table.shape, jnp.float32),
             jax.ShapeDtypeStruct((1, accum.shape[0]), jnp.float32),
         ),
-        in_specs=[vmem, vmem, vmem],
+        in_specs=[vmem, vmem, vmem, vmem],
         out_specs=(vmem, vmem),
-    )(got, table, accum.reshape(1, -1))
+    )(first, second, table, accum.reshape(1, -1))
 
 
 def shards(
@@ -345,25 +381,33 @@
     x, y = replica // SIDE, replica % SIDE
     exchange = partial(lax.all_to_all, split_axis=0, concat_axis=0, tiled=True)
 
-    slots = pack_slots(live_counts, hot_rows, hot_owner, hot_deltas)
-
     message = pack_tokens(block_order, output_grads, features)
     tokens = exchange(message, AXES, axis_index_groups=cube_groups())
-    tokens, slots = lax.optimization_barrier((tokens, slots))
+
+    parting, first = pack_slots(live_counts, core.reshape(1), hot_rows, hot_owner, hot_deltas)
+    tokens, parting, first = lax.optimization_barrier((tokens, parting, first))
 
     away = partial_grads((1 - core).reshape(1), tokens)
     arrived = lax.ppermute(away, AXES, core_pairs())
     kept = partial_grads(core.reshape(1), tokens)
     terms = exchange(share(kept, arrived), AXES, axis_index_groups=stride_groups(False))
+
+    second = lax.ppermute(parting, AXES, core_pairs())
+    for step, count in ((4, 1), (2, 2), (1, 4)):
+        bit = ((z // step) % 2).reshape(1)
+        parting, first = sort_slots(bit, first, second, count)
+        second = lax.ppermute(parting, AXES, z_pairs(step))
+    first, second = first.reshape(8, 32, 128), second.reshape(8, 32, 128)
+    terms, first, second = lax.optimization_barrier((terms, first, second))
+
     own = exchange(total(terms), AXES, axis_index_groups=stride_groups(True))
-    got = exchange(slots, "grp")
     other = lax.ppermute(own, AXES, core_pairs())
     turn = piece(x, y, z)
     first_row = (turn // 16) * 256 + core * 128 + (turn % 16) * 8
     rows = direction_rows(jnp.stack([core, first_row]).astype(jnp.int32), own, other)
     home = lax.ppermute(rows, AXES, home_pairs())
 
-    new_table, new_accum = update_rows(got, emb_table, row_accum)
+    new_table, new_accum = update_rows(first, second, emb_table, row_accum)
     directions = exchange(jnp.broadcast_to(home[None], (16, 8, 512)), "grp")
     return (new_table, new_accum.reshape(-1), directions)
 

time: 153 us -> 169 us (1.10)
  blocking collectives: 51.6 us -> 23.8 us
  starting transfers between devices: 45.8 us -> 68.3 us
  waiting for transfers between devices: 33.5 us -> 48.9 us
  Pallas kernels: 14.8 us -> 19.8 us
  local copies, waits for them, and re-layouts: 2.8 us -> 4.7 us
    all_to_all x1 -> x0, blocking collectives: 28.6 us -> none  [shards(): exchange(share(kept, arrived), AXES, axis_index_groups=stride_groups(False))]
    ppermute x0 -> x4, starting transfers between devices: none -> 19.2 us  [the longest x3 16.8 us: shards(): second = lax.ppermute(parting, AXES, z_pairs(step))]
    ppermute x0 -> x4, waiting for transfers between devices: none -> 15 us  [the longest x3 14.2 us: shards(): second = lax.ppermute(parting, AXES, z_pairs(step))]
    pallas_call x1 -> x4, Pallas kernels: 1.81 us -> 6.4 us  [the longest x3 4.59 us: sort_slots(): pl.pallas_call(sort_kernel, out_shape=(half, half), in_specs=[pl.BlockSpe...]
    all_to_all x1, waiting for transfers between devices: 2.25 us -> 0.01 us  [shards(): exchange(share(kept, arrived), AXES, axis_index_groups=stride_groups(False))]
    unnamed x8 -> x16, local copies, waits for them, and re-layouts: 1.4 us -> 3.3 us
    all_to_all x1, starting transfers between devices: 5.5 us -> 7.2 us  [shards(): exchange(share(kept, arrived), AXES, axis_index_groups=stride_groups(False))]
  transfers between devices with their start and end apart: 6 -> 10, of which waited for: 5 -> 9; matrix products, arithmetic and copies ran while one was open for 1% -> 1% of each run, Pallas kernels for 6% -> 6%
where the time goes in v6:
time: 169 us; the launch traced here: 167 us
  starting transfers between devices  68.3 us (40%)
  waiting for transfers between devices  48.9 us (29%)
  blocking collectives  23.8 us (14%)
  Pallas kernels  19.8 us (12%)
  local copies, waits for them, and re-layouts  4.7 us (3%)
    all_to_all x1, blocking collectives, shards(): own = exchange(total(terms), AXES, axis_index_groups=stride_groups(True))  23.8 us
    all_to_all x1, starting transfers between devices, shards(): tokens = exchange(message, AXES, axis_index_groups=cube_groups())  23.4 us
    all_to_all x1, waiting for transfers between devices, shards(): tokens = exchange(message, AXES, axis_index_groups=cube_groups())  21 us
    ppermute x3, starting transfers between devices, shards(): second = lax.ppermute(parting, AXES, z_pairs(step))  16.8 us
    ppermute x3, waiting for transfers between devices, shards(): second = lax.ppermute(parting, AXES, z_pairs(step))  14.2 us
    all_to_all x1, starting transfers between devices, shards(): exchange(share(kept, arrived), AXES, axis_index_groups=stride_groups(False))  7.2 us
    ppermute x1, starting transfers between devices, shards(): other = lax.ppermute(own, AXES, core_pairs())  7.04 us
    all_to_all x1, waiting for transfers between devices, shards(): directions = exchange(jnp.broadcast_to(home[None], (16, 8, 512)), 'grp')  6.87 us
  transfers between devices with their start and end apart: 10, of which 9 were waited for; matrix products, arithmetic and copies ran while one was open for 1% of the time, Pallas kernels for 6%

profile of v6, /device:TPU:1, one launch (start us, length us, event | category | flops | bytes accessed | tf_op | source)
XLA Modules:
  0.0 167.1 jit_solution(8553589555317285251)
XLA Ops:
  0.6 3.5 %shard_map.112 = bf16[8,3,128,512]{3,2,1,0:T(8,128)(2,1)} custom-call(s32[16]{0:T(128)} %order.1, bf16[128,8192]{1,0:T(8,128)(2,1)} %grads.1, bf16[128,512]{1,0:T(8,128)(2,1)} %features.1), custom_call_target="tpu_custom_call" | custom-call | tf_op jit(solution)/shard_map/pallas_call | solution.py:91
  4.1 23.4 %all-to-all-start = ((bf16[8,3,128,512]{3,2,1,0:T(8,128)(2,1)}), bf16[8,3,128,512]{3,2,1,0:T(8,128)(2,1)S(1)}, u32[]{:S(2)}, u32[]{:S(2)}) async-start(bf16[8,3,128,512]{3,2,1,0:T(8,128)(2,1)} %shard_map.112), calls=%async_computation | async-start | bytes 6291456 | tf_op jit(solution)/shard_map/all_to_all | solution.py:385
  29.6 1.8 %shard_map.113 = (bf16[8,32,128]{2,1,0:T(8,128)(2,1)}, bf16[8,32,128]{2,1,0:T(8,128)(2,1)}) custom-call(s32[1]{0:T(128)S(6)} %copy.16.live, s32[1]{0:T(128)} %bitcast.core.half, s32[128,1]{1,0:T(8,128)} %copy.12.rows, s32[128,1]{1,0:T(8,128)} %copy.13.owner_col, s32[1,128]{1,0:T(1,128)} %bitcast.28, bf16[128,128]{1,0:T(8,128)(2,1)} %deltas.1), custom_call_target="tpu_custom_call" | custom-call | tf_op jit(solution)/shard_map/pallas_call | solution.py:125
  31.4 21.0 %all-to-all-done.tokens = bf16[8,3,128,512]{3,2,1,0:T(8,128)(2,1)S(1)} async-done(((bf16[8,3,128,512]{3,2,1,0:T(8,128)(2,1)}), bf16[8,3,128,512]{3,2,1,0:T(8,128)(2,1)S(1)}, u32[]{:S(2)}, u32[]{:S(2)}) %all-to-all-start) | async-done | bytes 3145760 | tf_op jit(solution)/shard_map/all_to_all | solution.py:385
  53.1 2.1 %collective-permute-start = (f32[2,2,128,512]{3,2,1,0:T(8,128)S(1)}, f32[2,2,128,512]{3,2,1,0:T(8,128)S(1)}, u32[]{:S(2)}, u32[]{:S(2)}) collective-permute-start(f32[2,2,128,512]{3,2,1,0:T(8,128)S(1)} %shard_map.115), channel_id=1, source_target_pairs={{0,64},{64,0},{128,192},{192,128},{256,320},{320,256},{384,448},{4... | collective-permute-start | bytes 3145736 | tf_op jit(solution)/shard_map/ppermute | solution.py:391
  56.0 1.9 %collective-permute-done.arrived = f32[2,2,128,512]{3,2,1,0:T(8,128)S(1)} collective-permute-done((f32[2,2,128,512]{3,2,1,0:T(8,128)S(1)}, f32[2,2,128,512]{3,2,1,0:T(8,128)S(1)}, u32[]{:S(2)}, u32[]{:S(2)}) %collective-permute-start) | collective-permute-done | bytes 1048608 | tf_op jit(solution)/shard_map/ppermute | solution.py:391
  59.2 7.2 %all-to-all-start.1 = ((s16[64,40,128]{2,1,0:T(8,128)(2,1)}), s16[64,40,128]{2,1,0:T(8,128)(2,1)S(1)}, u32[]{:S(2)}, u32[]{:S(2)}) async-start(s16[64,40,128]{2,1,0:T(8,128)(2,1)} %shard_map.116), calls=%async_computation.1 | async-start | bytes 1310720 | tf_op jit(solution)/shard_map/all_to_all | solution.py:393
  66.4 2.3 %collective-permute-start.1 = (bf16[8,32,128]{2,1,0:T(8,128)(2,1)S(1)}, bf16[8,32,128]{2,1,0:T(8,128)(2,1)S(1)}, u32[]{:S(2)}, u32[]{:S(2)}) collective-permute-start(bf16[8,32,128]{2,1,0:T(8,128)(2,1)S(1)} %copy-done.6), channel_id=1, source_target_pairs={{0,64},{64,0},{128,192},{192,128},{256,320},{320,256},{384,448},{4... | collective-permute-start | bytes 196616 | tf_op jit(solution)/shard_map/ppermute | solution.py:395
  70.3 1.5 shard_map.117
  71.8 7.2 %collective-permute-start.2 = (bf16[2,4,32,128]{3,2,1,0:T(8,128)(2,1)}, bf16[2,4,32,128]{3,2,1,0:T(8,128)(2,1)S(1)}, u32[]{:S(2)}, u32[]{:S(2)}) collective-permute-start(bf16[2,4,32,128]{3,2,1,0:T(8,128)(2,1)} %get-tuple-element.25), channel_id=1, source_target_pairs={{0,512},{64,576},{128,640},{192,704},{256,768},{320,832},{384,896}... | collective-permute-start | bytes 196616 | tf_op jit(solution)/shard_map/ppermute | solution.py:399
  79.1 10.5 %collective-permute-done.2 = bf16[2,4,32,128]{3,2,1,0:T(8,128)(2,1)S(1)} collective-permute-done((bf16[2,4,32,128]{3,2,1,0:T(8,128)(2,1)}, bf16[2,4,32,128]{3,2,1,0:T(8,128)(2,1)S(1)}, u32[]{:S(2)}, u32[]{:S(2)}) %collective-permute-start.2) | collective-permute-done | bytes 65568 | tf_op jit(solution)/shard_map/ppermute | solution.py:399
  91.7 5.9 %collective-permute-start.3 = (bf16[4,2,32,128]{3,2,1,0:T(8,128)(2,1)}, bf16[4,2,32,128]{3,2,1,0:T(8,128)(2,1)S(1)}, u32[]{:S(2)}, u32[]{:S(2)}) collective-permute-start(bf16[4,2,32,128]{3,2,1,0:T(8,128)(2,1)} %get-tuple-element.27), channel_id=1, source_target_pairs={{0,256},{64,320},{128,384},{192,448},{256,0},{320,64},{384,128},{4... | collective-permute-start | bytes 196616 | tf_op jit(solution)/shard_map/ppermute | solution.py:399
  97.7 1.8 %collective-permute-done.3 = bf16[4,2,32,128]{3,2,1,0:T(8,128)(2,1)S(1)} collective-permute-done((bf16[4,2,32,128]{3,2,1,0:T(8,128)(2,1)}, bf16[4,2,32,128]{3,2,1,0:T(8,128)(2,1)S(1)}, u32[]{:S(2)}, u32[]{:S(2)}) %collective-permute-start.3) | collective-permute-done | bytes 65568 | tf_op jit(solution)/shard_map/ppermute | solution.py:399
  100.1 1.5 shard_map.119
  101.7 3.7 %collective-permute-start.4 = (bf16[8,1,32,128]{3,2,0,1:T(8,128)(2,1)}, bf16[8,1,32,128]{3,2,0,1:T(8,128)(2,1)S(1)}, u32[]{:S(2)}, u32[]{:S(2)}) collective-permute-start(bf16[8,1,32,128]{3,2,0,1:T(8,128)(2,1)} %bitcast.30), channel_id=1, source_target_pairs={{0,128},{64,192},{128,0},{192,64},{256,384},{320,448},{384,256},{4... | collective-permute-start | bytes 196616 | tf_op jit(solution)/shard_map/ppermute | solution.py:399
  105.4 1.9 %collective-permute-done.4 = bf16[8,1,32,128]{3,2,0,1:T(8,128)(2,1)S(1)} collective-permute-done((bf16[8,1,32,128]{3,2,0,1:T(8,128)(2,1)}, bf16[8,1,32,128]{3,2,0,1:T(8,128)(2,1)S(1)}, u32[]{:S(2)}, u32[]{:S(2)}) %collective-permute-start.4) | collective-permute-done | bytes 65568 | tf_op jit(solution)/shard_map/ppermute | solution.py:399
  107.8 23.8 %all_to_all.20.own = s16[32,40,128]{2,1,0:T(8,128)(2,1)S(1)} all-to-all(s16[32,40,128]{2,1,0:T(8,128)(2,1)S(1)} %shard_map.121), channel_id=1, replica_groups={{0,256,2,258,4,260,6,262,16,272,18,274,20,276,22,278,32,288,34,290,36,2..., dimensions={0} | all-to-all | bytes 655360 | tf_op jit(solution)/shard_map/all_to_all | solution.py:403
  131.5 7.0 %collective-permute-start.5 = (s16[32,40,128]{2,1,0:T(8,128)(2,1)S(1)}, s16[32,40,128]{2,1,0:T(8,128)(2,1)S(1)}, u32[]{:S(2)}, u32[]{:S(2)}) collective-permute-start(s16[32,40,128]{2,1,0:T(8,128)(2,1)S(1)} %all_to_all.20.own), channel_id=1, source_target_pairs={{0,64},{64,0},{128,192},{192,128},{256,320},{320,256},{384,448},{4... | collective-permute-start | bytes 983048 | tf_op jit(solution)/shard_map/ppermute | solution.py:404
  139.8 4.3 %shard_map.122 = bf16[8,512]{1,0:T(8,128)(2,1)S(1)} custom-call(s32[2]{0:T(128)S(1)} %pad_add_fusion.place, s16[32,40,128]{2,1,0:T(8,128)(2,1)S(1)} %all_to_all.20.own, s16[32,40,128]{2,1,0:T(8,128)(2,1)S(1)} %collective-permute-done.5.other), custom_call_target="tpu_custom_call" | custom-call | tf_op jit(solution)/shard_map/pallas_call | solution.py:325
  144.1 2.7 %collective-permute-start.6 = (bf16[8,512]{1,0:T(8,128)(2,1)S(1)}, bf16[8,512]{1,0:T(8,128)(2,1)S(1)}, u32[]{:S(2)}, u32[]{:S(2)}) collective-permute-start(bf16[8,512]{1,0:T(8,128)(2,1)S(1)} %shard_map.122), channel_id=1, source_target_pairs={{0,0},{64,16},{128,128},{192,144},{256,1},{320,17},{384,129},{448,... | collective-permute-start | bytes 24584 | tf_op jit(solution)/shard_map/ppermute | solution.py:408
  146.8 3.0 %collective-permute-done.6 = bf16[8,512]{1,0:T(8,128)(2,1)S(1)} collective-permute-done((bf16[8,512]{1,0:T(8,128)(2,1)S(1)}, bf16[8,512]{1,0:T(8,128)(2,1)S(1)}, u32[]{:S(2)}, u32[]{:S(2)}) %collective-permute-start.6) | collective-permute-done | bytes 8224 | tf_op jit(solution)/shard_map/ppermute | solution.py:408
  150.5 6.7 %all-to-all-start.3 = ((bf16[16,8,512]{2,1,0:T(8,128)(2,1)}), bf16[16,8,512]{2,1,0:T(8,128)(2,1)S(1)}, u32[]{:S(2)}, u32[]{:S(2)}) async-start(bf16[16,8,512]{2,1,0:T(8,128)(2,1)} %broadcast_in_dim.2), calls=%async_computation.3 | async-start | bytes 262144 | tf_op jit(solution)/shard_map/all_to_all | solution.py:411
  157.2 2.3 %shard_map.120 = (f32[512,128]{1,0:T(8,128)}, f32[1,512]{1,0:T(1,128)}) custom-call(bf16[8,32,128]{2,1,0:T(8,128)(2,1)} %bitcast.25, bf16[8,32,128]{2,1,0:T(8,128)(2,1)} %bitcast.26, f32[512,128]{1,0:T(8,128)} %table.1, f32[1,512]{1,0:T(1,128)} %bitcast.27), custom_call_target="tpu_custom_call" | custom-call | tf_op jit(solution)/shard_map/pallas_call | solution.py:357
  159.5 6.9 %all-to-all-done.3 = bf16[16,8,512]{2,1,0:T(8,128)(2,1)S(1)} async-done(((bf16[16,8,512]{2,1,0:T(8,128)(2,1)}), bf16[16,8,512]{2,1,0:T(8,128)(2,1)S(1)}, u32[]{:S(2)}, u32[]{:S(2)}) %all-to-all-start.3) | async-done | bytes 131104 | tf_op jit(solution)/shard_map/all_to_all | solution.py:411
  (27 shorter events, 11.5 us)
Async XLA Ops:
  4.1 24.0 %copy-start.5 = (s32[128]{0:T(128)S(1)}, s32[128]{0:T(128)}, u32[]{:S(2)}) copy-start(s32[128]{0:T(128)} %param.14) | copy-start | bytes 1540
  4.1 24.8 %copy-start.4 = (s32[128,1]{0,1:T(1,128)S(1)}, s32[128,1]{0,1:T(1,128)}, u32[]{:S(2)}) copy-start(s32[128,1]{0,1:T(1,128)} %param.15) | copy-start | bytes 1540
  4.1 48.3 %all-to-all-start = ((bf16[8,3,128,512]{3,2,1,0:T(8,128)(2,1)}), bf16[8,3,128,512]{3,2,1,0:T(8,128)(2,1)S(1)}, u32[]{:S(2)}, u32[]{:S(2)}) async-start(bf16[8,3,128,512]{3,2,1,0:T(8,128)(2,1)} %shard_map.112), calls=%async_computation | async-start | bytes 6291456 | tf_op jit(solution)/shard_map/all_to_all | solution.py:385
  53.1 13.3 %copy-start.6 = (bf16[8,32,128]{2,1,0:T(8,128)(2,1)S(1)}, bf16[8,32,128]{2,1,0:T(8,128)(2,1)}, u32[]{:S(2)}) copy-start(bf16[8,32,128]{2,1,0:T(8,128)(2,1)} %get-tuple-element.23) | copy-start | bytes 196612
  53.1 4.7 %collective-permute-start = (f32[2,2,128,512]{3,2,1,0:T(8,128)S(1)}, f32[2,2,128,512]{3,2,1,0:T(8,128)S(1)}, u32[]{:S(2)}, u32[]{:S(2)}) collective-permute-start(f32[2,2,128,512]{3,2,1,0:T(8,128)S(1)} %shard_map.115), channel_id=1, source_target_pairs={{0,64},{64,0},{128,192},{192,128},{256,320},{320,256},{384,448},{4... | collective-permute-start | bytes 3145736 | tf_op jit(solution)/shard_map/ppermute | solution.py:391
  59.2 48.1 %all-to-all-start.1 = ((s16[64,40,128]{2,1,0:T(8,128)(2,1)}), s16[64,40,128]{2,1,0:T(8,128)(2,1)S(1)}, u32[]{:S(2)}, u32[]{:S(2)}) async-start(s16[64,40,128]{2,1,0:T(8,128)(2,1)} %shard_map.116), calls=%async_computation.1 | async-start | bytes 1310720 | tf_op jit(solution)/shard_map/all_to_all | solution.py:393
  66.4 3.2 %collective-permute-start.1 = (bf16[8,32,128]{2,1,0:T(8,128)(2,1)S(1)}, bf16[8,32,128]{2,1,0:T(8,128)(2,1)S(1)}, u32[]{:S(2)}, u32[]{:S(2)}) collective-permute-start(bf16[8,32,128]{2,1,0:T(8,128)(2,1)S(1)} %copy-done.6), channel_id=1, source_target_pairs={{0,64},{64,0},{128,192},{192,128},{256,320},{320,256},{384,448},{4... | collective-permute-start | bytes 196616 | tf_op jit(solution)/shard_map/ppermute | solution.py:395
  69.7 0.6 copy-start
  71.8 17.8 %collective-permute-start.2 = (bf16[2,4,32,128]{3,2,1,0:T(8,128)(2,1)}, bf16[2,4,32,128]{3,2,1,0:T(8,128)(2,1)S(1)}, u32[]{:S(2)}, u32[]{:S(2)}) collective-permute-start(bf16[2,4,32,128]{3,2,1,0:T(8,128)(2,1)} %get-tuple-element.25), channel_id=1, source_target_pairs={{0,512},{64,576},{128,640},{192,704},{256,768},{320,832},{384,896}... | collective-permute-start | bytes 196616 | tf_op jit(solution)/shard_map/ppermute | solution.py:399
  89.6 0.6 copy-start.1
  91.7 7.8 %collective-permute-start.3 = (bf16[4,2,32,128]{3,2,1,0:T(8,128)(2,1)}, bf16[4,2,32,128]{3,2,1,0:T(8,128)(2,1)S(1)}, u32[]{:S(2)}, u32[]{:S(2)}) collective-permute-start(bf16[4,2,32,128]{3,2,1,0:T(8,128)(2,1)} %get-tuple-element.27), channel_id=1, source_target_pairs={{0,256},{64,320},{128,384},{192,448},{256,0},{320,64},{384,128},{4... | collective-permute-start | bytes 196616 | tf_op jit(solution)/shard_map/ppermute | solution.py:399
  99.5 0.6 copy-start.2
  101.7 5.6 %collective-permute-start.4 = (bf16[8,1,32,128]{3,2,0,1:T(8,128)(2,1)}, bf16[8,1,32,128]{3,2,0,1:T(8,128)(2,1)S(1)}, u32[]{:S(2)}, u32[]{:S(2)}) collective-permute-start(bf16[8,1,32,128]{3,2,0,1:T(8,128)(2,1)} %bitcast.30), channel_id=1, source_target_pairs={{0,128},{64,192},{128,0},{192,64},{256,384},{320,448},{384,256},{4... | collective-permute-start | bytes 196616 | tf_op jit(solution)/shard_map/ppermute | solution.py:399
  107.3 50.0 %copy-start.3 = (bf16[8,1,32,128]{3,2,0,1:T(8,128)(2,1)}, bf16[8,1,32,128]{3,2,0,1:T(8,128)(2,1)S(1)}, u32[]{:S(2)}) copy-start(bf16[8,1,32,128]{3,2,0,1:T(8,128)(2,1)S(1)} %collective-permute-done.4) | copy-start | bytes 196612
  131.5 8.3 %collective-permute-start.5 = (s16[32,40,128]{2,1,0:T(8,128)(2,1)S(1)}, s16[32,40,128]{2,1,0:T(8,128)(2,1)S(1)}, u32[]{:S(2)}, u32[]{:S(2)}) collective-permute-start(s16[32,40,128]{2,1,0:T(8,128)(2,1)S(1)} %all_to_all.20.own), channel_id=1, source_target_pairs={{0,64},{64,0},{128,192},{192,128},{256,320},{320,256},{384,448},{4... | collective-permute-start | bytes 983048 | tf_op jit(solution)/shard_map/ppermute | solution.py:404
  144.1 5.8 %collective-permute-start.6 = (bf16[8,512]{1,0:T(8,128)(2,1)S(1)}, bf16[8,512]{1,0:T(8,128)(2,1)S(1)}, u32[]{:S(2)}, u32[]{:S(2)}) collective-permute-start(bf16[8,512]{1,0:T(8,128)(2,1)S(1)} %shard_map.122), channel_id=1, source_target_pairs={{0,0},{64,16},{128,128},{192,144},{256,1},{320,17},{384,129},{448,... | collective-permute-start | bytes 24584 | tf_op jit(solution)/shard_map/ppermute | solution.py:408
  150.5 15.9 %all-to-all-start.3 = ((bf16[16,8,512]{2,1,0:T(8,128)(2,1)}), bf16[16,8,512]{2,1,0:T(8,128)(2,1)S(1)}, u32[]{:S(2)}, u32[]{:S(2)}) async-start(bf16[16,8,512]{2,1,0:T(8,128)(2,1)} %broadcast_in_dim.2), calls=%async_computation.3 | async-start | bytes 262144 | tf_op jit(solution)/shard_map/all_to_all | solution.py:411

commit v7 on v5

--- a/solution.py
+++ b/solution.py
@@ -25,7 +25,7 @@
 
 
 def parity(x, y, z):
-    return (y % 2) * 4 + (z % 2) * 2 + x % 2
+    return (1 - y % 2) * 4 + (z % 2) * 2 + x % 2
 
 
 def cube_groups():
@@ -69,7 +69,7 @@
         for core in range(2):
             to_x = (x & 4) | (core << 1) | ((x >> 1) & 1)
             to_y = (y & 6) | ((z >> 1) & 1)
-            to_z = (z & 5) | ((y & 1) << 1)
+            to_z = (z & 5) | ((1 - (y & 1)) << 1)
             pairs.append((device(x, y, z, core), device(to_x, to_y, to_z, x & 1)))
     return pairs
 
@@ -228,9 +228,9 @@
     return lax.dot_general(a, b, (contract, ((), ())), preferred_element_type=jnp.float32)
 
 
-def full_product(a, b, contract):
-    (ah, al), (bh, bl) = a, b
-    return product(ah, bh, contract) + (product(ah, bl, contract) + product(al, bh, contract))
+def symmetric_product(high, low, contract):
+    side = product(high, low, contract)
+    return product(high, high, contract) + (side + jnp.transpose(side))
 
 
 def rows_product(rows, b):
@@ -254,31 +254,33 @@
     width = g.shape[0]
     frobenius = jnp.sum(g * g) + 1e-06
     g_parts = parts_of(g)
-    normal = full_product(g_parts, g_parts, ((1,), (1,))) / frobenius
+    normal = symmetric_product(*g_parts, ((1,), (1,))) * (1.0 / frobenius)
     n_parts = parts_of(normal)
-    squared = full_product(n_parts, n_parts, ((1,), (0,)))
+    squared = symmetric_product(*n_parts, ((1,), (1,)))
     total = jnp.sum(jnp.sum(squared * squared, axis=0, keepdims=True), axis=1, keepdims=True)
     bound = jnp.sqrt(jnp.sqrt(total))
     scale = frobenius * bound
-    m = normal / bound
-    m2 = squared / (bound * bound)
-    power[...] = m
-    square[...] = m2
+    to_m = 1.0 / bound
+    to_m2 = to_m * to_m
+    power[...] = normal
+    square[...] = squared
     diagonal = lax.broadcasted_iota(jnp.int32, (width, width), 0) == lax.broadcasted_iota(
         jnp.int32, (width, width), 1
     )
-    f2 = (jnp.where(diagonal, 25.0, 0.0) - 10.0 * m + m2) / 16.0
-    m_parts, f_parts = parts_of(m), parts_of(f2)
-    m_rows = power[pl.ds(first_row, 8), :]
-    m2_rows = square[pl.ds(first_row, 8), :]
+    f2 = jnp.where(diagonal, 25.0 / 16.0, 0.0) + (
+        normal * (to_m * (-10.0 / 16.0)) + squared * (to_m2 / 16.0)
+    )
+    f_parts = parts_of(f2)
+    m_rows = power[pl.ds(first_row, 8), :] * to_m
+    m2_rows = square[pl.ds(first_row, 8), :] * to_m2
     basis = lax.broadcasted_iota(jnp.int32, (8, width), 1) == first_row + lax.broadcasted_iota(
         jnp.int32, (8, width), 0
     )
     f_rows = (jnp.where(basis, 5.0, 0.0) - m_rows) / 4.0
     fm_rows = (5.0 * m_rows - m2_rows) / 4.0
     root = (5.0 * f_rows - rows_product(rows_product(fm_rows, f_parts), f_parts)) / 4.0
-    m_root = rows_product(root, m_parts)
-    m2_root = rows_product(m_root, m_parts)
+    m_root = rows_product(root, n_parts) * to_m
+    m2_root = rows_product(m_root, n_parts) * to_m
     f_rows = (5.0 * root - m_root) / 4.0
     fm_rows = (5.0 * m_root - m2_root) / 4.0
     root = (5.0 * f_rows - rows_product(rows_product(fm_rows, f_parts), f_parts)) / 4.0

time: 153 us -> 152 us (level)
  waiting for transfers between devices: 33.5 us -> 30.2 us
  blocking collectives: 51.6 us -> 53.6 us
  starting transfers between devices: 45.8 us -> 47.6 us
    all_to_all x1, blocking collectives: 28.6 us -> 31.5 us  [shards(): exchange(share(kept, arrived), AXES, axis_index_groups=stride_groups(False))]
    all_to_all x1, waiting for transfers between devices: 21 us -> 18.6 us  [shards(): tokens = exchange(message, AXES, axis_index_groups=cube_groups())]
where the time goes in v7:
time: 152 us; the launch traced here: 150 us
  blocking collectives  53.6 us (35%)
  starting transfers between devices  47.6 us (31%)
  waiting for transfers between devices  30.2 us (20%)
  Pallas kernels  14.3 us (9%)
  local copies, waits for them, and re-layouts  2.8 us (2%)
    all_to_all x1, blocking collectives, shards(): exchange(share(kept, arrived), AXES, axis_index_groups=stride_groups(False))  31.5 us
    all_to_all x1, starting transfers between devices, shards(): tokens = exchange(message, AXES, axis_index_groups=cube_groups())  23.7 us
    all_to_all x1, blocking collectives, shards(): own = exchange(total(terms), AXES, axis_index_groups=stride_groups(True))  22.2 us
    all_to_all x1, waiting for transfers between devices, shards(): tokens = exchange(message, AXES, axis_index_groups=cube_groups())  18.6 us
    all_to_all x1, starting transfers between devices, shards(): directions = exchange(jnp.broadcast_to(home[None], (16, 8, 512)), 'grp')  7.11 us
    all_to_all x1, waiting for transfers between devices, shards(): directions = exchange(jnp.broadcast_to(home[None], (16, 8, 512)), 'grp')  6.91 us
    all_to_all x1, starting transfers between devices, shards(): got = exchange(slots, 'grp')  6.37 us
    ppermute x1, starting transfers between devices, shards(): other = lax.ppermute(own, AXES, core_pairs())  5.41 us
  transfers between devices with their start and end apart: 6, of which 5 were waited for; matrix products, arithmetic and copies ran while one was open for 1% of the time, Pallas kernels for 6%

profile of v7, /device:TPU:1, one launch (start us, length us, event | category | flops | bytes accessed | tf_op | source)
XLA Modules:
  0.0 149.9 jit_solution(2733838397524507091)
XLA Ops:
  0.6 3.5 %shard_map.112 = bf16[8,3,128,512]{3,2,1,0:T(8,128)(2,1)} custom-call(s32[16]{0:T(128)} %order.1, bf16[128,8192]{1,0:T(8,128)(2,1)} %grads.1, bf16[128,512]{1,0:T(8,128)(2,1)} %features.1), custom_call_target="tpu_custom_call" | custom-call | tf_op jit(solution)/shard_map/pallas_call | solution.py:87
  4.1 23.7 %all-to-all-start = ((bf16[8,3,128,512]{3,2,1,0:T(8,128)(2,1)}), bf16[8,3,128,512]{3,2,1,0:T(8,128)(2,1)S(1)}, u32[]{:S(2)}, u32[]{:S(2)}) async-start(bf16[8,3,128,512]{3,2,1,0:T(8,128)(2,1)} %shard_map.112), calls=%async_computation | async-start | bytes 6291456 | tf_op jit(solution)/shard_map/all_to_all | solution.py:353
  28.4 0.7 copy.12.rows
  29.1 0.7 copy.13.owner_col
  29.9 1.8 %shard_map.113 = bf16[16,32,128]{2,1,0:T(8,128)(2,1)} custom-call(s32[1]{0:T(128)S(6)} %copy.15.live, s32[128,1]{1,0:T(8,128)} %copy.12.rows, s32[128,1]{1,0:T(8,128)} %copy.13.owner_col, s32[1,128]{1,0:T(1,128)} %bitcast.8, bf16[128,128]{1,0:T(8,128)(2,1)} %deltas.1), custom_call_target="tpu_custom_call" | custom-call | tf_op jit(solution)/shard_map/pallas_call | solution.py:116
  31.7 18.6 %all-to-all-done.tokens = bf16[8,3,128,512]{3,2,1,0:T(8,128)(2,1)S(1)} async-done(((bf16[8,3,128,512]{3,2,1,0:T(8,128)(2,1)}), bf16[8,3,128,512]{3,2,1,0:T(8,128)(2,1)S(1)}, u32[]{:S(2)}, u32[]{:S(2)}) %all-to-all-start) | async-done | bytes 3145760 | tf_op jit(solution)/shard_map/all_to_all | solution.py:353
  50.3 0.7 shard_map.116
  51.0 1.9 %collective-permute-start = (f32[2,2,128,512]{3,2,1,0:T(8,128)S(1)}, f32[2,2,128,512]{3,2,1,0:T(8,128)S(1)}, u32[]{:S(2)}, u32[]{:S(2)}) collective-permute-start(f32[2,2,128,512]{3,2,1,0:T(8,128)S(1)} %shard_map.116), channel_id=1, source_target_pairs={{0,64},{64,0},{128,192},{192,128},{256,320},{320,256},{384,448},{4... | collective-permute-start | bytes 3145736 | tf_op jit(solution)/shard_map/ppermute | solution.py:357
  53.0 0.7 shard_map.115.kept
  53.7 1.9 %collective-permute-done.arrived = f32[2,2,128,512]{3,2,1,0:T(8,128)S(1)} collective-permute-done((f32[2,2,128,512]{3,2,1,0:T(8,128)S(1)}, f32[2,2,128,512]{3,2,1,0:T(8,128)S(1)}, u32[]{:S(2)}, u32[]{:S(2)}) %collective-permute-start) | collective-permute-done | bytes 1048608 | tf_op jit(solution)/shard_map/ppermute | solution.py:357
  55.6 0.5 shard_map.117
  56.1 31.5 %all_to_all.25.terms = s16[64,40,128]{2,1,0:T(8,128)(2,1)S(1)} all-to-all(s16[64,40,128]{2,1,0:T(8,128)(2,1)S(1)} %shard_map.117), channel_id=1, replica_groups={{0,256,2,258,4,260,6,262,16,272,18,274,20,276,22,278,32,288,34,290,36,2..., dimensions={0} | all-to-all | bytes 1310720 | tf_op jit(solution)/shard_map/all_to_all | solution.py:359
  88.0 22.2 %all_to_all.26.own = s16[32,40,128]{2,1,0:T(8,128)(2,1)S(1)} all-to-all(s16[32,40,128]{2,1,0:T(8,128)(2,1)S(1)} %shard_map.118), channel_id=1, replica_groups={{0,256,2,258,4,260,6,262,16,272,18,274,20,276,22,278,32,288,34,290,36,2..., dimensions={0} | all-to-all | bytes 655360 | tf_op jit(solution)/shard_map/all_to_all | solution.py:360
  110.2 5.4 %collective-permute-start.1 = (s16[32,40,128]{2,1,0:T(8,128)(2,1)S(1)}, s16[32,40,128]{2,1,0:T(8,128)(2,1)S(1)}, u32[]{:S(2)}, u32[]{:S(2)}) collective-permute-start(s16[32,40,128]{2,1,0:T(8,128)(2,1)S(1)} %all_to_all.26.own), channel_id=1, source_target_pairs={{0,64},{64,0},{128,192},{192,128},{256,320},{320,256},{384,448},{4... | collective-permute-start | bytes 983048 | tf_op jit(solution)/shard_map/ppermute | solution.py:362
  115.6 6.4 %all-to-all-start.1 = ((bf16[16,32,128]{2,1,0:T(8,128)(2,1)}), bf16[16,32,128]{2,1,0:T(8,128)(2,1)S(1)}, u32[]{:S(2)}, u32[]{:S(2)}) async-start(bf16[16,32,128]{2,1,0:T(8,128)(2,1)} %shard_map.113), calls=%async_computation.1 | async-start | bytes 262144 | tf_op jit(solution)/shard_map/all_to_all | solution.py:361
  122.1 4.3 %shard_map.119 = bf16[8,512]{1,0:T(8,128)(2,1)S(1)} custom-call(s32[2]{0:T(128)S(1)} %pad_add_fusion.place, s16[32,40,128]{2,1,0:T(8,128)(2,1)S(1)} %all_to_all.26.own, s16[32,40,128]{2,1,0:T(8,128)(2,1)S(1)} %collective-permute-done.1.other), custom_call_target="tpu_custom_call" | custom-call | tf_op jit(solution)/shard_map/pallas_call | solution.py:295
  126.4 3.1 %collective-permute-start.2 = (bf16[8,512]{1,0:T(8,128)(2,1)S(1)}, bf16[8,512]{1,0:T(8,128)(2,1)S(1)}, u32[]{:S(2)}, u32[]{:S(2)}) collective-permute-start(bf16[8,512]{1,0:T(8,128)(2,1)S(1)} %shard_map.119), channel_id=1, source_target_pairs={{0,256},{64,272},{128,384},{192,400},{256,257},{320,273},{384,385}... | collective-permute-start | bytes 24584 | tf_op jit(solution)/shard_map/ppermute | solution.py:366
  129.5 1.6 %all-to-all-done.1.got = bf16[16,32,128]{2,1,0:T(8,128)(2,1)S(1)} async-done(((bf16[16,32,128]{2,1,0:T(8,128)(2,1)}), bf16[16,32,128]{2,1,0:T(8,128)(2,1)S(1)}, u32[]{:S(2)}, u32[]{:S(2)}) %all-to-all-start.1) | async-done | bytes 131104 | tf_op jit(solution)/shard_map/all_to_all | solution.py:361
  131.2 1.1 collective-permute-done.2
  132.3 0.7 broadcast_in_dim.2
  132.9 7.1 %all-to-all-start.4 = ((bf16[16,8,512]{2,1,0:T(8,128)(2,1)}), bf16[16,8,512]{2,1,0:T(8,128)(2,1)S(1)}, u32[]{:S(2)}, u32[]{:S(2)}) async-start(bf16[16,8,512]{2,1,0:T(8,128)(2,1)} %broadcast_in_dim.2), calls=%async_computation.4 | async-start | bytes 262144 | tf_op jit(solution)/shard_map/all_to_all | solution.py:369
  140.1 2.3 %shard_map.114 = (f32[512,128]{1,0:T(8,128)}, f32[1,512]{1,0:T(1,128)}) custom-call(bf16[16,32,128]{2,1,0:T(8,128)(2,1)} %copy-done, f32[512,128]{1,0:T(8,128)} %table.1, f32[1,512]{1,0:T(1,128)} %bitcast.7), custom_call_target="tpu_custom_call" | custom-call | tf_op jit(solution)/shard_map/pallas_call | solution.py:323
  142.3 6.9 %all-to-all-done.4 = bf16[16,8,512]{2,1,0:T(8,128)(2,1)S(1)} async-done(((bf16[16,8,512]{2,1,0:T(8,128)(2,1)}), bf16[16,8,512]{2,1,0:T(8,128)(2,1)S(1)}, u32[]{:S(2)}, u32[]{:S(2)}) %all-to-all-start.4) | async-done | bytes 131104 | tf_op jit(solution)/shard_map/all_to_all | solution.py:369
  149.2 0.7 copy.16
  (9 shorter events, 0.6 us)
Async XLA Ops:
  4.1 24.3 %copy-start.2 = (s32[128]{0:T(128)S(1)}, s32[128]{0:T(128)}, u32[]{:S(2)}) copy-start(s32[128]{0:T(128)} %param.14) | copy-start | bytes 1540
  4.1 25.1 %copy-start.1 = (s32[128,1]{0,1:T(1,128)S(1)}, s32[128,1]{0,1:T(1,128)}, u32[]{:S(2)}) copy-start(s32[128,1]{0,1:T(1,128)} %param.15) | copy-start | bytes 1540
  4.1 46.2 %all-to-all-start = ((bf16[8,3,128,512]{3,2,1,0:T(8,128)(2,1)}), bf16[8,3,128,512]{3,2,1,0:T(8,128)(2,1)S(1)}, u32[]{:S(2)}, u32[]{:S(2)}) async-start(bf16[8,3,128,512]{3,2,1,0:T(8,128)(2,1)} %shard_map.112), calls=%async_computation | async-start | bytes 6291456 | tf_op jit(solution)/shard_map/all_to_all | solution.py:353
  51.0 4.6 %collective-permute-start = (f32[2,2,128,512]{3,2,1,0:T(8,128)S(1)}, f32[2,2,128,512]{3,2,1,0:T(8,128)S(1)}, u32[]{:S(2)}, u32[]{:S(2)}) collective-permute-start(f32[2,2,128,512]{3,2,1,0:T(8,128)S(1)} %shard_map.116), channel_id=1, source_target_pairs={{0,64},{64,0},{128,192},{192,128},{256,320},{320,256},{384,448},{4... | collective-permute-start | bytes 3145736 | tf_op jit(solution)/shard_map/ppermute | solution.py:357
  110.2 11.9 %collective-permute-start.1 = (s16[32,40,128]{2,1,0:T(8,128)(2,1)S(1)}, s16[32,40,128]{2,1,0:T(8,128)(2,1)S(1)}, u32[]{:S(2)}, u32[]{:S(2)}) collective-permute-start(s16[32,40,128]{2,1,0:T(8,128)(2,1)S(1)} %all_to_all.26.own), channel_id=1, source_target_pairs={{0,64},{64,0},{128,192},{192,128},{256,320},{320,256},{384,448},{4... | collective-permute-start | bytes 983048 | tf_op jit(solution)/shard_map/ppermute | solution.py:362
  115.6 15.5 %all-to-all-start.1 = ((bf16[16,32,128]{2,1,0:T(8,128)(2,1)}), bf16[16,32,128]{2,1,0:T(8,128)(2,1)S(1)}, u32[]{:S(2)}, u32[]{:S(2)}) async-start(bf16[16,32,128]{2,1,0:T(8,128)(2,1)} %shard_map.113), calls=%async_computation.1 | async-start | bytes 262144 | tf_op jit(solution)/shard_map/all_to_all | solution.py:361
  126.4 5.9 %collective-permute-start.2 = (bf16[8,512]{1,0:T(8,128)(2,1)S(1)}, bf16[8,512]{1,0:T(8,128)(2,1)S(1)}, u32[]{:S(2)}, u32[]{:S(2)}) collective-permute-start(bf16[8,512]{1,0:T(8,128)(2,1)S(1)} %shard_map.119), channel_id=1, source_target_pairs={{0,256},{64,272},{128,384},{192,400},{256,257},{320,273},{384,385}... | collective-permute-start | bytes 24584 | tf_op jit(solution)/shard_map/ppermute | solution.py:366
  131.2 8.9 %copy-start = (bf16[16,32,128]{2,1,0:T(8,128)(2,1)}, bf16[16,32,128]{2,1,0:T(8,128)(2,1)S(1)}, u32[]{:S(2)}) copy-start(bf16[16,32,128]{2,1,0:T(8,128)(2,1)S(1)} %all-to-all-done.1.got) | copy-start | bytes 393220
  132.9 16.3 %all-to-all-start.4 = ((bf16[16,8,512]{2,1,0:T(8,128)(2,1)}), bf16[16,8,512]{2,1,0:T(8,128)(2,1)S(1)}, u32[]{:S(2)}, u32[]{:S(2)}) async-start(bf16[16,8,512]{2,1,0:T(8,128)(2,1)} %broadcast_in_dim.2), calls=%async_computation.4 | async-start | bytes 262144 | tf_op jit(solution)/shard_map/all_to_all | solution.py:369

commit v8 on v7

--- a/solution.py
+++ b/solution.py
@@ -254,7 +254,8 @@
     width = g.shape[0]
     frobenius = jnp.sum(g * g) + 1e-06
     g_parts = parts_of(g)
-    normal = symmetric_product(*g_parts, ((1,), (1,))) * (1.0 / frobenius)
+    inverse = 1.0 / jnp.sqrt(frobenius)
+    normal = symmetric_product(*g_parts, ((1,), (1,))) * inverse * inverse
     n_parts = parts_of(normal)
     squared = symmetric_product(*n_parts, ((1,), (1,)))
     total = jnp.sum(jnp.sum(squared * squared, axis=0, keepdims=True), axis=1, keepdims=True)

time: 152 us -> 152 us (level)
  no operation moved by 1% of the time
where the time goes in v8:
time: 152 us; the launch traced here: 150 us
  blocking collectives  53.6 us (35%)
  starting transfers between devices  47.6 us (31%)
  waiting for transfers between devices  30.2 us (20%)
  Pallas kernels  14.3 us (9%)
  local copies, waits for them, and re-layouts  2.8 us (2%)
    all_to_all x1, blocking collectives, shards(): exchange(share(kept, arrived), AXES, axis_index_groups=stride_groups(False))  31.5 us
    all_to_all x1, starting transfers between devices, shards(): tokens = exchange(message, AXES, axis_index_groups=cube_groups())  23.7 us
    all_to_all x1, blocking collectives, shards(): own = exchange(total(terms), AXES, axis_index_groups=stride_groups(True))  22.2 us
    all_to_all x1, waiting for transfers between devices, shards(): tokens = exchange(message, AXES, axis_index_groups=cube_groups())  18.6 us
    all_to_all x1, starting transfers between devices, shards(): directions = exchange(jnp.broadcast_to(home[None], (16, 8, 512)), 'grp')  7.07 us
    all_to_all x1, waiting for transfers between devices, shards(): directions = exchange(jnp.broadcast_to(home[None], (16, 8, 512)), 'grp')  6.91 us
    all_to_all x1, starting transfers between devices, shards(): got = exchange(slots, 'grp')  6.36 us
    ppermute x1, starting transfers between devices, shards(): other = lax.ppermute(own, AXES, core_pairs())  5.4 us
  transfers between devices with their start and end apart: 6, of which 5 were waited for; matrix products, arithmetic and copies ran while one was open for 1% of the time, Pallas kernels for 6%

profile of v8, /device:TPU:1, one launch (start us, length us, event | category | flops | bytes accessed | tf_op | source)
XLA Modules:
  0.0 149.9 jit_solution(17035253594070177496)
XLA Ops:
  0.6 3.4 %shard_map.112 = bf16[8,3,128,512]{3,2,1,0:T(8,128)(2,1)} custom-call(s32[16]{0:T(128)} %order.1, bf16[128,8192]{1,0:T(8,128)(2,1)} %grads.1, bf16[128,512]{1,0:T(8,128)(2,1)} %features.1), custom_call_target="tpu_custom_call" | custom-call | tf_op jit(solution)/shard_map/pallas_call | solution.py:87
  4.1 23.7 %all-to-all-start = ((bf16[8,3,128,512]{3,2,1,0:T(8,128)(2,1)}), bf16[8,3,128,512]{3,2,1,0:T(8,128)(2,1)S(1)}, u32[]{:S(2)}, u32[]{:S(2)}) async-start(bf16[8,3,128,512]{3,2,1,0:T(8,128)(2,1)} %shard_map.112), calls=%async_computation | async-start | bytes 6291456 | tf_op jit(solution)/shard_map/all_to_all | solution.py:354
  28.4 0.7 copy.12.rows
  29.1 0.7 copy.13.owner_col
  29.9 1.8 %shard_map.113 = bf16[16,32,128]{2,1,0:T(8,128)(2,1)} custom-call(s32[1]{0:T(128)S(6)} %copy.15.live, s32[128,1]{1,0:T(8,128)} %copy.12.rows, s32[128,1]{1,0:T(8,128)} %copy.13.owner_col, s32[1,128]{1,0:T(1,128)} %bitcast.8, bf16[128,128]{1,0:T(8,128)(2,1)} %deltas.1), custom_call_target="tpu_custom_call" | custom-call | tf_op jit(solution)/shard_map/pallas_call | solution.py:116
  31.7 18.6 %all-to-all-done.tokens = bf16[8,3,128,512]{3,2,1,0:T(8,128)(2,1)S(1)} async-done(((bf16[8,3,128,512]{3,2,1,0:T(8,128)(2,1)}), bf16[8,3,128,512]{3,2,1,0:T(8,128)(2,1)S(1)}, u32[]{:S(2)}, u32[]{:S(2)}) %all-to-all-start) | async-done | bytes 3145760 | tf_op jit(solution)/shard_map/all_to_all | solution.py:354
  50.3 0.7 shard_map.116
  51.0 1.9 %collective-permute-start = (f32[2,2,128,512]{3,2,1,0:T(8,128)S(1)}, f32[2,2,128,512]{3,2,1,0:T(8,128)S(1)}, u32[]{:S(2)}, u32[]{:S(2)}) collective-permute-start(f32[2,2,128,512]{3,2,1,0:T(8,128)S(1)} %shard_map.116), channel_id=1, source_target_pairs={{0,64},{64,0},{128,192},{192,128},{256,320},{320,256},{384,448},{4... | collective-permute-start | bytes 3145736 | tf_op jit(solution)/shard_map/ppermute | solution.py:358
  52.9 0.7 shard_map.115.kept
  53.7 1.9 %collective-permute-done.arrived = f32[2,2,128,512]{3,2,1,0:T(8,128)S(1)} collective-permute-done((f32[2,2,128,512]{3,2,1,0:T(8,128)S(1)}, f32[2,2,128,512]{3,2,1,0:T(8,128)S(1)}, u32[]{:S(2)}, u32[]{:S(2)}) %collective-permute-start) | collective-permute-done | bytes 1048608 | tf_op jit(solution)/shard_map/ppermute | solution.py:358
  55.6 0.5 shard_map.117
  56.1 31.5 %all_to_all.25.terms = s16[64,40,128]{2,1,0:T(8,128)(2,1)S(1)} all-to-all(s16[64,40,128]{2,1,0:T(8,128)(2,1)S(1)} %shard_map.117), channel_id=1, replica_groups={{0,256,2,258,4,260,6,262,16,272,18,274,20,276,22,278,32,288,34,290,36,2..., dimensions={0} | all-to-all | bytes 1310720 | tf_op jit(solution)/shard_map/all_to_all | solution.py:360
  88.0 22.2 %all_to_all.26.own = s16[32,40,128]{2,1,0:T(8,128)(2,1)S(1)} all-to-all(s16[32,40,128]{2,1,0:T(8,128)(2,1)S(1)} %shard_map.118), channel_id=1, replica_groups={{0,256,2,258,4,260,6,262,16,272,18,274,20,276,22,278,32,288,34,290,36,2..., dimensions={0} | all-to-all | bytes 655360 | tf_op jit(solution)/shard_map/all_to_all | solution.py:361
  110.2 5.4 %collective-permute-start.1 = (s16[32,40,128]{2,1,0:T(8,128)(2,1)S(1)}, s16[32,40,128]{2,1,0:T(8,128)(2,1)S(1)}, u32[]{:S(2)}, u32[]{:S(2)}) collective-permute-start(s16[32,40,128]{2,1,0:T(8,128)(2,1)S(1)} %all_to_all.26.own), channel_id=1, source_target_pairs={{0,64},{64,0},{128,192},{192,128},{256,320},{320,256},{384,448},{4... | collective-permute-start | bytes 983048 | tf_op jit(solution)/shard_map/ppermute | solution.py:363
  115.6 6.4 %all-to-all-start.1 = ((bf16[16,32,128]{2,1,0:T(8,128)(2,1)}), bf16[16,32,128]{2,1,0:T(8,128)(2,1)S(1)}, u32[]{:S(2)}, u32[]{:S(2)}) async-start(bf16[16,32,128]{2,1,0:T(8,128)(2,1)} %shard_map.113), calls=%async_computation.1 | async-start | bytes 262144 | tf_op jit(solution)/shard_map/all_to_all | solution.py:362
  122.1 4.3 %shard_map.119 = bf16[8,512]{1,0:T(8,128)(2,1)S(1)} custom-call(s32[2]{0:T(128)S(1)} %pad_add_fusion.place, s16[32,40,128]{2,1,0:T(8,128)(2,1)S(1)} %all_to_all.26.own, s16[32,40,128]{2,1,0:T(8,128)(2,1)S(1)} %collective-permute-done.1.other), custom_call_target="tpu_custom_call" | custom-call | tf_op jit(solution)/shard_map/pallas_call | solution.py:296
  126.4 3.1 %collective-permute-start.2 = (bf16[8,512]{1,0:T(8,128)(2,1)S(1)}, bf16[8,512]{1,0:T(8,128)(2,1)S(1)}, u32[]{:S(2)}, u32[]{:S(2)}) collective-permute-start(bf16[8,512]{1,0:T(8,128)(2,1)S(1)} %shard_map.119), channel_id=1, source_target_pairs={{0,256},{64,272},{128,384},{192,400},{256,257},{320,273},{384,385}... | collective-permute-start | bytes 24584 | tf_op jit(solution)/shard_map/ppermute | solution.py:367
  129.6 1.6 %all-to-all-done.1.got = bf16[16,32,128]{2,1,0:T(8,128)(2,1)S(1)} async-done(((bf16[16,32,128]{2,1,0:T(8,128)(2,1)}), bf16[16,32,128]{2,1,0:T(8,128)(2,1)S(1)}, u32[]{:S(2)}, u32[]{:S(2)}) %all-to-all-start.1) | async-done | bytes 131104 | tf_op jit(solution)/shard_map/all_to_all | solution.py:362
  131.2 1.2 collective-permute-done.2
  132.3 0.7 broadcast_in_dim.2
  133.0 7.1 %all-to-all-start.4 = ((bf16[16,8,512]{2,1,0:T(8,128)(2,1)}), bf16[16,8,512]{2,1,0:T(8,128)(2,1)S(1)}, u32[]{:S(2)}, u32[]{:S(2)}) async-start(bf16[16,8,512]{2,1,0:T(8,128)(2,1)} %broadcast_in_dim.2), calls=%async_computation.4 | async-start | bytes 262144 | tf_op jit(solution)/shard_map/all_to_all | solution.py:370
  140.1 2.2 %shard_map.114 = (f32[512,128]{1,0:T(8,128)}, f32[1,512]{1,0:T(1,128)}) custom-call(bf16[16,32,128]{2,1,0:T(8,128)(2,1)} %copy-done, f32[512,128]{1,0:T(8,128)} %table.1, f32[1,512]{1,0:T(1,128)} %bitcast.7), custom_call_target="tpu_custom_call" | custom-call | tf_op jit(solution)/shard_map/pallas_call | solution.py:324
  142.3 6.9 %all-to-all-done.4 = bf16[16,8,512]{2,1,0:T(8,128)(2,1)S(1)} async-done(((bf16[16,8,512]{2,1,0:T(8,128)(2,1)}), bf16[16,8,512]{2,1,0:T(8,128)(2,1)S(1)}, u32[]{:S(2)}, u32[]{:S(2)}) %all-to-all-start.4) | async-done | bytes 131104 | tf_op jit(solution)/shard_map/all_to_all | solution.py:370
  149.2 0.7 copy.16
  (9 shorter events, 0.6 us)
Async XLA Ops:
  4.1 24.3 %copy-start.2 = (s32[128]{0:T(128)S(1)}, s32[128]{0:T(128)}, u32[]{:S(2)}) copy-start(s32[128]{0:T(128)} %param.14) | copy-start | bytes 1540
  4.1 25.1 %copy-start.1 = (s32[128,1]{0,1:T(1,128)S(1)}, s32[128,1]{0,1:T(1,128)}, u32[]{:S(2)}) copy-start(s32[128,1]{0,1:T(1,128)} %param.15) | copy-start | bytes 1540
  4.1 46.2 %all-to-all-start = ((bf16[8,3,128,512]{3,2,1,0:T(8,128)(2,1)}), bf16[8,3,128,512]{3,2,1,0:T(8,128)(2,1)S(1)}, u32[]{:S(2)}, u32[]{:S(2)}) async-start(bf16[8,3,128,512]{3,2,1,0:T(8,128)(2,1)} %shard_map.112), calls=%async_computation | async-start | bytes 6291456 | tf_op jit(solution)/shard_map/all_to_all | solution.py:354
  51.0 4.6 %collective-permute-start = (f32[2,2,128,512]{3,2,1,0:T(8,128)S(1)}, f32[2,2,128,512]{3,2,1,0:T(8,128)S(1)}, u32[]{:S(2)}, u32[]{:S(2)}) collective-permute-start(f32[2,2,128,512]{3,2,1,0:T(8,128)S(1)} %shard_map.116), channel_id=1, source_target_pairs={{0,64},{64,0},{128,192},{192,128},{256,320},{320,256},{384,448},{4... | collective-permute-start | bytes 3145736 | tf_op jit(solution)/shard_map/ppermute | solution.py:358
  110.2 11.9 %collective-permute-start.1 = (s16[32,40,128]{2,1,0:T(8,128)(2,1)S(1)}, s16[32,40,128]{2,1,0:T(8,128)(2,1)S(1)}, u32[]{:S(2)}, u32[]{:S(2)}) collective-permute-start(s16[32,40,128]{2,1,0:T(8,128)(2,1)S(1)} %all_to_all.26.own), channel_id=1, source_target_pairs={{0,64},{64,0},{128,192},{192,128},{256,320},{320,256},{384,448},{4... | collective-permute-start | bytes 983048 | tf_op jit(solution)/shard_map/ppermute | solution.py:363
  115.6 15.5 %all-to-all-start.1 = ((bf16[16,32,128]{2,1,0:T(8,128)(2,1)}), bf16[16,32,128]{2,1,0:T(8,128)(2,1)S(1)}, u32[]{:S(2)}, u32[]{:S(2)}) async-start(bf16[16,32,128]{2,1,0:T(8,128)(2,1)} %shard_map.113), calls=%async_computation.1 | async-start | bytes 262144 | tf_op jit(solution)/shard_map/all_to_all | solution.py:362
  126.4 5.9 %collective-permute-start.2 = (bf16[8,512]{1,0:T(8,128)(2,1)S(1)}, bf16[8,512]{1,0:T(8,128)(2,1)S(1)}, u32[]{:S(2)}, u32[]{:S(2)}) collective-permute-start(bf16[8,512]{1,0:T(8,128)(2,1)S(1)} %shard_map.119), channel_id=1, source_target_pairs={{0,256},{64,272},{128,384},{192,400},{256,257},{320,273},{384,385}... | collective-permute-start | bytes 24584 | tf_op jit(solution)/shard_map/ppermute | solution.py:367
  131.2 8.9 %copy-start = (bf16[16,32,128]{2,1,0:T(8,128)(2,1)}, bf16[16,32,128]{2,1,0:T(8,128)(2,1)S(1)}, u32[]{:S(2)}) copy-start(bf16[16,32,128]{2,1,0:T(8,128)(2,1)S(1)} %all-to-all-done.1.got) | copy-start | bytes 393220
  133.0 16.2 %all-to-all-start.4 = ((bf16[16,8,512]{2,1,0:T(8,128)(2,1)}), bf16[16,8,512]{2,1,0:T(8,128)(2,1)S(1)}, u32[]{:S(2)}, u32[]{:S(2)}) async-start(bf16[16,8,512]{2,1,0:T(8,128)(2,1)} %broadcast_in_dim.2), calls=%async_computation.4 | async-start | bytes 262144 | tf_op jit(solution)/shard_map/all_to_all | solution.py:370

commit v9 on v8

--- a/solution.py
+++ b/solution.py
@@ -367,6 +367,7 @@
     home = lax.ppermute(rows, AXES, home_pairs())
 
     new_table, new_accum = update_rows(got, emb_table, row_accum)
+    home, new_accum = lax.optimization_barrier((home, new_accum))
     directions = exchange(jnp.broadcast_to(home[None], (16, 8, 512)), "grp")
     return (new_table, new_accum.reshape(-1), directions)
 

time: 152 us -> 151 us (level)
  blocking collectives: 53.6 us -> 67.6 us
  waiting for transfers between devices: 30.2 us -> 21.1 us
  starting transfers between devices: 47.6 us -> 41.7 us
    all_to_all x0 -> x1, blocking collectives: none -> 14.2 us  [shards(): directions = exchange(jnp.broadcast_to(home[None], (16, 8, 512)), 'grp')]
    all_to_all x1 -> x0, starting transfers between devices: 7.07 us -> none  [shards(): directions = exchange(jnp.broadcast_to(home[None], (16, 8, 512)), 'grp')]
    all_to_all x1 -> x0, waiting for transfers between devices: 6.91 us -> none  [shards(): directions = exchange(jnp.broadcast_to(home[None], (16, 8, 512)), 'grp')]
  transfers between devices with their start and end apart: 6 -> 5, of which waited for: 5 -> 3; matrix products, arithmetic and copies ran while one was open for 1% -> 1% of each run, Pallas kernels for 6% -> 6%
where the time goes in v9:
time: 151 us; the launch traced here: 149 us
  blocking collectives  67.6 us (45%)
  starting transfers between devices  41.7 us (28%)
  waiting for transfers between devices  21.1 us (14%)
  Pallas kernels  14.3 us (9%)
  local copies, waits for them, and re-layouts  2.79 us (2%)
    all_to_all x1, blocking collectives, shards(): exchange(share(kept, arrived), AXES, axis_index_groups=stride_groups(False))  31.5 us
    all_to_all x1, starting transfers between devices, shards(): tokens = exchange(message, AXES, axis_index_groups=cube_groups())  23.7 us
    all_to_all x1, blocking collectives, shards(): own = exchange(total(terms), AXES, axis_index_groups=stride_groups(True))  21.9 us
    all_to_all x1, waiting for transfers between devices, shards(): tokens = exchange(message, AXES, axis_index_groups=cube_groups())  18.6 us
    all_to_all x1, blocking collectives, shards(): directions = exchange(jnp.broadcast_to(home[None], (16, 8, 512)), 'grp')  14.2 us
    all_to_all x1, starting transfers between devices, shards(): got = exchange(slots, 'grp')  6.37 us
    ppermute x1, starting transfers between devices, shards(): other = lax.ppermute(own, AXES, core_pairs())  5.69 us
    pallas_call x1, Pallas kernels, direction_rows(): pl.pallas_call(direction_kernel, out_shape=jax.ShapeDtypeStruct((8, 512),...  4.34 us
  transfers between devices with their start and end apart: 5, of which 3 were waited for; matrix products, arithmetic and copies ran while one was open for 1% of the time, Pallas kernels for 6%

profile of v9, /device:TPU:1, one launch (start us, length us, event | category | flops | bytes accessed | tf_op | source)
XLA Modules:
  0.0 149.0 jit_solution(7159745802898411723)
XLA Ops:
  0.6 3.5 %shard_map.112 = bf16[8,3,128,512]{3,2,1,0:T(8,128)(2,1)} custom-call(s32[16]{0:T(128)} %order.1, bf16[128,8192]{1,0:T(8,128)(2,1)} %grads.1, bf16[128,512]{1,0:T(8,128)(2,1)} %features.1), custom_call_target="tpu_custom_call" | custom-call | tf_op jit(solution)/shard_map/pallas_call | solution.py:87
  4.1 23.7 %all-to-all-start = ((bf16[8,3,128,512]{3,2,1,0:T(8,128)(2,1)}), bf16[8,3,128,512]{3,2,1,0:T(8,128)(2,1)S(1)}, u32[]{:S(2)}, u32[]{:S(2)}) async-start(bf16[8,3,128,512]{3,2,1,0:T(8,128)(2,1)} %shard_map.112), calls=%async_computation | async-start | bytes 6291456 | tf_op jit(solution)/shard_map/all_to_all | solution.py:354
  28.4 0.7 copy.12.rows
  29.1 0.7 copy.13.owner_col
  29.9 1.8 %shard_map.113 = bf16[16,32,128]{2,1,0:T(8,128)(2,1)} custom-call(s32[1]{0:T(128)S(6)} %copy.15.live, s32[128,1]{1,0:T(8,128)} %copy.12.rows, s32[128,1]{1,0:T(8,128)} %copy.13.owner_col, s32[1,128]{1,0:T(1,128)} %bitcast.8, bf16[128,128]{1,0:T(8,128)(2,1)} %deltas.1), custom_call_target="tpu_custom_call" | custom-call | tf_op jit(solution)/shard_map/pallas_call | solution.py:116
  31.7 18.6 %all-to-all-done.tokens = bf16[8,3,128,512]{3,2,1,0:T(8,128)(2,1)S(1)} async-done(((bf16[8,3,128,512]{3,2,1,0:T(8,128)(2,1)}), bf16[8,3,128,512]{3,2,1,0:T(8,128)(2,1)S(1)}, u32[]{:S(2)}, u32[]{:S(2)}) %all-to-all-start) | async-done | bytes 3145760 | tf_op jit(solution)/shard_map/all_to_all | solution.py:354
  50.3 0.7 shard_map.116
  51.0 1.9 %collective-permute-start = (f32[2,2,128,512]{3,2,1,0:T(8,128)S(1)}, f32[2,2,128,512]{3,2,1,0:T(8,128)S(1)}, u32[]{:S(2)}, u32[]{:S(2)}) collective-permute-start(f32[2,2,128,512]{3,2,1,0:T(8,128)S(1)} %shard_map.116), channel_id=1, source_target_pairs={{0,64},{64,0},{128,192},{192,128},{256,320},{320,256},{384,448},{4... | collective-permute-start | bytes 3145736 | tf_op jit(solution)/shard_map/ppermute | solution.py:358
  53.0 0.7 shard_map.115.kept
  53.7 1.9 %collective-permute-done.arrived = f32[2,2,128,512]{3,2,1,0:T(8,128)S(1)} collective-permute-done((f32[2,2,128,512]{3,2,1,0:T(8,128)S(1)}, f32[2,2,128,512]{3,2,1,0:T(8,128)S(1)}, u32[]{:S(2)}, u32[]{:S(2)}) %collective-permute-start) | collective-permute-done | bytes 1048608 | tf_op jit(solution)/shard_map/ppermute | solution.py:358
  55.6 0.5 shard_map.117
  56.1 31.5 %all_to_all.25.terms = s16[64,40,128]{2,1,0:T(8,128)(2,1)S(1)} all-to-all(s16[64,40,128]{2,1,0:T(8,128)(2,1)S(1)} %shard_map.117), channel_id=1, replica_groups={{0,256,2,258,4,260,6,262,16,272,18,274,20,276,22,278,32,288,34,290,36,2..., dimensions={0} | all-to-all | bytes 1310720 | tf_op jit(solution)/shard_map/all_to_all | solution.py:360
  87.6 0.5 shard_map.118
  88.1 21.9 %all_to_all.26.own = s16[32,40,128]{2,1,0:T(8,128)(2,1)S(1)} all-to-all(s16[32,40,128]{2,1,0:T(8,128)(2,1)S(1)} %shard_map.118), channel_id=1, replica_groups={{0,256,2,258,4,260,6,262,16,272,18,274,20,276,22,278,32,288,34,290,36,2..., dimensions={0} | all-to-all | bytes 655360 | tf_op jit(solution)/shard_map/all_to_all | solution.py:361
  110.0 5.7 %collective-permute-start.1 = (s16[32,40,128]{2,1,0:T(8,128)(2,1)S(1)}, s16[32,40,128]{2,1,0:T(8,128)(2,1)S(1)}, u32[]{:S(2)}, u32[]{:S(2)}) collective-permute-start(s16[32,40,128]{2,1,0:T(8,128)(2,1)S(1)} %all_to_all.26.own), channel_id=1, source_target_pairs={{0,64},{64,0},{128,192},{192,128},{256,320},{320,256},{384,448},{4... | collective-permute-start | bytes 983048 | tf_op jit(solution)/shard_map/ppermute | solution.py:363
  115.7 6.4 %all-to-all-start.1 = ((bf16[16,32,128]{2,1,0:T(8,128)(2,1)}), bf16[16,32,128]{2,1,0:T(8,128)(2,1)S(1)}, u32[]{:S(2)}, u32[]{:S(2)}) async-start(bf16[16,32,128]{2,1,0:T(8,128)(2,1)} %shard_map.113), calls=%async_computation.1 | async-start | bytes 262144 | tf_op jit(solution)/shard_map/all_to_all | solution.py:362
  122.0 0.1 pad_add_fusion.place
  122.1 4.3 %shard_map.119 = bf16[8,512]{1,0:T(8,128)(2,1)S(1)} custom-call(s32[2]{0:T(128)S(1)} %pad_add_fusion.place, s16[32,40,128]{2,1,0:T(8,128)(2,1)S(1)} %all_to_all.26.own, s16[32,40,128]{2,1,0:T(8,128)(2,1)S(1)} %collective-permute-done.1.other), custom_call_target="tpu_custom_call" | custom-call | tf_op jit(solution)/shard_map/pallas_call | solution.py:296
  126.4 4.1 %collective-permute-start.2 = (bf16[8,512]{1,0:T(8,128)(2,1)S(1)}, bf16[8,512]{1,0:T(8,128)(2,1)S(1)}, u32[]{:S(2)}, u32[]{:S(2)}) collective-permute-start(bf16[8,512]{1,0:T(8,128)(2,1)S(1)} %shard_map.119), channel_id=1, source_target_pairs={{0,256},{64,272},{128,384},{192,400},{256,257},{320,273},{384,385}... | collective-permute-start | bytes 24584 | tf_op jit(solution)/shard_map/ppermute | solution.py:367
  130.6 0.6 all-to-all-done.1.got
  131.2 0.7 copy-done
  131.8 2.2 %shard_map.114 = (f32[512,128]{1,0:T(8,128)}, f32[1,512]{1,0:T(1,128)}) custom-call(bf16[16,32,128]{2,1,0:T(8,128)(2,1)} %copy-done, f32[512,128]{1,0:T(8,128)} %table.1, f32[1,512]{1,0:T(1,128)} %bitcast.7), custom_call_target="tpu_custom_call" | custom-call | tf_op jit(solution)/shard_map/pallas_call | solution.py:324
  134.1 14.2 %all_to_all.27 = bf16[16,8,512]{2,1,0:T(8,128)(2,1)S(1)} all-to-all(bf16[16,8,512]{2,1,0:T(8,128)(2,1)S(1)} %broadcast_in_dim.2), channel_id=1, replica_groups=mesh['grp'=16,'rep'=64] {'grp'}, dimensions={0} | all-to-all | bytes 262144 | tf_op jit(solution)/shard_map/all_to_all | solution.py:371
  148.3 0.7 copy.16
  (8 shorter events, 0.0 us)
Async XLA Ops:
  4.1 24.3 %copy-start.2 = (s32[128]{0:T(128)S(1)}, s32[128]{0:T(128)}, u32[]{:S(2)}) copy-start(s32[128]{0:T(128)} %param.14) | copy-start | bytes 1540
  4.1 25.1 %copy-start.1 = (s32[128,1]{0,1:T(1,128)S(1)}, s32[128,1]{0,1:T(1,128)}, u32[]{:S(2)}) copy-start(s32[128,1]{0,1:T(1,128)} %param.15) | copy-start | bytes 1540
  4.1 46.2 %all-to-all-start = ((bf16[8,3,128,512]{3,2,1,0:T(8,128)(2,1)}), bf16[8,3,128,512]{3,2,1,0:T(8,128)(2,1)S(1)}, u32[]{:S(2)}, u32[]{:S(2)}) async-start(bf16[8,3,128,512]{3,2,1,0:T(8,128)(2,1)} %shard_map.112), calls=%async_computation | async-start | bytes 6291456 | tf_op jit(solution)/shard_map/all_to_all | solution.py:354
  51.0 4.6 %collective-permute-start = (f32[2,2,128,512]{3,2,1,0:T(8,128)S(1)}, f32[2,2,128,512]{3,2,1,0:T(8,128)S(1)}, u32[]{:S(2)}, u32[]{:S(2)}) collective-permute-start(f32[2,2,128,512]{3,2,1,0:T(8,128)S(1)} %shard_map.116), channel_id=1, source_target_pairs={{0,64},{64,0},{128,192},{192,128},{256,320},{320,256},{384,448},{4... | collective-permute-start | bytes 3145736 | tf_op jit(solution)/shard_map/ppermute | solution.py:358
  110.0 12.1 %collective-permute-start.1 = (s16[32,40,128]{2,1,0:T(8,128)(2,1)S(1)}, s16[32,40,128]{2,1,0:T(8,128)(2,1)S(1)}, u32[]{:S(2)}, u32[]{:S(2)}) collective-permute-start(s16[32,40,128]{2,1,0:T(8,128)(2,1)S(1)} %all_to_all.26.own), channel_id=1, source_target_pairs={{0,64},{64,0},{128,192},{192,128},{256,320},{320,256},{384,448},{4... | collective-permute-start | bytes 983048 | tf_op jit(solution)/shard_map/ppermute | solution.py:363
  115.7 15.5 %all-to-all-start.1 = ((bf16[16,32,128]{2,1,0:T(8,128)(2,1)}), bf16[16,32,128]{2,1,0:T(8,128)(2,1)S(1)}, u32[]{:S(2)}, u32[]{:S(2)}) async-start(bf16[16,32,128]{2,1,0:T(8,128)(2,1)} %shard_map.113), calls=%async_computation.1 | async-start | bytes 262144 | tf_op jit(solution)/shard_map/all_to_all | solution.py:362
  126.4 7.7 %collective-permute-start.2 = (bf16[8,512]{1,0:T(8,128)(2,1)S(1)}, bf16[8,512]{1,0:T(8,128)(2,1)S(1)}, u32[]{:S(2)}, u32[]{:S(2)}) collective-permute-start(bf16[8,512]{1,0:T(8,128)(2,1)S(1)} %shard_map.119), channel_id=1, source_target_pairs={{0,256},{64,272},{128,384},{192,400},{256,257},{320,273},{384,385}... | collective-permute-start | bytes 24584 | tf_op jit(solution)/shard_map/ppermute | solution.py:367
  131.2 0.7 copy-start
